TPU v7x, 32 devices: a whole 2x2x4 slice. The times are simulated.
32 devices in a mesh: groups: 2 (over y), expert: 8 (over z, x), tensor: 2 (over core).
Axes of the slice: x: 2, y: 2, z: 4, core: 2. Of those that a mesh axis runs over, the one named last changes fastest.
Arguments:
- tokens: bfloat16 [2, 256, 3584], P(None, ('groups', 'expert')), parts along dimension 1, may hold values from -6 to 6
- routes: int32 [2, 256, 8], P(None, ('groups', 'expert')), parts along dimension 1, may hold values from 0 to 63, as said below
- gating: float32 [2, 256, 8], P(None, ('groups', 'expert')), parts along dimension 1, may hold values from 0.05 to 0.5
- gate_weight: bfloat16 [64, 3584, 1024], P('expert', None, 'tensor'), may hold values from -0.09375 to 0.09375
- up_weight: bfloat16 [64, 3584, 1024], P('expert', None, 'tensor'), may hold values from -0.09375 to 0.09375
- down_weight: bfloat16 [64, 1024, 3584], P('expert', 'tensor'), may hold values from -0.1875 to 0.1875
Outputs:
- combined: bfloat16 [2, 256, 3584], P(None, ('groups', 'expert'), 'tensor'), parts along dimension 1
There are 2 independent parts, one for each index of `groups`. A program takes and returns all parts, laid end to end along the dimension named above; an argument that names none is the same for every part. Nothing has to cross between parts.
Inputs may be any that keep to these rules, and one draw needn't show every extreme that they name: `routes`: each row names 8 different experts. In every step the same 1 expert is named by exactly 10 of the rows of every device (aligned blocks of 16 rows). Every other expert is named by at most 2 rows of one device, and in every block some expert reaches 2.
All inputs are finite; a program needn't handle non-finite values.
Results may differ from a plain program's by a relative error of at most 0.0058.
Values may be sent and summed in bfloat16 or wider, within the bound.
No kernel may reach another device: no remote copies, remote signals or barrier semaphores. Data moves between devices by JAX's collectives and lax.ppermute only.
A program may use at most 256 MiB of HBM per device.

v0:
```python
import jax
import jax.numpy as jnp
from jax import lax
from jax.sharding import PartitionSpec as P


def expert_block(received, w_gate, w_up, w_down):
    gate_proj = jnp.einsum("nemd,edf->nemf", received, w_gate, preferred_element_type=jnp.float32)
    up_proj = jnp.einsum("nemd,edf->nemf", received, w_up, preferred_element_type=jnp.float32)
    active = (jax.nn.silu(gate_proj) * up_proj).astype(jnp.bfloat16)
    return jnp.einsum("nemf,efd->nemd", active, w_down, preferred_element_type=jnp.float32).astype(
        jnp.bfloat16
    )


def pair_ranks(flat_ids):
    pair_count = flat_ids.shape[0]
    positions = jnp.arange(pair_count, dtype=jnp.int32)
    earlier = (flat_ids[:, None] == flat_ids[None, :]) & (positions[None, :] < positions[:, None])
    return jnp.sum(earlier.astype(jnp.int32), axis=1)


def pack_rows(slot_of_pair, slot_count, topk, row_data):
    slot_ids = jnp.arange(slot_count, dtype=jnp.int32)
    hits = (slot_ids[:, None] == slot_of_pair[None, :]).reshape(slot_count, -1, topk)
    selector = jnp.any(hits, axis=2).astype(jnp.bfloat16)
    return jnp.dot(selector, row_data, preferred_element_type=jnp.float32).astype(jnp.bfloat16)


def local(tokens, routes, gating, gate_weight, up_weight, down_weight):
    step_count, tok_dev, feature_count = tokens.shape
    topk = routes.shape[2]
    experts_here = gate_weight.shape[0]
    device_count = lax.axis_size("expert")
    experts = experts_here * device_count
    hot_cap = tok_dev * 5 // 8
    outputs = []
    for step_index in range(step_count):
        token_rows = tokens[step_index]
        flat_ids = routes[step_index].reshape(-1)
        ranks = pair_ranks(flat_ids)
        send_slot = flat_ids * hot_cap + ranks
        send_buffer = pack_rows(send_slot, experts * hot_cap, topk, token_rows).reshape(
            device_count, experts_here, hot_cap, token_rows.shape[1]
        )
        results = expert_block(
            lax.all_to_all(send_buffer, "expert", split_axis=0, concat_axis=0, tiled=True),
            gate_weight,
            up_weight,
            down_weight,
        )
        returned = lax.all_to_all(
            results, "expert", split_axis=0, concat_axis=0, tiled=True
        ).reshape(experts * hot_cap, feature_count)
        pair_rows = returned[send_slot]
        weighted = (
            pair_rows.astype(jnp.float32).reshape(tok_dev, topk, feature_count)
            * gating[step_index][:, :, None]
        )
        running = jnp.sum(weighted, axis=1)
        outputs.append(
            lax.psum_scatter(running, "tensor", scatter_dimension=1, tiled=True).astype(
                jnp.bfloat16
            )
        )
    return jnp.stack(outputs)


def solution(mesh):
    in_specs = (
        P(None, ("groups", "expert"), None),
        P(None, ("groups", "expert"), None),
        P(None, ("groups", "expert"), None),
        P("expert", None, "tensor"),
        P("expert", None, "tensor"),
        P("expert", "tensor", None),
    )
    out_specs = P(None, ("groups", "expert"), "tensor")
    return jax.shard_map(local, mesh=mesh, in_specs=in_specs, out_specs=out_specs, check_vma=False)
```

profile of v0, /device:TPU:0, one launch (start us, length us, event | category | flops | bytes accessed | tf_op | source)
XLA Modules:
  0.0 492.5 jit_solution(13612331660478085537)
XLA Ops:
  6.5 0.7 broadcast_multiply_fusion.1
  7.3 0.1 eq.59
  7.4 0.2 convert_reduce_fusion.1
  7.6 0.1 reduce_sum.45
  7.7 0.1 copy.54
  7.8 0.1 eq.66
  7.9 0.2 convert_reduce_fusion
  8.1 0.1 reduce_sum.49
  8.2 0.1 copy.64
  8.3 0.7 bitcast_add_fusion.1
  9.0 0.1 copy.55
  9.1 0.2 fusion.56
  9.2 4.5 convolution_convert_fusion.1
  13.7 7.7 %reshape.122 = bf16[8,8,10,3584]{3,2,1,0:T(8,128)(2,1)} reshape(bf16[640,3584]{1,0:T(8,128)(2,1)} %convolution_convert_fusion.1) | data formatting | bytes 9175040 | tf_op jit(solution)/shard_map/reshape | solution.py:43
  21.4 7.8 %copy.56 = bf16[8,8,10,3584]{3,1,2,0:T(8,128)(2,1)} copy(bf16[8,8,10,3584]{3,2,1,0:T(8,128)(2,1)} %reshape.122) | data formatting | bytes 9175040 | tf_op jit(solution)/shard_map/reshape | solution.py:43
  29.2 7.4 %all-to-all-start = ((bf16[8,8,10,3584]{3,1,2,0:T(8,128)(2,1)}), bf16[8,8,10,3584]{3,1,2,0:T(8,128)(2,1)}, u32[]{:S(2)}, u32[]{:S(2)}) async-start(bf16[8,8,10,3584]{3,1,2,0:T(8,128)(2,1)} %copy.56), calls=%async_computation | async-start | bytes 9175040 | tf_op jit(solution)/shard_map/all_to_all | solution.py:47
  36.6 0.2 fusion.57
  36.8 3.5 convolution_convert_fusion
  40.3 7.7 %reshape.124 = bf16[8,8,10,3584]{3,2,1,0:T(8,128)(2,1)} reshape(bf16[640,3584]{1,0:T(8,128)(2,1)} %convolution_convert_fusion) | data formatting | bytes 9175040 | tf_op jit(solution)/shard_map/reshape | solution.py:43
  48.0 7.8 %copy.66 = bf16[8,8,10,3584]{3,1,2,0:T(8,128)(2,1)} copy(bf16[8,8,10,3584]{3,2,1,0:T(8,128)(2,1)} %reshape.124) | data formatting | bytes 9175040 | tf_op jit(solution)/shard_map/reshape | solution.py:43
  55.8 82.5 %all-to-all-done = bf16[8,8,10,3584]{3,1,2,0:T(8,128)(2,1)} async-done(((bf16[8,8,10,3584]{3,1,2,0:T(8,128)(2,1)}), bf16[8,8,10,3584]{3,1,2,0:T(8,128)(2,1)}, u32[]{:S(2)}, u32[]{:S(2)}) %all-to-all-start) | async-done | bytes 4587552 | tf_op jit(solution)/shard_map/all_to_all | solution.py:47
  138.3 4.7 all-to-all-start.2
  143.0 14.0 %fusion.6 = f32[8,8,10,512]{3,2,1,0:T(8,128)S(1)} fusion(bf16[8,3584,512]{2,1,0:T(8,128)(2,1)} %param.10, bf16[8,8,10,3584]{3,1,2,0:T(8,128)(2,1)} %all-to-all-done), kind=kOutput, calls=%fused_computation.8 | convolution fusion | flops 2348810240 | bytes 35258368 | tf_op jit(solution)/shard_map/nemd,edf->nemf/dot_general | solution.py:9
  157.0 34.3 %fusion.25 = bf16[8,8,10,3584]{3,2,0,1:T(8,128)(2,1)} fusion(bf16[8,512,3584]{2,1,0:T(8,128)(2,1)} %param.11, f32[8,8,10,512]{3,2,1,0:T(8,128)S(1)} %fusion.6, bf16[8,3584,512]{2,1,0:T(8,128)(2,1)} %param.9, bf16[8,8,10,3584]{3,1,2,0:T(8,128)(2,1)} %all-to-all-done), kind=kOutput, calls=%fused_computation.21 | convolution fusion | flops 4701880320 | bytes 69206016 | tf_op jit(solution)/shard_map/nemf,efd->nemd/dot_general | solution.py:11
  191.4 7.8 %copy.59 = bf16[8,8,10,3584]{3,1,2,0:T(8,128)(2,1)} copy(bf16[8,8,10,3584]{3,2,0,1:T(8,128)(2,1)} %fusion.25) | data formatting | bytes 9175040 | tf_op jit(solution)/shard_map/convert_element_type | solution.py:11
  199.2 44.8 %all-to-all-done.2 = bf16[8,8,10,3584]{3,1,2,0:T(8,128)(2,1)} async-done(((bf16[8,8,10,3584]{3,1,2,0:T(8,128)(2,1)}), bf16[8,8,10,3584]{3,1,2,0:T(8,128)(2,1)}, u32[]{:S(2)}, u32[]{:S(2)}) %all-to-all-start.2) | async-done | bytes 4587552 | tf_op jit(solution)/shard_map/all_to_all | solution.py:47
  244.0 4.8 all-to-all-start.1
  248.8 14.0 %fusion.4 = f32[8,8,10,512]{3,2,1,0:T(8,128)S(1)} fusion(bf16[8,3584,512]{2,1,0:T(8,128)(2,1)} %param.10, bf16[8,8,10,3584]{3,1,2,0:T(8,128)(2,1)} %all-to-all-done.2), kind=kOutput, calls=%fused_computation.6 | convolution fusion | flops 2348810240 | bytes 35258368 | tf_op jit(solution)/shard_map/nemd,edf->nemf/dot_general | solution.py:9
  262.8 34.2 %fusion.22 = bf16[8,8,10,3584]{3,2,0,1:T(8,128)(2,1)} fusion(bf16[8,512,3584]{2,1,0:T(8,128)(2,1)} %param.11, f32[8,8,10,512]{3,2,1,0:T(8,128)S(1)} %fusion.4, bf16[8,3584,512]{2,1,0:T(8,128)(2,1)} %param.9, bf16[8,8,10,3584]{3,1,2,0:T(8,128)(2,1)} %all-to-all-done.2), kind=kOutput, calls=%fused_computation.20 | convolution fusion | flops 4701880320 | bytes 69206016 | tf_op jit(solution)/shard_map/nemf,efd->nemd/dot_general | solution.py:11
  297.0 7.9 %copy.69 = bf16[8,8,10,3584]{3,1,2,0:T(8,128)(2,1)} copy(bf16[8,8,10,3584]{3,2,0,1:T(8,128)(2,1)} %fusion.22) | data formatting | bytes 9175040 | tf_op jit(solution)/shard_map/convert_element_type | solution.py:11
  304.9 44.8 %all-to-all-done.1 = bf16[8,8,10,3584]{3,1,2,0:T(8,128)(2,1)} async-done(((bf16[8,8,10,3584]{3,1,2,0:T(8,128)(2,1)}), bf16[8,8,10,3584]{3,1,2,0:T(8,128)(2,1)}, u32[]{:S(2)}, u32[]{:S(2)}) %all-to-all-start.1) | async-done | bytes 4587552 | tf_op jit(solution)/shard_map/all_to_all | solution.py:52
  349.7 4.6 all-to-all-start.3
  354.3 0.3 reduce-scatter.3.cloned.1.call-start
  354.7 0.1 mul.77
  354.9 0.1 mul.85
  355.1 7.3 %copy.60 = bf16[8,8,10,3584]{3,2,1,0:T(8,128)(2,1)} copy(bf16[8,8,10,3584]{3,1,2,0:T(8,128)(2,1)} %all-to-all-done.1) | data formatting | bytes 9175040 | tf_op jit(solution)/shard_map/all_to_all | solution.py:52
  362.4 7.9 %reshape.123 = bf16[640,3584]{1,0:T(8,128)(2,1)} reshape(bf16[8,8,10,3584]{3,2,1,0:T(8,128)(2,1)} %copy.60) | data formatting | bytes 9175040 | tf_op jit(solution)/shard_map/reshape | solution.py:54
  370.3 4.9 gather_fusion
  375.2 1.4 fusion.37
  376.7 78.6 %all-to-all-done.3 = bf16[8,8,10,3584]{3,1,2,0:T(8,128)(2,1)} async-done(((bf16[8,8,10,3584]{3,1,2,0:T(8,128)(2,1)}), bf16[8,8,10,3584]{3,1,2,0:T(8,128)(2,1)}, u32[]{:S(2)}, u32[]{:S(2)}) %all-to-all-start.3) | async-done | bytes 4587552 | tf_op jit(solution)/shard_map/all_to_all | solution.py:52
  455.3 7.2 %copy.70 = bf16[8,8,10,3584]{3,2,1,0:T(8,128)(2,1)} copy(bf16[8,8,10,3584]{3,1,2,0:T(8,128)(2,1)} %all-to-all-done.3) | data formatting | bytes 9175040 | tf_op jit(solution)/shard_map/all_to_all | solution.py:52
  462.5 8.0 %reshape.125 = bf16[640,3584]{1,0:T(8,128)(2,1)} reshape(bf16[8,8,10,3584]{3,2,1,0:T(8,128)(2,1)} %copy.70) | data formatting | bytes 9175040 | tf_op jit(solution)/shard_map/reshape | solution.py:54
  470.5 4.9 gather_fusion.1
  475.5 1.4 fusion.36
  476.9 0.9 convert_bitcast_fusion.1
  477.8 5.9 %reduce-scatter.5.cloned.1.call-done = f32[16,1792]{1,0:T(8,128)} async-done(((f32[16,3584]{1,0:T(8,128)}), f32[16,1792]{1,0:T(8,128)}) %reduce-scatter.5.cloned.1.call-update) | async-done | bytes 114704 | tf_op jit(solution)/shard_map/reduce_scatter | solution.py:62
  483.7 0.9 convert_bitcast_fusion
  484.6 0.7 pad_maximum_fusion
  (20 shorter events, 0.6 us)
Async XLA Ops:
  29.2 7.6 %copy-start = (bf16[2,16,3584]{2,1,0:T(8,128)(2,1)S(1)}, bf16[2,16,3584]{2,1,0:T(8,128)(2,1)}, u32[]{:S(2)}) copy-start(bf16[2,16,3584]{2,1,0:T(8,128)(2,1)} %param.6) | copy-start | bytes 688132
  29.2 109.1 %all-to-all-start = ((bf16[8,8,10,3584]{3,1,2,0:T(8,128)(2,1)}), bf16[8,8,10,3584]{3,1,2,0:T(8,128)(2,1)}, u32[]{:S(2)}, u32[]{:S(2)}) async-start(bf16[8,8,10,3584]{3,1,2,0:T(8,128)(2,1)} %copy.56), calls=%async_computation | async-start | bytes 9175040 | tf_op jit(solution)/shard_map/all_to_all | solution.py:47
  138.3 105.7 %all-to-all-start.2 = ((bf16[8,8,10,3584]{3,1,2,0:T(8,128)(2,1)}), bf16[8,8,10,3584]{3,1,2,0:T(8,128)(2,1)}, u32[]{:S(2)}, u32[]{:S(2)}) async-start(bf16[8,8,10,3584]{3,1,2,0:T(8,128)(2,1)} %copy.66), calls=%async_computation.3 | async-start | bytes 9175040 | tf_op jit(solution)/shard_map/all_to_all | solution.py:47
  244.0 105.7 %all-to-all-start.1 = ((bf16[8,8,10,3584]{3,1,2,0:T(8,128)(2,1)}), bf16[8,8,10,3584]{3,1,2,0:T(8,128)(2,1)}, u32[]{:S(2)}, u32[]{:S(2)}) async-start(bf16[8,8,10,3584]{3,1,2,0:T(8,128)(2,1)} %copy.59), calls=%async_computation.1 | async-start | bytes 9175040 | tf_op jit(solution)/shard_map/all_to_all | solution.py:52
  304.9 49.9 %copy-start.1 = (f32[2,16,8]{1,2,0:T(8,128)S(1)}, f32[2,16,8]{1,2,0:T(8,128)}, u32[]{:S(2)}) copy-start(f32[2,16,8]{1,2,0:T(8,128)} %param.8) | copy-start | bytes 3076
  349.7 105.5 %all-to-all-start.3 = ((bf16[8,8,10,3584]{3,1,2,0:T(8,128)(2,1)}), bf16[8,8,10,3584]{3,1,2,0:T(8,128)(2,1)}, u32[]{:S(2)}, u32[]{:S(2)}) async-start(bf16[8,8,10,3584]{3,1,2,0:T(8,128)(2,1)} %copy.69), calls=%async_computation.4 | async-start | bytes 9175040 | tf_op jit(solution)/shard_map/all_to_all | solution.py:52
  354.3 122.6 %reduce-scatter.3.cloned.1.call-start = ((), (), s32[]{:S(2)}) async-start(), calls=%async_computation.6 | async-start | bytes 344064 | tf_op jit(solution)/shard_map/reduce_scatter | solution.py:62
  376.6 107.1 %reduce-scatter.5.cloned.1.call-start = ((), (), s32[]{:S(2)}) async-start(), calls=%async_computation.7 | async-start | bytes 344064 | tf_op jit(solution)/shard_map/reduce_scatter | solution.py:62
Sparse Core Ops, SparseCore 0:
  376.8 8.9 reduce-scatter.2
  477.0 6.6 reduce-scatter.4
where the time goes:
time: 501 us; the launch traced here: 493 us
  waiting for transfers between devices  257 us (51%)
  matrix products  104 us (21%)
  local copies, waits for them, and re-layouts  88.2 us (18%)
  starting transfers between devices  21.9 us (4%)
  between operations  14 us (3%)
  other arithmetic  7.36 us (1%)
    all_to_all x2, waiting for transfers between devices, local(): lax.all_to_all(send_buffer, 'expert', split_axis=0, concat_axis=0, tiled=...  127 us
    all_to_all x2, waiting for transfers between devices, local(): lax.all_to_all(results, 'expert', split_axis=0, concat_axis=0, tiled=True)  123 us
    dot_general x2, matrix products, expert_block(): jnp.einsum('nemf,efd->nemd', active, w_down, preferred_element_type=jnp.f...  68.5 us
    reshape x4, local copies, waits for them, and re-layouts, local(): pack_rows(send_slot, experts * hot_cap, topk, token_rows)  30.9 us
    dot_general x2, matrix products, expert_block(): jnp.einsum('nemd,edf->nemf', received, w_up, preferred_element_type=jnp.f...  28 us
    reshape x2, local copies, waits for them, and re-layouts, local(): returned = lax.all_to_all(results, 'expert', split_axis=0, concat_axis=0,...  16 us
    convert_element_type x2, local copies, waits for them, and re-layouts, expert_block(): jnp.einsum('nemf,efd->nemd', active, w_down, preferred_element_type=jnp.f...  15.7 us
    all_to_all x2, local copies, waits for them, and re-layouts, local(): lax.all_to_all(results, 'expert', split_axis=0, concat_axis=0, tiled=True)  14.5 us
  transfers between devices with their start and end apart: 6, of which 5 were waited for; matrix products, arithmetic and copies ran while one was open for 36% of the time, Pallas kernels for 0%

commit v1 on v0

--- a/solution.py
+++ b/solution.py
@@ -1,7 +1,240 @@
+import functools
+
 import jax
 import jax.numpy as jnp
 from jax import lax
+from jax.experimental import pallas as pl
+from jax.experimental.pallas import tpu as pltpu
 from jax.sharding import PartitionSpec as P
+
+META = 128
+
+
+def expert_kernel(
+    topk,
+    cap_cold,
+    cap_hot,
+    place_ref,
+    mine_ref,
+    theirs_ref,
+    gate_ref,
+    up_ref,
+    down_ref,
+    keep_ref,
+    send_ref,
+    rank_rows,
+    weight_rows,
+    counts,
+    gathered,
+    returned,
+    hot_rows,
+    hot_sum,
+    hot_seen,
+):
+    step = pl.program_id(0)
+    experts_here = pl.num_programs(0)
+    rows = mine_ref.shape[0]
+    half = mine_ref.shape[1] - META
+    core = place_ref[1]
+    my_half = pl.ds(pl.multiple_of(core * half, 128), half)
+    other_half = pl.ds(pl.multiple_of((1 - core) * half, 128), half)
+
+    def gather(selector, target):
+        target[:, my_half] = jnp.dot(
+            selector, mine_ref[:, :half], preferred_element_type=jnp.float32
+        ).astype(jnp.bfloat16)
+        target[:, other_half] = jnp.dot(
+            selector, theirs_ref[:, :half], preferred_element_type=jnp.float32
+        ).astype(jnp.bfloat16)
+
+    def pick(expert, count):
+        slots = lax.broadcasted_iota(jnp.int32, (count, rows), 0).astype(jnp.float32)
+        return jnp.where(rank_rows[pl.ds(expert, 1), :] == slots, 1.0, 0.0)
+
+    @pl.when(step == 0)
+    def _():
+        hot_seen[0] = 0
+        meta = mine_ref[:, half:].astype(jnp.float32)
+        lane = lax.broadcasted_iota(jnp.int32, (rows, 128), 1)
+        wanted = (place_ref[0] * experts_here + lane).astype(jnp.float32)
+        member = jnp.zeros((rows, 128), jnp.float32)
+        weight = jnp.zeros((rows, 128), jnp.float32)
+        for k in range(topk):
+            gate = (
+                meta[:, topk + k : topk + k + 1]
+                + meta[:, 2 * topk + k : 2 * topk + k + 1]
+                + meta[:, 3 * topk + k : 3 * topk + k + 1]
+            )
+            hit = (meta[:, k : k + 1] == wanted) & (lane < experts_here)
+            member = member + jnp.where(hit, 1.0, 0.0)
+            weight = weight + jnp.where(hit, gate, 0.0)
+        earlier = (
+            lax.broadcasted_iota(jnp.int32, (rows, rows), 1)
+            < lax.broadcasted_iota(jnp.int32, (rows, rows), 0)
+        )
+        rank = jnp.dot(
+            jnp.where(earlier, 1.0, 0.0).astype(jnp.bfloat16),
+            member.astype(jnp.bfloat16),
+            preferred_element_type=jnp.float32,
+        )
+        rank_rows[...] = jnp.where(member > 0.0, rank, -1.0).T
+        weight_rows[...] = weight.T
+        totals = jnp.sum(member, axis=0, keepdims=True)
+        for e in range(counts.shape[0]):
+            counts[e] = totals[0, e].astype(jnp.int32)
+        selector = jnp.concatenate(
+            [pick(e, cap_cold) for e in range(counts.shape[0])], axis=0
+        ).astype(jnp.bfloat16)
+        gather(selector, gathered)
+
+    def forward(row_data, weight_column):
+        gate_proj = jnp.dot(row_data, gate_ref[0], preferred_element_type=jnp.float32)
+        up_proj = jnp.dot(row_data, up_ref[0], preferred_element_type=jnp.float32)
+        active = (jax.nn.silu(gate_proj) * up_proj).astype(jnp.bfloat16)
+        partial = jnp.dot(active, down_ref[0], preferred_element_type=jnp.float32)
+        return (partial * weight_column).astype(jnp.bfloat16)
+
+    block = pl.ds(pl.multiple_of(step * cap_cold, cap_cold), cap_cold)
+    is_hot = counts[step] > cap_cold
+
+    @pl.when(jnp.logical_not(is_hot))
+    def _():
+        weight_column = jnp.sum(
+            pick(step, cap_cold) * weight_rows[pl.ds(step, 1), :], axis=1, keepdims=True
+        )
+        returned[block, :] = forward(gathered[block, :], weight_column)
+
+    @pl.when(is_hot)
+    def _():
+        selector = pick(step, cap_hot)
+        gather(selector.astype(jnp.bfloat16), hot_rows)
+        weight_column = jnp.sum(
+            selector * weight_rows[pl.ds(step, 1), :], axis=1, keepdims=True
+        )
+        returned[block, :] = jnp.zeros((cap_cold, returned.shape[1]), jnp.bfloat16)
+        hot_rows[...] = forward(hot_rows[...], weight_column)
+        spread = jnp.dot(
+            selector.T.astype(jnp.bfloat16), hot_rows[...], preferred_element_type=jnp.float32
+        )
+
+        @pl.when(hot_seen[0] == 0)
+        def _():
+            hot_sum[...] = spread
+
+        @pl.when(hot_seen[0] != 0)
+        def _():
+            hot_sum[...] += spread
+
+        hot_seen[0] = 1
+
+    @pl.when(step == experts_here - 1)
+    def _():
+        selector = jnp.concatenate(
+            [pick(e, cap_cold) for e in range(counts.shape[0])], axis=0
+        )
+        spread = selector.T.astype(jnp.bfloat16)
+        for columns, out_ref in ((my_half, keep_ref), (other_half, send_ref)):
+            value = jnp.dot(
+                spread, returned[:, columns], preferred_element_type=jnp.float32
+            )
+            out_ref[...] = value.astype(jnp.bfloat16)
+
+            @pl.when(hot_seen[0] != 0)
+            def _():
+                out_ref[...] = (value + hot_sum[:, columns]).astype(jnp.bfloat16)
+
+
+def run_experts(place, mine, theirs, gate_weight, up_weight, down_weight, topk, cap_cold, cap_hot):
+    rows = mine.shape[0]
+    half = mine.shape[1] - META
+    experts_here, features, hidden = gate_weight.shape
+    out = jax.ShapeDtypeStruct((rows, half), jnp.bfloat16)
+    whole = lambda shape: pl.BlockSpec(shape, lambda e, *_: (0,) * len(shape))
+    return pl.pallas_call(
+        functools.partial(expert_kernel, topk, cap_cold, cap_hot),
+        grid_spec=pltpu.PrefetchScalarGridSpec(
+            num_scalar_prefetch=1,
+            grid=(experts_here,),
+            in_specs=[
+                whole(mine.shape),
+                whole(theirs.shape),
+                pl.BlockSpec((1, features, hidden), lambda e, *_: (e, 0, 0)),
+                pl.BlockSpec((1, features, hidden), lambda e, *_: (e, 0, 0)),
+                pl.BlockSpec((1, hidden, features), lambda e, *_: (e, 0, 0)),
+            ],
+            out_specs=[whole((rows, half)), whole((rows, half))],
+            scratch_shapes=[
+                pltpu.VMEM((128, rows), jnp.float32),
+                pltpu.VMEM((128, rows), jnp.float32),
+                pltpu.SMEM((experts_here,), jnp.int32),
+                pltpu.VMEM((experts_here * cap_cold, features), jnp.bfloat16),
+                pltpu.VMEM((experts_here * cap_cold, features), jnp.bfloat16),
+                pltpu.VMEM((cap_hot, features), jnp.bfloat16),
+                pltpu.VMEM((rows, features), jnp.float32),
+                pltpu.SMEM((1,), jnp.int32),
+            ],
+        ),
+        out_shape=[out, out],
+        compiler_params=pltpu.CompilerParams(vmem_limit_bytes=56 * 1024 * 1024),
+        cost_estimate=pl.CostEstimate(
+            flops=6 * rows * features * hidden,
+            bytes_accessed=6 * experts_here * features * hidden,
+            transcendentals=0,
+        ),
+    )(place, mine, theirs, gate_weight, up_weight, down_weight)
+
+
+def local(tokens, routes, gating, gate_weight, up_weight, down_weight):
+    step_count, tok_dev, features = tokens.shape
+    topk = routes.shape[2]
+    devices = lax.axis_size("expert")
+    pairs = devices // 2
+    half = features // 2
+    rows_here = step_count * tok_dev
+    core = lax.axis_index("tensor")
+    swap = [(0, 1), (1, 0)]
+    flip = [(i, i ^ 1) for i in range(devices)]
+
+    def shift(value, k):
+        return lax.ppermute(
+            value, "expert", [(i, (i + 2 * k) % devices) for i in range(devices)]
+        )
+
+    top = gating.astype(jnp.bfloat16)
+    rest = gating - top.astype(jnp.float32)
+    middle = rest.astype(jnp.bfloat16)
+    low = (rest - middle.astype(jnp.float32)).astype(jnp.bfloat16)
+    meta = jnp.concatenate([routes.astype(jnp.bfloat16), top, middle, low], axis=2)
+    meta = jnp.pad(meta, ((0, 0), (0, 0), (0, META - meta.shape[2])))
+    mine = jnp.concatenate(
+        [lax.dynamic_slice_in_dim(tokens, core * half, half, 2), meta], axis=2
+    ).reshape(rows_here, half + META)
+
+    mine = jnp.concatenate([mine] + [shift(mine, k) for k in range(1, pairs)])
+    mine = jnp.concatenate([mine, lax.ppermute(mine, "expert", flip)])
+    theirs = lax.ppermute(mine, "tensor", swap)
+
+    place = jnp.stack([lax.axis_index("expert"), core]).astype(jnp.int32)
+    keep, send = run_experts(
+        place,
+        mine,
+        theirs,
+        gate_weight,
+        up_weight,
+        down_weight,
+        topk,
+        step_count * devices * 2,
+        step_count * devices * (tok_dev * 5 // 8),
+    )
+
+    f32 = jnp.float32
+    both = keep.astype(f32) + lax.ppermute(send, "tensor", swap).astype(f32)
+    both = both.reshape(2, pairs, rows_here, half)
+    column = both[0] + lax.ppermute(both[1].astype(jnp.bfloat16), "expert", flip).astype(f32)
+    total = column[0]
+    for k in range(1, pairs):
+        total = total + shift(column[k].astype(jnp.bfloat16), pairs - k).astype(f32)
+    return total.astype(jnp.bfloat16).reshape(step_count, tok_dev, half)
 
 
 def expert_block(received, w_gate, w_up, w_down):
@@ -27,7 +260,7 @@
     return jnp.dot(selector, row_data, preferred_element_type=jnp.float32).astype(jnp.bfloat16)
 
 
-def local(tokens, routes, gating, gate_weight, up_weight, down_weight):
+def local_by_slots(tokens, routes, gating, gate_weight, up_weight, down_weight):
     step_count, tok_dev, feature_count = tokens.shape
     topk = routes.shape[2]
     experts_here = gate_weight.shape[0]
@@ -67,6 +300,7 @@
 
 
 def solution(mesh):
+    body = local if mesh.shape["expert"] <= 16 else local_by_slots
     in_specs = (
         P(None, ("groups", "expert"), None),
         P(None, ("groups", "expert"), None),
@@ -76,4 +310,4 @@
         P("expert", "tensor", None),
     )
     out_specs = P(None, ("groups", "expert"), "tensor")
-    return jax.shard_map(local, mesh=mesh, in_specs=in_specs, out_specs=out_specs, check_vma=False)
+    return jax.shard_map(body, mesh=mesh, in_specs=in_specs, out_specs=out_specs, check_vma=False)

time: 501 us -> 98.7 us (0.20); the launches traced: 493 us -> 98.4 us
  waiting for transfers between devices: 257 us -> 44 us
  matrix products: 104 us -> 0 us
  local copies, waits for them, and re-layouts: 88.2 us -> 1.34 us
  Pallas kernels: 0 us -> 34.5 us
  between operations: 14 us -> 0.1 us
  starting transfers between devices: 21.9 us -> 13.9 us
    all_to_all x4 -> x0, waiting for transfers between devices: 251 us -> none  [the longest x2 127 us: local(): lax.all_to_all(send_buffer, 'expert', split_axis=0, concat_axis=0, tiled=...]
    dot_general x6 -> x0, matrix products: 104 us -> none  [the longest x2 68.5 us: expert_block(): jnp.einsum('nemf,efd->nemd', active, w_down, preferred_element_type=jnp.f...]
    reshape x6 -> x0, local copies, waits for them, and re-layouts: 46.9 us -> none  [the longest x4 30.9 us: local(): pack_rows(send_slot, experts * hot_cap, topk, token_rows)]
    ppermute x0 -> x10, waiting for transfers between devices: none -> 44 us  [the longest x6 17.7 us: shift(): lax.ppermute(value, 'expert', [(i, (i + 2 * k) % devices) for i in range(...]
    pallas_call x0 -> x1, Pallas kernels: none -> 34.5 us  [run_experts(): pl.pallas_call(functools.partial(expert_kernel, topk, cap_cold, cap_hot),...]
    all_to_all x4 -> x0, starting transfers between devices: 21.5 us -> none  [the longest x2 12.1 us: local(): lax.all_to_all(send_buffer, 'expert', split_axis=0, concat_axis=0, tiled=...]
    convert_element_type x2 -> x1, local copies, waits for them, and re-layouts: 15.7 us -> 0.02 us  [local(): total = total + shift(column[k].astype(jnp.bfloat16), pairs - k).astype(f32)]
    all_to_all x2 -> x0, local copies, waits for them, and re-layouts: 14.5 us -> none  [local(): lax.all_to_all(results, 'expert', split_axis=0, concat_axis=0, tiled=True)]
  transfers between devices with their start and end apart: 6 -> 10, of which waited for: 5 -> 9; matrix products, arithmetic and copies ran while one was open for 36% -> 1% of each run, Pallas kernels for 0% -> 0%
where the time goes in v1:
time: 98.7 us; the launch traced here: 98.4 us
  waiting for transfers between devices  44 us (45%)
  Pallas kernels  34.5 us (35%)
  starting transfers between devices  13.9 us (14%)
  other arithmetic  4.53 us (5%)
  local copies, waits for them, and re-layouts  1.34 us (1%)
    pallas_call x1, Pallas kernels, run_experts(): pl.pallas_call(functools.partial(expert_kernel, topk, cap_cold, cap_hot),...  34.5 us
    ppermute x6, waiting for transfers between devices, shift(): lax.ppermute(value, 'expert', [(i, (i + 2 * k) % devices) for i in range(...  17.7 us
    ppermute x1, waiting for transfers between devices, local(): lax.ppermute(both[1].astype(jnp.bfloat16), 'expert', flip).astype(f32)  11 us
    ppermute x1, waiting for transfers between devices, local(): mine = jnp.concatenate([mine, lax.ppermute(mine, 'expert', flip)])  10.9 us
    ppermute x6, starting transfers between devices, shift(): lax.ppermute(value, 'expert', [(i, (i + 2 * k) % devices) for i in range(...  10.6 us
    ppermute x1, waiting for transfers between devices, local(): both = keep.astype(f32) + lax.ppermute(send, 'tensor', swap).astype(f32)  2.56 us
  transfers between devices with their start and end apart: 10, of which 9 were waited for; matrix products, arithmetic and copies ran while one was open for 1% of the time, Pallas kernels for 0%

profile of v1, /device:TPU:0, one launch (start us, length us, event | category | flops | bytes accessed | tf_op | source)
XLA Modules:
  0.0 98.4 jit_solution(6570156486680629980)
XLA Ops:
  0.0 0.0 copy-start
  0.0 0.7 convert_element_type.57
  0.7 0.8 fusion.8
  1.5 0.1 copy.8
  1.6 0.0 copy-done
  1.7 5.1 %collective-permute-start.2 = (bf16[32,1920]{1,0:T(8,128)(2,1)S(1)}, bf16[32,1920]{1,0:T(8,128)(2,1)S(1)}, u32[]{:S(2)}, u32[]{:S(2)}) collective-permute-start(bf16[32,1920]{1,0:T(8,128)(2,1)S(1)} %bitcast.23), channel_id=1, source_target_pairs={{0,12},{2,14},{4,0},{6,2},{8,4},{10,6},{12,8},{14,10},{1,13},{3,15... | collective-permute-start | bytes 368648 | tf_op jit(solution)/shard_map/ppermute | solution.py:199
  6.8 0.0 collective-permute-start.1
  6.8 1.0 %collective-permute-start = (bf16[32,1920]{1,0:T(8,128)(2,1)S(1)}, bf16[32,1920]{1,0:T(8,128)(2,1)S(1)}, u32[]{:S(2)}, u32[]{:S(2)}) collective-permute-start(bf16[32,1920]{1,0:T(8,128)(2,1)S(1)} %bitcast.25), channel_id=1, source_target_pairs={{0,4},{2,6},{4,8},{6,10},{8,12},{10,14},{12,0},{14,2},{1,5},{3,7},... | collective-permute-start | bytes 368648 | tf_op jit(solution)/shard_map/ppermute | solution.py:199
  7.8 2.7 %collective-permute-done.2 = bf16[32,1920]{1,0:T(8,128)(2,1)S(1)} collective-permute-done((bf16[32,1920]{1,0:T(8,128)(2,1)S(1)}, bf16[32,1920]{1,0:T(8,128)(2,1)S(1)}, u32[]{:S(2)}, u32[]{:S(2)}) %collective-permute-start.2) | collective-permute-done | bytes 122912 | tf_op jit(solution)/shard_map/ppermute | solution.py:199
  10.5 6.9 %collective-permute-done.1 = bf16[32,1920]{1,0:T(8,128)(2,1)S(1)} collective-permute-done((bf16[32,1920]{1,0:T(8,128)(2,1)S(1)}, bf16[32,1920]{1,0:T(8,128)(2,1)S(1)}, u32[]{:S(2)}, u32[]{:S(2)}) %collective-permute-start.1) | collective-permute-done | bytes 122912 | tf_op jit(solution)/shard_map/ppermute | solution.py:199
  17.3 0.0 collective-permute-done
  17.4 1.6 %collective-permute-start.3 = (bf16[128,1920]{1,0:T(8,128)(2,1)S(1)}, bf16[128,1920]{1,0:T(8,128)(2,1)S(1)}, u32[]{:S(2)}, u32[]{:S(2)}) collective-permute-start(bf16[128,1920]{1,0:T(8,128)(2,1)S(1)} %pad_maximum_fusion), channel_id=1, source_target_pairs={{0,2},{2,0},{4,6},{6,4},{8,10},{10,8},{12,14},{14,12},{1,3},{3,1},... | collective-permute-start | bytes 1474568 | tf_op jit(solution)/shard_map/ppermute | solution.py:214
  19.0 10.9 %collective-permute-done.3 = bf16[128,1920]{1,0:T(8,128)(2,1)S(1)} collective-permute-done((bf16[128,1920]{1,0:T(8,128)(2,1)S(1)}, bf16[128,1920]{1,0:T(8,128)(2,1)S(1)}, u32[]{:S(2)}, u32[]{:S(2)}) %collective-permute-start.3) | collective-permute-done | bytes 491552 | tf_op jit(solution)/shard_map/ppermute | solution.py:214
  30.0 0.0 copy-start.2
  30.0 0.1 collective-permute-start.4
  30.1 0.7 pad_add_fusion.place_ref
  30.8 1.8 %collective-permute-done.4.theirs_ref = bf16[256,1920]{1,0:T(8,128)(2,1)S(1)} collective-permute-done((bf16[256,1920]{1,0:T(8,128)(2,1)S(1)}, bf16[256,1920]{1,0:T(8,128)(2,1)S(1)}, u32[]{:S(2)}, u32[]{:S(2)}) %collective-permute-start.4) | collective-permute-done | bytes 983072 | tf_op jit(solution)/shard_map/ppermute | solution.py:215
  32.6 0.0 copy-done.2
  32.6 0.0 copy-start.3
  32.6 1.0 %copy-done.3 = bf16[256,1920]{1,0:T(8,128)(2,1)} copy-done((bf16[256,1920]{1,0:T(8,128)(2,1)}, bf16[256,1920]{1,0:T(8,128)(2,1)S(1)}, u32[]{:S(2)}) %copy-start.3) | copy-done | bytes 983064
  33.6 34.5 %shard_map.64 = (bf16[256,1792]{1,0:T(8,128)(2,1)}, bf16[256,1792]{1,0:T(8,128)(2,1)}) custom-call(s32[2]{0:T(128)} %pad_add_fusion.place_ref, bf16[256,1920]{1,0:T(8,128)(2,1)} %copy-done.2, bf16[256,1920]{1,0:T(8,128)(2,1)} %copy-done.3, bf16[8,3584,512]{2,1,0:T(8,128)(2,1)} %gate_ref.1, bf16[8,3584,512]{2,1,0:T(8,128)(2,1)} %up_ref.1, ...), custom_call_target="tpu_custom_call" | custom-call | flops 2818572288 | bytes 88080384 | tf_op jit(solution)/shard_map/pallas_call | solution.py:153
  68.1 0.1 collective-permute-start.5
  68.3 2.6 %collective-permute-done.5 = bf16[256,1792]{1,0:T(8,128)(2,1)S(1)} collective-permute-done((bf16[256,1792]{1,0:T(8,128)(2,1)}, bf16[256,1792]{1,0:T(8,128)(2,1)S(1)}, u32[]{:S(2)}, u32[]{:S(2)}) %collective-permute-start.5) | collective-permute-done | bytes 917536 | tf_op jit(solution)/shard_map/ppermute | solution.py:231
  70.8 1.4 %convert_add_fusion = f32[256,1792]{1,0:T(8,128)S(1)} fusion(bf16[256,1792]{1,0:T(8,128)(2,1)S(1)} %collective-permute-done.5, bf16[256,1792]{1,0:T(8,128)(2,1)} %get-tuple-element.7), kind=kLoop, calls=%fused_computation | loop fusion | flops 1376256 | bytes 3670016 | tf_op jit(solution)/shard_map/add | solution.py:231
  72.3 1.6 %collective-permute-start.6 = (bf16[4,32,1792]{2,1,0:T(8,128)(2,1)S(1)}, bf16[4,32,1792]{2,1,0:T(8,128)(2,1)S(1)}, u32[]{:S(2)}, u32[]{:S(2)}) collective-permute-start(bf16[4,32,1792]{2,1,0:T(8,128)(2,1)S(1)} %bitcast.28), channel_id=1, source_target_pairs={{0,2},{2,0},{4,6},{6,4},{8,10},{10,8},{12,14},{14,12},{1,3},{3,1},... | collective-permute-start | bytes 1376264 | tf_op jit(solution)/shard_map/ppermute | solution.py:233
  73.9 0.1 slice.30
  73.9 11.0 %collective-permute-done.6 = bf16[4,32,1792]{2,1,0:T(8,128)(2,1)S(1)} collective-permute-done((bf16[4,32,1792]{2,1,0:T(8,128)(2,1)S(1)}, bf16[4,32,1792]{2,1,0:T(8,128)(2,1)S(1)}, u32[]{:S(2)}, u32[]{:S(2)}) %collective-permute-start.6) | collective-permute-done | bytes 458784 | tf_op jit(solution)/shard_map/ppermute | solution.py:233
  84.9 0.0 copy-start.1
  84.9 0.1 fusion.7
  85.1 2.0 %collective-permute-start.7 = (bf16[32,1792]{1,0:T(8,128)(2,1)S(1)}, bf16[32,1792]{1,0:T(8,128)(2,1)S(1)}, u32[]{:S(2)}, u32[]{:S(2)}) collective-permute-start(bf16[32,1792]{1,0:T(8,128)(2,1)S(1)} %get-tuple-element.11), channel_id=1, source_target_pairs={{0,12},{2,14},{4,0},{6,2},{8,4},{10,6},{12,8},{14,10},{1,13},{3,15... | collective-permute-start | bytes 344072 | tf_op jit(solution)/shard_map/ppermute | solution.py:199
  87.1 0.1 collective-permute-start.9
  87.2 2.4 %collective-permute-start.8 = (bf16[32,1792]{1,0:T(8,128)(2,1)S(1)}, bf16[32,1792]{1,0:T(8,128)(2,1)S(1)}, u32[]{:S(2)}, u32[]{:S(2)}) collective-permute-start(bf16[32,1792]{1,0:T(8,128)(2,1)S(1)} %get-tuple-element.13), channel_id=1, source_target_pairs={{0,8},{2,10},{4,12},{6,14},{8,0},{10,2},{12,4},{14,6},{1,9},{3,11}... | collective-permute-start | bytes 344072 | tf_op jit(solution)/shard_map/ppermute | solution.py:199
  89.6 1.1 %collective-permute-done.7 = bf16[32,1792]{1,0:T(8,128)(2,1)S(1)} collective-permute-done((bf16[32,1792]{1,0:T(8,128)(2,1)S(1)}, bf16[32,1792]{1,0:T(8,128)(2,1)S(1)}, u32[]{:S(2)}, u32[]{:S(2)}) %collective-permute-start.7) | collective-permute-done | bytes 114720 | tf_op jit(solution)/shard_map/ppermute | solution.py:199
  90.7 4.7 %collective-permute-done.9 = bf16[32,1792]{1,0:T(8,128)(2,1)S(1)} collective-permute-done((bf16[32,1792]{1,0:T(8,128)(2,1)S(1)}, bf16[32,1792]{1,0:T(8,128)(2,1)S(1)}, u32[]{:S(2)}, u32[]{:S(2)}) %collective-permute-start.9) | collective-permute-done | bytes 114720 | tf_op jit(solution)/shard_map/ppermute | solution.py:199
  95.4 2.3 %collective-permute-done.8 = bf16[32,1792]{1,0:T(8,128)(2,1)S(1)} collective-permute-done((bf16[32,1792]{1,0:T(8,128)(2,1)S(1)}, bf16[32,1792]{1,0:T(8,128)(2,1)S(1)}, u32[]{:S(2)}, u32[]{:S(2)}) %collective-permute-start.8) | collective-permute-done | bytes 114720 | tf_op jit(solution)/shard_map/ppermute | solution.py:199
  97.7 0.7 fusion.4
  98.4 0.0 copy-done.1
  (11 shorter events, 0.2 us)
Async XLA Ops:
  0.0 1.6 %copy-start = (bf16[2,16,3584]{2,1,0:T(8,128)(2,1)S(1)}, bf16[2,16,3584]{2,1,0:T(8,128)(2,1)}, u32[]{:S(2)}) copy-start(bf16[2,16,3584]{2,1,0:T(8,128)(2,1)} %param.6) | copy-start | bytes 688132
  1.7 8.8 %collective-permute-start.2 = (bf16[32,1920]{1,0:T(8,128)(2,1)S(1)}, bf16[32,1920]{1,0:T(8,128)(2,1)S(1)}, u32[]{:S(2)}, u32[]{:S(2)}) collective-permute-start(bf16[32,1920]{1,0:T(8,128)(2,1)S(1)} %bitcast.23), channel_id=1, source_target_pairs={{0,12},{2,14},{4,0},{6,2},{8,4},{10,6},{12,8},{14,10},{1,13},{3,15... | collective-permute-start | bytes 368648 | tf_op jit(solution)/shard_map/ppermute | solution.py:199
  6.8 10.6 %collective-permute-start.1 = (bf16[32,1920]{1,0:T(8,128)(2,1)S(1)}, bf16[32,1920]{1,0:T(8,128)(2,1)S(1)}, u32[]{:S(2)}, u32[]{:S(2)}) collective-permute-start(bf16[32,1920]{1,0:T(8,128)(2,1)S(1)} %bitcast.24), channel_id=1, source_target_pairs={{0,8},{2,10},{4,12},{6,14},{8,0},{10,2},{12,4},{14,6},{1,9},{3,11}... | collective-permute-start | bytes 368648 | tf_op jit(solution)/shard_map/ppermute | solution.py:199
  6.8 10.6 %collective-permute-start = (bf16[32,1920]{1,0:T(8,128)(2,1)S(1)}, bf16[32,1920]{1,0:T(8,128)(2,1)S(1)}, u32[]{:S(2)}, u32[]{:S(2)}) collective-permute-start(bf16[32,1920]{1,0:T(8,128)(2,1)S(1)} %bitcast.25), channel_id=1, source_target_pairs={{0,4},{2,6},{4,8},{6,10},{8,12},{10,14},{12,0},{14,2},{1,5},{3,7},... | collective-permute-start | bytes 368648 | tf_op jit(solution)/shard_map/ppermute | solution.py:199
  17.4 12.5 %collective-permute-start.3 = (bf16[128,1920]{1,0:T(8,128)(2,1)S(1)}, bf16[128,1920]{1,0:T(8,128)(2,1)S(1)}, u32[]{:S(2)}, u32[]{:S(2)}) collective-permute-start(bf16[128,1920]{1,0:T(8,128)(2,1)S(1)} %pad_maximum_fusion), channel_id=1, source_target_pairs={{0,2},{2,0},{4,6},{6,4},{8,10},{10,8},{12,14},{14,12},{1,3},{3,1},... | collective-permute-start | bytes 1474568 | tf_op jit(solution)/shard_map/ppermute | solution.py:214
  30.0 2.6 %copy-start.2 = (bf16[256,1920]{1,0:T(8,128)(2,1)}, bf16[256,1920]{1,0:T(8,128)(2,1)S(1)}, u32[]{:S(2)}) copy-start(bf16[256,1920]{1,0:T(8,128)(2,1)S(1)} %constant_dynamic-update-slice_fusion.mine_ref) | copy-start | bytes 2949124
  30.0 2.6 %collective-permute-start.4 = (bf16[256,1920]{1,0:T(8,128)(2,1)S(1)}, bf16[256,1920]{1,0:T(8,128)(2,1)S(1)}, u32[]{:S(2)}, u32[]{:S(2)}) collective-permute-start(bf16[256,1920]{1,0:T(8,128)(2,1)S(1)} %constant_dynamic-update-slice_fusion.mine_ref), channel_id=1, source_target_pairs={{0,1},{1,0},{2,3},{3,2},{4,5},{5,4},{6,7},{7,6},{8,9},{9,8},{10,11... | collective-permute-start | bytes 2949128 | tf_op jit(solution)/shard_map/ppermute | solution.py:215
  32.6 1.0 %copy-start.3 = (bf16[256,1920]{1,0:T(8,128)(2,1)}, bf16[256,1920]{1,0:T(8,128)(2,1)S(1)}, u32[]{:S(2)}) copy-start(bf16[256,1920]{1,0:T(8,128)(2,1)S(1)} %collective-permute-done.4.theirs_ref) | copy-start | bytes 2949124
  68.1 2.7 %collective-permute-start.5 = (bf16[256,1792]{1,0:T(8,128)(2,1)}, bf16[256,1792]{1,0:T(8,128)(2,1)S(1)}, u32[]{:S(2)}, u32[]{:S(2)}) collective-permute-start(bf16[256,1792]{1,0:T(8,128)(2,1)} %get-tuple-element.8), channel_id=1, source_target_pairs={{0,1},{1,0},{2,3},{3,2},{4,5},{5,4},{6,7},{7,6},{8,9},{9,8},{10,11... | collective-permute-start | bytes 2752520 | tf_op jit(solution)/shard_map/ppermute | solution.py:231
  72.3 12.6 %collective-permute-start.6 = (bf16[4,32,1792]{2,1,0:T(8,128)(2,1)S(1)}, bf16[4,32,1792]{2,1,0:T(8,128)(2,1)S(1)}, u32[]{:S(2)}, u32[]{:S(2)}) collective-permute-start(bf16[4,32,1792]{2,1,0:T(8,128)(2,1)S(1)} %bitcast.28), channel_id=1, source_target_pairs={{0,2},{2,0},{4,6},{6,4},{8,10},{10,8},{12,14},{14,12},{1,3},{3,1},... | collective-permute-start | bytes 1376264 | tf_op jit(solution)/shard_map/ppermute | solution.py:233
  84.9 13.5 %copy-start.1 = (bf16[2,16,3584]{2,1,0:T(8,128)(2,1)S(1)}, bf16[2,16,3584]{2,1,0:T(8,128)(2,1)}, u32[]{:S(2)}) copy-start(bf16[2,16,3584]{2,1,0:T(8,128)(2,1)} %param.6) | copy-start | bytes 688132
  85.1 5.6 %collective-permute-start.7 = (bf16[32,1792]{1,0:T(8,128)(2,1)S(1)}, bf16[32,1792]{1,0:T(8,128)(2,1)S(1)}, u32[]{:S(2)}, u32[]{:S(2)}) collective-permute-start(bf16[32,1792]{1,0:T(8,128)(2,1)S(1)} %get-tuple-element.11), channel_id=1, source_target_pairs={{0,12},{2,14},{4,0},{6,2},{8,4},{10,6},{12,8},{14,10},{1,13},{3,15... | collective-permute-start | bytes 344072 | tf_op jit(solution)/shard_map/ppermute | solution.py:199
  87.1 8.3 %collective-permute-start.9 = (bf16[32,1792]{1,0:T(8,128)(2,1)S(1)}, bf16[32,1792]{1,0:T(8,128)(2,1)S(1)}, u32[]{:S(2)}, u32[]{:S(2)}) collective-permute-start(bf16[32,1792]{1,0:T(8,128)(2,1)S(1)} %get-tuple-element.12), channel_id=1, source_target_pairs={{0,4},{2,6},{4,8},{6,10},{8,12},{10,14},{12,0},{14,2},{1,5},{3,7},... | collective-permute-start | bytes 344072 | tf_op jit(solution)/shard_map/ppermute | solution.py:199
  87.2 10.5 %collective-permute-start.8 = (bf16[32,1792]{1,0:T(8,128)(2,1)S(1)}, bf16[32,1792]{1,0:T(8,128)(2,1)S(1)}, u32[]{:S(2)}, u32[]{:S(2)}) collective-permute-start(bf16[32,1792]{1,0:T(8,128)(2,1)S(1)} %get-tuple-element.13), channel_id=1, source_target_pairs={{0,8},{2,10},{4,12},{6,14},{8,0},{10,2},{12,4},{14,6},{1,9},{3,11}... | collective-permute-start | bytes 344072 | tf_op jit(solution)/shard_map/ppermute | solution.py:199

commit v2 on v0

--- a/solution.py
+++ b/solution.py
@@ -1,7 +1,474 @@
+import functools
+
 import jax
 import jax.numpy as jnp
 from jax import lax
+from jax.experimental import pallas as pl
+from jax.experimental.pallas import tpu as pltpu
 from jax.sharding import PartitionSpec as P
+
+META = 128
+AHEAD = 2
+RING = 4
+MIB = 1024 * 1024
+
+
+def in_vmem(value):
+    return pltpu.with_memory_space_constraint(value, pltpu.VMEM)
+
+
+def in_hbm(value):
+    return pltpu.with_memory_space_constraint(value, pltpu.HBM)
+
+
+VMEM_SPEC = pl.BlockSpec(memory_space=pltpu.VMEM)
+HBM_SPEC = pl.BlockSpec(memory_space=pl.ANY)
+DONE = pltpu.VMEM((8, 128), jnp.float32)
+SMALL = pl.CostEstimate(flops=1, bytes_accessed=1, transcendentals=0)
+
+
+def run_copies(copies):
+    for copy in copies:
+        copy.start()
+    for copy in copies:
+        copy.wait()
+
+
+def prepare(core, tokens, routes, gating):
+    step_count, tok_dev, features = tokens.shape
+    topk = routes.shape[2]
+    half = features // 2
+
+    def kernel(core_ref, tokens_ref, routes_hbm, gating_hbm, out_ref, routes_ref, gating_ref, sems):
+        columns = pl.ds(pl.multiple_of(core_ref[0] * half, 128), half)
+        copies = [
+            pltpu.make_async_copy(
+                tokens_ref.at[s, :, columns],
+                out_ref.at[s * tok_dev : (s + 1) * tok_dev, :half],
+                sems.at[s],
+            )
+            for s in range(step_count)
+        ]
+        small = [
+            pltpu.make_async_copy(routes_hbm, routes_ref, sems.at[step_count]),
+            pltpu.make_async_copy(gating_hbm, gating_ref, sems.at[step_count + 1]),
+        ]
+        for copy in small + copies:
+            copy.start()
+        for copy in small:
+            copy.wait()
+        for s in range(step_count):
+            weight = gating_ref[s].T
+            top = weight.astype(jnp.bfloat16)
+            rest = weight - top.astype(jnp.float32)
+            middle = rest.astype(jnp.bfloat16)
+            low = rest - middle.astype(jnp.float32)
+            parts = [
+                routes_ref[s].astype(jnp.float32).T,
+                top.astype(jnp.float32),
+                middle.astype(jnp.float32),
+                low,
+                jnp.zeros((tok_dev, META - 4 * topk), jnp.float32),
+            ]
+            out_ref[s * tok_dev : (s + 1) * tok_dev, half:] = jnp.concatenate(
+                parts, axis=1
+            ).astype(jnp.bfloat16)
+        for copy in copies:
+            copy.wait()
+
+    return pl.pallas_call(
+        kernel,
+        in_specs=[pl.BlockSpec(memory_space=pltpu.SMEM), HBM_SPEC, HBM_SPEC, HBM_SPEC],
+        out_specs=VMEM_SPEC,
+        out_shape=pltpu.VMEM((step_count * tok_dev, half + META), jnp.bfloat16),
+        scratch_shapes=[
+            pltpu.VMEM((step_count, topk, tok_dev), jnp.int32),
+            pltpu.VMEM((step_count, topk, tok_dev), jnp.float32),
+            pltpu.SemaphoreType.DMA((step_count + 2,)),
+        ],
+        compiler_params=pltpu.CompilerParams(vmem_limit_bytes=2 * MIB),
+    )(
+        core,
+        in_hbm(tokens),
+        in_hbm(routes.transpose(0, 2, 1)),
+        in_hbm(gating.transpose(0, 2, 1)),
+    )
+
+
+def fetch_first(gate_weight, up_weight, after):
+    def kernel(gate_ref, up_ref, after_ref, out_ref, done_ref, sems):
+        done_ref[...] = jnp.zeros_like(done_ref)
+        run_copies(
+            [
+                pltpu.make_async_copy(
+                    (gate_ref, up_ref)[j % 2].at[j // 2], out_ref.at[j], sems.at[j]
+                )
+                for j in range(AHEAD)
+            ]
+        )
+
+    shape = (AHEAD,) + gate_weight.shape[1:]
+    return pl.pallas_call(
+        kernel,
+        in_specs=[HBM_SPEC, HBM_SPEC, HBM_SPEC],
+        out_specs=(VMEM_SPEC, VMEM_SPEC),
+        out_shape=(pltpu.VMEM(shape, gate_weight.dtype), DONE),
+        scratch_shapes=[pltpu.SemaphoreType.DMA((AHEAD,))],
+        compiler_params=pltpu.CompilerParams(vmem_limit_bytes=MIB),
+        cost_estimate=pl.CostEstimate(
+            flops=0, bytes_accessed=2 * AHEAD * gate_weight[0].size, transcendentals=0
+        ),
+    )(in_hbm(gate_weight), in_hbm(up_weight), in_vmem(after))
+
+
+def fetch_part(weight, lower, upper, after):
+    def kernel(weight_ref, after_ref, out_ref, done_ref, sems):
+        done_ref[...] = jnp.zeros_like(done_ref)
+        run_copies(
+            [
+                pltpu.make_async_copy(weight_ref.at[lower + e], out_ref.at[e], sems.at[e])
+                for e in range(upper - lower)
+            ]
+        )
+
+    return pl.pallas_call(
+        kernel,
+        in_specs=[HBM_SPEC, HBM_SPEC],
+        out_specs=(VMEM_SPEC, VMEM_SPEC),
+        out_shape=(pltpu.VMEM((upper - lower,) + weight.shape[1:], weight.dtype), DONE),
+        scratch_shapes=[pltpu.SemaphoreType.DMA((upper - lower,))],
+        compiler_params=pltpu.CompilerParams(vmem_limit_bytes=MIB),
+        cost_estimate=pl.CostEstimate(
+            flops=0, bytes_accessed=2 * (upper - lower) * weight[0].size, transcendentals=0
+        ),
+    )(in_hbm(weight), in_vmem(after))
+
+
+def add(out_rows, *terms, after=None):
+    extra = [] if after is None else [in_vmem(after)]
+
+    def kernel(*refs):
+        total = None
+        for ref, (_, lower) in zip(refs, terms):
+            value = ref[lower : lower + out_rows, :].astype(jnp.float32)
+            total = value if total is None else total + value
+        refs[-1][...] = total.astype(jnp.bfloat16)
+
+    return pl.pallas_call(
+        kernel,
+        in_specs=[VMEM_SPEC] * len(terms) + [HBM_SPEC] * len(extra),
+        out_specs=VMEM_SPEC,
+        out_shape=pltpu.VMEM((out_rows, terms[0][0].shape[1]), jnp.bfloat16),
+        compiler_params=pltpu.CompilerParams(vmem_limit_bytes=2 * MIB),
+        cost_estimate=SMALL,
+    )(*[in_vmem(value) for value, _ in terms], *extra)
+
+
+def stack(parts, after):
+    heights = [part.shape[0] for part in parts]
+
+    def kernel(*refs):
+        base = 0
+        for ref, height in zip(refs, heights):
+            refs[-1][base : base + height, :] = ref[...]
+            base += height
+
+    return pl.pallas_call(
+        kernel,
+        in_specs=[VMEM_SPEC] * len(parts) + [HBM_SPEC],
+        out_specs=VMEM_SPEC,
+        out_shape=pltpu.VMEM((sum(heights), parts[0].shape[1]), parts[0].dtype),
+        compiler_params=pltpu.CompilerParams(vmem_limit_bytes=2 * MIB),
+        cost_estimate=SMALL,
+    )(*[in_vmem(part) for part in parts], in_vmem(after))
+
+
+def expert_kernel(
+    topk,
+    cap_cold,
+    cap_hot,
+    place_ref,
+    mine_ref,
+    theirs_ref,
+    gate_ref,
+    up_ref,
+    down_refs,
+    first_ref,
+    keep_near,
+    keep_far,
+    send_near,
+    send_far,
+    rank_rows,
+    weight_rows,
+    counts,
+    gathered,
+    returned,
+    hot_rows,
+    hot_seen,
+    ring,
+    sems,
+):
+    experts_here, features, hidden = gate_ref.shape
+    rows = mine_ref.shape[0]
+    half = features // 2
+    cold_rows = experts_here * cap_cold
+    blocks = 2 * experts_here
+    core = place_ref[1]
+    my_half = pl.ds(pl.multiple_of(core * half, 128), half)
+    other_half = pl.ds(pl.multiple_of((1 - core) * half, 128), half)
+
+    def slot_of(block):
+        return lax.rem(block, RING)
+
+    def refill(block, which):
+        source = (gate_ref, up_ref)[which]
+        slot = slot_of(block)
+        return pltpu.make_async_copy(
+            source.at[lax.div(block, 2)], ring.at[slot], sems.at[slot]
+        )
+
+    for block in range(AHEAD, min(AHEAD + RING, blocks)):
+        refill(block, block % 2).start()
+
+    def gather(selector, target):
+        target[:, my_half] = jnp.dot(
+            selector, mine_ref[:, :half], preferred_element_type=jnp.float32
+        ).astype(jnp.bfloat16)
+        target[:, other_half] = jnp.dot(
+            selector, theirs_ref[:, :half], preferred_element_type=jnp.float32
+        ).astype(jnp.bfloat16)
+
+    def pick(expert, count):
+        slots = lax.broadcasted_iota(jnp.int32, (count, rows), 0).astype(jnp.float32)
+        return jnp.where(rank_rows[pl.ds(expert, 1), :] == slots, 1.0, 0.0)
+
+    hot_seen[0] = -1
+    meta = mine_ref[:, half:].astype(jnp.float32)
+    lane = lax.broadcasted_iota(jnp.int32, (rows, 128), 1)
+    wanted = (place_ref[0] * experts_here + lane).astype(jnp.float32)
+    member = jnp.zeros((rows, 128), jnp.float32)
+    weight = jnp.zeros((rows, 128), jnp.float32)
+    for k in range(topk):
+        gate = (
+            meta[:, topk + k : topk + k + 1]
+            + meta[:, 2 * topk + k : 2 * topk + k + 1]
+            + meta[:, 3 * topk + k : 3 * topk + k + 1]
+        )
+        hit = (meta[:, k : k + 1] == wanted) & (lane < experts_here)
+        member = member + jnp.where(hit, 1.0, 0.0)
+        weight = weight + jnp.where(hit, gate, 0.0)
+    earlier = lax.broadcasted_iota(jnp.int32, (rows, rows), 1) < lax.broadcasted_iota(
+        jnp.int32, (rows, rows), 0
+    )
+    rank = jnp.dot(
+        jnp.where(earlier, 1.0, 0.0).astype(jnp.bfloat16),
+        member.astype(jnp.bfloat16),
+        preferred_element_type=jnp.float32,
+    )
+    rank_rows[...] = jnp.where(member > 0.0, rank, -1.0).T
+    weight_rows[...] = weight.T
+    totals = jnp.sum(member, axis=0, keepdims=True)
+    for e in range(experts_here):
+        counts[e] = totals[0, e].astype(jnp.int32)
+    selector = jnp.concatenate([pick(e, cap_cold) for e in range(experts_here)], axis=0)
+    gather(selector.astype(jnp.bfloat16), gathered)
+
+    def project(expert, which, row_data, fetched):
+        if fetched:
+            return jnp.dot(row_data, first_ref[which], preferred_element_type=jnp.float32)
+        block = 2 * expert + which
+        refill(block, which).wait()
+        value = jnp.dot(row_data, ring[slot_of(block)], preferred_element_type=jnp.float32)
+
+        @pl.when(block + RING < blocks)
+        def _():
+            refill(block + RING, which).start()
+
+        return value
+
+    def visit(expert, fetched, down_ref, base):
+        def forward(row_data, weight_column):
+            gate_proj = project(expert, 0, row_data, fetched)
+            up_proj = project(expert, 1, row_data, fetched)
+            active = (jax.nn.silu(gate_proj) * up_proj).astype(jnp.bfloat16)
+            partial = jnp.dot(
+                active, down_ref[expert - base], preferred_element_type=jnp.float32
+            )
+            return (partial * weight_column).astype(jnp.bfloat16)
+
+        first_row = expert * cap_cold
+        if not isinstance(first_row, int):
+            first_row = pl.multiple_of(first_row, cap_cold)
+        block = pl.ds(first_row, cap_cold)
+        is_hot = counts[expert] > cap_cold
+
+        @pl.when(jnp.logical_not(is_hot))
+        def _():
+            weight_column = jnp.sum(
+                pick(expert, cap_cold) * weight_rows[pl.ds(expert, 1), :],
+                axis=1,
+                keepdims=True,
+            )
+            returned[block, :] = forward(gathered[block, :], weight_column)
+
+        @pl.when(is_hot)
+        def _():
+            selector = pick(expert, cap_hot)
+            gather(selector.astype(jnp.bfloat16), hot_rows)
+            weight_column = jnp.sum(
+                selector * weight_rows[pl.ds(expert, 1), :], axis=1, keepdims=True
+            )
+            returned[block, :] = jnp.zeros((cap_cold, features), jnp.bfloat16)
+            returned[cold_rows:, :] = forward(hot_rows[...], weight_column)
+            hot_seen[0] = expert
+
+    visit(0, True, down_refs[0], 0)
+    base = 0
+    for down_ref in down_refs:
+
+        @pl.loop(max(base, 1), base + down_ref.shape[0])
+        def _(expert):
+            visit(expert, False, down_ref, base)
+
+        base += down_ref.shape[0]
+
+    near = rows // 2
+    spread = jnp.concatenate(
+        [pick(e, cap_cold) for e in range(experts_here)], axis=0
+    ).T.astype(jnp.bfloat16)
+
+    def combine(spread, slots):
+        for start in range(0, half, half // 2):
+            for core_of, near_ref, far_ref in (
+                (core, keep_near, keep_far),
+                (1 - core, send_near, send_far),
+            ):
+                columns = pl.ds(pl.multiple_of(core_of * half + start, 128), half // 2)
+                value = jnp.dot(
+                    spread, returned[:slots, columns], preferred_element_type=jnp.float32
+                ).astype(jnp.bfloat16)
+                near_ref[:, start : start + half // 2] = value[:near]
+                far_ref[:, start : start + half // 2] = value[near:]
+
+    @pl.when(hot_seen[0] < 0)
+    def _():
+        combine(spread, cold_rows)
+
+    @pl.when(hot_seen[0] >= 0)
+    def _():
+        hot_spread = pick(hot_seen[0], cap_hot).T.astype(jnp.bfloat16)
+        combine(jnp.concatenate([spread, hot_spread], axis=1), cold_rows + cap_hot)
+
+
+def run_experts(
+    place, mine, theirs, gate_weight, up_weight, down_parts, first, topk, cap_cold, cap_hot
+):
+    rows = mine.shape[0]
+    experts_here, features, hidden = gate_weight.shape
+    half = features // 2
+    out = pltpu.VMEM((rows // 2, half), jnp.bfloat16)
+    return pl.pallas_call(
+        functools.partial(expert_kernel, topk, cap_cold, cap_hot),
+        in_specs=[
+            pl.BlockSpec(memory_space=pltpu.SMEM),
+            VMEM_SPEC,
+            VMEM_SPEC,
+            HBM_SPEC,
+            HBM_SPEC,
+            [VMEM_SPEC] * len(down_parts),
+            VMEM_SPEC,
+        ],
+        out_specs=[VMEM_SPEC] * 4,
+        out_shape=[out] * 4,
+        scratch_shapes=[
+            pltpu.VMEM((128, rows), jnp.float32),
+            pltpu.VMEM((128, rows), jnp.float32),
+            pltpu.SMEM((experts_here,), jnp.int32),
+            pltpu.VMEM((experts_here * cap_cold, features), jnp.bfloat16),
+            pltpu.VMEM((experts_here * cap_cold + cap_hot, features), jnp.bfloat16),
+            pltpu.VMEM((cap_hot, features), jnp.bfloat16),
+            pltpu.SMEM((1,), jnp.int32),
+            pltpu.VMEM((RING, features, hidden), jnp.bfloat16),
+            pltpu.SemaphoreType.DMA((RING,)),
+        ],
+        compiler_params=pltpu.CompilerParams(vmem_limit_bytes=24 * MIB),
+        cost_estimate=pl.CostEstimate(
+            flops=6 * rows * features * hidden,
+            bytes_accessed=4 * experts_here * features * hidden,
+            transcendentals=0,
+        ),
+    )(
+        place,
+        in_vmem(mine),
+        in_vmem(theirs),
+        in_hbm(gate_weight),
+        in_hbm(up_weight),
+        [in_vmem(part) for part in down_parts],
+        in_vmem(first),
+    )
+
+
+def local(tokens, routes, gating, gate_weight, up_weight, down_weight):
+    step_count, tok_dev, features = tokens.shape
+    topk = routes.shape[2]
+    experts_here = gate_weight.shape[0]
+    devices = lax.axis_size("expert")
+    half = features // 2
+    rows = step_count * tok_dev
+    core = lax.axis_index("tensor").astype(jnp.int32)
+
+    def across(value):
+        return lax.ppermute(value, "tensor", [(0, 1), (1, 0)])
+
+    def trade(value, k):
+        return lax.ppermute(value, "expert", [(i, i ^ k) for i in range(devices)])
+
+    own = prepare(core[None], tokens, routes, gating)
+    there2 = trade(own, 4)
+    there1 = trade(own, 2)
+    beside0 = trade(own, 1)
+    down_a, _ = fetch_part(down_weight, 0, 4, own)
+    there3 = trade(there2, 2)
+    beside12 = trade(jnp.concatenate([there1, there2]), 1)
+    down_b, fetched_b = fetch_part(down_weight, 4, 7, there1)
+    there3 = stack([there3], fetched_b)
+    beside3 = trade(there3, 1)
+    first, fetched_first = fetch_first(gate_weight, up_weight, there3)
+    column = jnp.concatenate([own, there1, there2, there3])
+    beside = stack([beside0, beside12, beside3], fetched_first)
+    down_c, _ = fetch_part(down_weight, 7, 8, beside3)
+    mine = jnp.concatenate([column, beside])
+    theirs = jnp.concatenate([across(column), across(beside)])
+
+    place = jnp.stack([lax.axis_index("expert").astype(jnp.int32), core])
+    keep_near, keep_far, send_near, send_far = run_experts(
+        place,
+        mine,
+        theirs,
+        gate_weight,
+        up_weight,
+        [down_a, down_b, down_c],
+        first,
+        topk,
+        step_count * devices * 2,
+        step_count * devices * (tok_dev * 5 // 8),
+    )
+
+    other_far = across(send_far)
+    other_near = across(send_near)
+    from3 = trade(add(rows, (keep_far, 3 * rows), (other_far, 3 * rows)), 1)
+    from2 = trade(add(rows, (keep_far, 2 * rows), (other_far, 2 * rows)), 1)
+    sum3 = add(rows, (keep_near, 3 * rows), (other_near, 3 * rows), (from3, 0))
+    from01 = trade(add(2 * rows, (keep_far, 0), (other_far, 0), after=sum3), 1)
+    on3 = trade(sum3, 2)
+    sum2 = add(rows, (keep_near, 2 * rows), (other_near, 2 * rows), (from2, 0), (on3, 0))
+    on2 = trade(sum2, 4)
+    sum1 = add(rows, (keep_near, rows), (other_near, rows), (from01, rows))
+    on1 = trade(sum1, 2)
+    total = on2.astype(jnp.float32)
+    for term in (on1, from01[:rows], other_near[:rows], keep_near[:rows]):
+        total = total + term.astype(jnp.float32)
+    return total.astype(jnp.bfloat16).reshape(step_count, tok_dev, half)
 
 
 def expert_block(received, w_gate, w_up, w_down):
@@ -27,7 +494,7 @@
     return jnp.dot(selector, row_data, preferred_element_type=jnp.float32).astype(jnp.bfloat16)
 
 
-def local(tokens, routes, gating, gate_weight, up_weight, down_weight):
+def local_by_slots(tokens, routes, gating, gate_weight, up_weight, down_weight):
     step_count, tok_dev, feature_count = tokens.shape
     topk = routes.shape[2]
     experts_here = gate_weight.shape[0]
@@ -67,6 +534,7 @@
 
 
 def solution(mesh):
+    body = local if mesh.shape["expert"] == 8 else local_by_slots
     in_specs = (
         P(None, ("groups", "expert"), None),
         P(None, ("groups", "expert"), None),
@@ -76,4 +544,4 @@
         P("expert", "tensor", None),
     )
     out_specs = P(None, ("groups", "expert"), "tensor")
-    return jax.shard_map(local, mesh=mesh, in_specs=in_specs, out_specs=out_specs, check_vma=False)
+    return jax.shard_map(body, mesh=mesh, in_specs=in_specs, out_specs=out_specs, check_vma=False)

time: 501 us -> 74.5 us (0.15); the launches traced: 493 us -> 74.8 us
  waiting for transfers between devices: 257 us -> 18.3 us
  matrix products: 104 us -> 0 us
  local copies, waits for them, and re-layouts: 88.2 us -> 0.1 us
  Pallas kernels: 0 us -> 38 us
  between operations: 14 us -> 0.19 us
  other arithmetic: 7.36 us -> 1.47 us
  starting transfers between devices: 21.9 us -> 16.7 us
    all_to_all x4 -> x0, waiting for transfers between devices: 251 us -> none  [the longest x2 127 us: local(): lax.all_to_all(send_buffer, 'expert', split_axis=0, concat_axis=0, tiled=...]
    dot_general x6 -> x0, matrix products: 104 us -> none  [the longest x2 68.5 us: expert_block(): jnp.einsum('nemf,efd->nemd', active, w_down, preferred_element_type=jnp.f...]
    reshape x6 -> x0, local copies, waits for them, and re-layouts: 46.9 us -> none  [the longest x4 30.9 us: local(): pack_rows(send_slot, experts * hot_cap, topk, token_rows)]
    pallas_call x0 -> x14, Pallas kernels: none -> 38 us  [the longest x1 20.9 us: run_experts(): pl.pallas_call(functools.partial(expert_kernel, topk, cap_cold, cap_hot),...]
    all_to_all x4 -> x0, starting transfers between devices: 21.5 us -> none  [the longest x2 12.1 us: local(): lax.all_to_all(send_buffer, 'expert', split_axis=0, concat_axis=0, tiled=...]
    ppermute x0 -> x16, waiting for transfers between devices: none -> 18.3 us  [the longest x12 16.9 us: trade(): return lax.ppermute(value, 'expert', [(i, i ^ k) for i in range(devices)])]
    ppermute x0 -> x16, starting transfers between devices: none -> 16.7 us  [the longest x12 15.6 us: trade(): return lax.ppermute(value, 'expert', [(i, i ^ k) for i in range(devices)])]
    convert_element_type x2 -> x0, local copies, waits for them, and re-layouts: 15.7 us -> none  [expert_block(): jnp.einsum('nemf,efd->nemd', active, w_down, preferred_element_type=jnp.f...]
  transfers between devices with their start and end apart: 6 -> 16, of which waited for: 5 -> 6; matrix products, arithmetic and copies ran while one was open for 36% -> 1% of each run, Pallas kernels for 0% -> 22%
where the time goes in v2:
time: 74.5 us; the launch traced here: 74.8 us
  Pallas kernels  38 us (51%)
  waiting for transfers between devices  18.3 us (25%)
  starting transfers between devices  16.7 us (22%)
  other arithmetic  1.47 us (2%)
    pallas_call x1, Pallas kernels, run_experts(): pl.pallas_call(functools.partial(expert_kernel, topk, cap_cold, cap_hot),...  20.9 us
    ppermute x12, waiting for transfers between devices, trade(): return lax.ppermute(value, 'expert', [(i, i ^ k) for i in range(devices)])  16.9 us
    ppermute x12, starting transfers between devices, trade(): return lax.ppermute(value, 'expert', [(i, i ^ k) for i in range(devices)])  15.6 us
    pallas_call x3, Pallas kernels, fetch_part(): pl.pallas_call(kernel, in_specs=[HBM_SPEC, HBM_SPEC], out_specs=(VMEM_SPE...  12.7 us
    pallas_call x1, Pallas kernels, fetch_first(): pl.pallas_call(kernel, in_specs=[HBM_SPEC, HBM_SPEC, HBM_SPEC], out_specs...  3.18 us
  transfers between devices with their start and end apart: 16, of which 6 were waited for; matrix products, arithmetic and copies ran while one was open for 1% of the time, Pallas kernels for 22%

profile of v2, /device:TPU:0, one launch (start us, length us, event | category | flops | bytes accessed | tf_op | source)
XLA Modules:
  0.0 74.8 jit_solution(8802508189703812441)
XLA Ops:
  0.0 0.9 %shard_map.64.after_ref = bf16[32,1920]{1,0:T(8,128)(2,1)S(1)} custom-call(s32[1]{0:T(128)} %bitcast.1.core_ref, bf16[2,16,3584]{2,1,0:T(8,128)(2,1)} %tokens_ref.1, s32[2,8,16]{2,1,0:T(8,128)} %bitcast.5, f32[2,8,16]{2,1,0:T(8,128)} %bitcast.6), custom_call_target="tpu_custom_call" | custom-call | tf_op jit(solution)/shard_map/pallas_call | solution.py:79
  0.9 3.0 %collective-permute-start.3 = (bf16[32,1920]{1,0:T(8,128)(2,1)S(1)}, bf16[32,1920]{1,0:T(8,128)(2,1)S(1)}, u32[]{:S(2)}, u32[]{:S(2)}) collective-permute-start(bf16[32,1920]{1,0:T(8,128)(2,1)S(1)} %shard_map.64.after_ref), channel_id=1, source_target_pairs={{0,2},{2,0},{4,6},{6,4},{8,10},{10,8},{12,14},{14,12},{1,3},{3,1},... | collective-permute-start | bytes 368648 | tf_op jit(solution)/shard_map/ppermute | solution.py:424
  3.9 2.6 %collective-permute-start.1 = (bf16[32,1920]{1,0:T(8,128)(2,1)S(1)}, bf16[32,1920]{1,0:T(8,128)(2,1)S(1)}, u32[]{:S(2)}, u32[]{:S(2)}) collective-permute-start(bf16[32,1920]{1,0:T(8,128)(2,1)S(1)} %shard_map.64.after_ref), channel_id=1, source_target_pairs={{0,8},{2,10},{4,12},{6,14},{8,0},{10,2},{12,4},{14,6},{1,9},{3,11}... | collective-permute-start | bytes 368648 | tf_op jit(solution)/shard_map/ppermute | solution.py:424
  6.5 1.6 %collective-permute-start = (bf16[32,1920]{1,0:T(8,128)(2,1)S(1)}, bf16[32,1920]{1,0:T(8,128)(2,1)S(1)}, u32[]{:S(2)}, u32[]{:S(2)}) collective-permute-start(bf16[32,1920]{1,0:T(8,128)(2,1)S(1)} %shard_map.64.after_ref), channel_id=1, source_target_pairs={{0,4},{2,6},{4,0},{6,2},{8,12},{10,14},{12,8},{14,10},{1,5},{3,7},... | collective-permute-start | bytes 368648 | tf_op jit(solution)/shard_map/ppermute | solution.py:424
  8.1 5.9 %shard_map.69 = (bf16[4,512,3584]{2,1,0:T(8,128)(2,1)S(1)}, f32[8,128]{1,0:T(8,128)}) custom-call(bf16[8,512,3584]{2,1,0:T(8,128)(2,1)} %weight_ref.5, bf16[32,1920]{1,0:T(8,128)(2,1)S(1)} %shard_map.64.after_ref), custom_call_target="tpu_custom_call" | custom-call | bytes 14680064 | tf_op jit(solution)/shard_map/pallas_call | solution.py:134
  14.0 0.6 pad_add_fusion.place_ref
  14.6 0.0 collective-permute-done.1
  14.6 0.0 collective-permute-done.after_ref
  14.6 0.6 collective-permute-start.4
  15.2 0.4 collective-permute-start.2
  15.7 4.2 %shard_map.65 = (bf16[3,512,3584]{2,1,0:T(8,128)(2,1)S(1)}, f32[8,128]{1,0:T(8,128)S(1)}) custom-call(bf16[8,512,3584]{2,1,0:T(8,128)(2,1)} %weight_ref.5, bf16[32,1920]{1,0:T(8,128)(2,1)S(1)} %collective-permute-done.after_ref), custom_call_target="tpu_custom_call" | custom-call | bytes 11010048 | tf_op jit(solution)/shard_map/pallas_call | solution.py:134
  20.0 0.2 collective-permute-done.2.refs_0_
  20.1 1.6 %collective-permute-start.5 = (bf16[32,1920]{1,0:T(8,128)(2,1)S(1)}, bf16[32,1920]{1,0:T(8,128)(2,1)S(1)}, u32[]{:S(2)}, u32[]{:S(2)}) collective-permute-start(bf16[32,1920]{1,0:T(8,128)(2,1)S(1)} %shard_map.66.after_ref), channel_id=1, source_target_pairs={{0,2},{2,0},{4,6},{6,4},{8,10},{10,8},{12,14},{14,12},{1,3},{3,1},... | collective-permute-start | bytes 368648 | tf_op jit(solution)/shard_map/ppermute | solution.py:424
  21.7 0.1 collective-permute-start.6
  21.8 3.2 %shard_map.67 = (bf16[2,3584,512]{2,1,0:T(8,128)(2,1)S(1)}, f32[8,128]{1,0:T(8,128)S(1)}) custom-call(bf16[8,3584,512]{2,1,0:T(8,128)(2,1)} %gate_ref.3, bf16[8,3584,512]{2,1,0:T(8,128)(2,1)} %up_ref.3, bf16[32,1920]{1,0:T(8,128)(2,1)S(1)} %shard_map.66.after_ref), custom_call_target="tpu_custom_call" | custom-call | bytes 7340032 | tf_op jit(solution)/shard_map/pallas_call | solution.py:111
  25.0 0.0 collective-permute-done.3.refs_0_
  25.0 0.0 collective-permute-done.4.refs_1_
  25.0 0.1 collective-permute-done.5.refs_2_.after_ref
  25.1 0.5 collective-permute-start.7
  25.7 2.6 %shard_map.70 = (bf16[1,512,3584]{2,1,0:T(8,128)(2,1)S(1)}, f32[8,128]{1,0:T(8,128)}) custom-call(bf16[8,512,3584]{2,1,0:T(8,128)(2,1)} %weight_ref.5, bf16[32,1920]{1,0:T(8,128)(2,1)S(1)} %collective-permute-done.5.refs_2_.after_ref), custom_call_target="tpu_custom_call" | custom-call | bytes 3670016 | tf_op jit(solution)/shard_map/pallas_call | solution.py:134
  28.4 0.0 collective-permute-done.6
  28.4 0.0 collective-permute-done.7
  28.4 0.1 pad_maximum_fusion.theirs_ref
  28.5 20.9 %shard_map.71 = (bf16[128,1792]{1,0:T(8,128)(2,1)S(1)}, bf16[128,1792]{1,0:T(8,128)(2,1)S(1)}, bf16[128,1792]{1,0:T(8,128)(2,1)S(1)}, bf16[128,1792]{1,0:T(8,128)(2,1)S(1)}) custom-call(s32[2]{0:T(128)} %pad_add_fusion.place_ref, bf16[256,1920]{1,0:T(8,128)(2,1)S(1)} %constant_dynamic-update-slice_fusion.mine_ref, ...), custom_call_target="tpu_custom_call" | custom-call | flops 2818572288 | bytes 58720256 | tf_op jit(solution)/shard_map/pallas_call | solution.py:370
  49.4 0.1 collective-permute-start.9
  49.5 0.4 collective-permute-start.8
  49.9 1.3 %collective-permute-done.9.refs_1_ = bf16[128,1792]{1,0:T(8,128)(2,1)S(1)} collective-permute-done((bf16[128,1792]{1,0:T(8,128)(2,1)S(1)}, bf16[128,1792]{1,0:T(8,128)(2,1)S(1)}, u32[]{:S(2)}, u32[]{:S(2)}) %collective-permute-start.9) | collective-permute-done | bytes 458784 | tf_op jit(solution)/shard_map/ppermute | solution.py:421
  51.3 2.3 %collective-permute-start.11 = (bf16[32,1792]{1,0:T(8,128)(2,1)S(1)}, bf16[32,1792]{1,0:T(8,128)(2,1)S(1)}, u32[]{:S(2)}, u32[]{:S(2)}) collective-permute-start(bf16[32,1792]{1,0:T(8,128)(2,1)S(1)} %shard_map.73), channel_id=1, source_target_pairs={{0,2},{2,0},{4,6},{6,4},{8,10},{10,8},{12,14},{14,12},{1,3},{3,1},... | collective-permute-start | bytes 344072 | tf_op jit(solution)/shard_map/ppermute | solution.py:424
  53.6 0.0 collective-permute-done.8.refs_1_
  53.6 3.7 %collective-permute-done.11.refs_2_ = bf16[32,1792]{1,0:T(8,128)(2,1)S(1)} collective-permute-done((bf16[32,1792]{1,0:T(8,128)(2,1)S(1)}, bf16[32,1792]{1,0:T(8,128)(2,1)S(1)}, u32[]{:S(2)}, u32[]{:S(2)}) %collective-permute-start.11) | collective-permute-done | bytes 114720 | tf_op jit(solution)/shard_map/ppermute | solution.py:424
  57.3 0.1 shard_map.76
  57.4 1.8 %collective-permute-start.14 = (bf16[64,1792]{1,0:T(8,128)(2,1)S(1)}, bf16[64,1792]{1,0:T(8,128)(2,1)S(1)}, u32[]{:S(2)}, u32[]{:S(2)}) collective-permute-start(bf16[64,1792]{1,0:T(8,128)(2,1)S(1)} %shard_map.76), channel_id=1, source_target_pairs={{0,2},{2,0},{4,6},{6,4},{8,10},{10,8},{12,14},{14,12},{1,3},{3,1},... | collective-permute-start | bytes 688136 | tf_op jit(solution)/shard_map/ppermute | solution.py:424
  59.2 0.4 collective-permute-start.10
  59.6 0.7 collective-permute-start.12
  60.2 7.0 %collective-permute-done.10.refs_2_ = bf16[32,1792]{1,0:T(8,128)(2,1)S(1)} collective-permute-done((bf16[32,1792]{1,0:T(8,128)(2,1)S(1)}, bf16[32,1792]{1,0:T(8,128)(2,1)S(1)}, u32[]{:S(2)}, u32[]{:S(2)}) %collective-permute-start.10) | collective-permute-done | bytes 114720 | tf_op jit(solution)/shard_map/ppermute | solution.py:424
  67.2 0.0 collective-permute-done.12.refs_3_
  67.2 0.1 shard_map.75
  67.3 0.1 collective-permute-start.13
  67.4 0.0 collective-permute-done.14.refs_2_
  67.4 0.6 collective-permute-start.15
  68.0 6.0 %collective-permute-done.13 = bf16[32,1792]{1,0:T(8,128)(2,1)S(1)} collective-permute-done((bf16[32,1792]{1,0:T(8,128)(2,1)S(1)}, bf16[32,1792]{1,0:T(8,128)(2,1)S(1)}, u32[]{:S(2)}, u32[]{:S(2)}) %collective-permute-start.13) | collective-permute-done | bytes 114720 | tf_op jit(solution)/shard_map/ppermute | solution.py:424
  74.0 0.0 collective-permute-done.15
  74.0 0.7 add_convert_fusion
  (13 shorter events, 0.4 us)
Async XLA Ops:
  0.9 24.1 %collective-permute-start.3 = (bf16[32,1920]{1,0:T(8,128)(2,1)S(1)}, bf16[32,1920]{1,0:T(8,128)(2,1)S(1)}, u32[]{:S(2)}, u32[]{:S(2)}) collective-permute-start(bf16[32,1920]{1,0:T(8,128)(2,1)S(1)} %shard_map.64.after_ref), channel_id=1, source_target_pairs={{0,2},{2,0},{4,6},{6,4},{8,10},{10,8},{12,14},{14,12},{1,3},{3,1},... | collective-permute-start | bytes 368648 | tf_op jit(solution)/shard_map/ppermute | solution.py:424
  3.9 10.7 %collective-permute-start.1 = (bf16[32,1920]{1,0:T(8,128)(2,1)S(1)}, bf16[32,1920]{1,0:T(8,128)(2,1)S(1)}, u32[]{:S(2)}, u32[]{:S(2)}) collective-permute-start(bf16[32,1920]{1,0:T(8,128)(2,1)S(1)} %shard_map.64.after_ref), channel_id=1, source_target_pairs={{0,8},{2,10},{4,12},{6,14},{8,0},{10,2},{12,4},{14,6},{1,9},{3,11}... | collective-permute-start | bytes 368648 | tf_op jit(solution)/shard_map/ppermute | solution.py:424
  6.5 8.1 %collective-permute-start = (bf16[32,1920]{1,0:T(8,128)(2,1)S(1)}, bf16[32,1920]{1,0:T(8,128)(2,1)S(1)}, u32[]{:S(2)}, u32[]{:S(2)}) collective-permute-start(bf16[32,1920]{1,0:T(8,128)(2,1)S(1)} %shard_map.64.after_ref), channel_id=1, source_target_pairs={{0,4},{2,6},{4,0},{6,2},{8,12},{10,14},{12,8},{14,10},{1,5},{3,7},... | collective-permute-start | bytes 368648 | tf_op jit(solution)/shard_map/ppermute | solution.py:424
  14.6 10.4 %collective-permute-start.4 = (bf16[64,1920]{1,0:T(8,128)(2,1)S(1)}, bf16[64,1920]{1,0:T(8,128)(2,1)S(1)}, u32[]{:S(2)}, u32[]{:S(2)}) collective-permute-start(bf16[64,1920]{1,0:T(8,128)(2,1)S(1)} %pad_maximum_fusion.2), channel_id=1, source_target_pairs={{0,2},{2,0},{4,6},{6,4},{8,10},{10,8},{12,14},{14,12},{1,3},{3,1},... | collective-permute-start | bytes 737288 | tf_op jit(solution)/shard_map/ppermute | solution.py:424
  15.2 4.9 %collective-permute-start.2 = (bf16[32,1920]{1,0:T(8,128)(2,1)S(1)}, bf16[32,1920]{1,0:T(8,128)(2,1)S(1)}, u32[]{:S(2)}, u32[]{:S(2)}) collective-permute-start(bf16[32,1920]{1,0:T(8,128)(2,1)S(1)} %collective-permute-done.1), channel_id=1, source_target_pairs={{0,4},{2,6},{4,0},{6,2},{8,12},{10,14},{12,8},{14,10},{1,5},{3,7},... | collective-permute-start | bytes 368648 | tf_op jit(solution)/shard_map/ppermute | solution.py:424
  20.1 4.9 %collective-permute-start.5 = (bf16[32,1920]{1,0:T(8,128)(2,1)S(1)}, bf16[32,1920]{1,0:T(8,128)(2,1)S(1)}, u32[]{:S(2)}, u32[]{:S(2)}) collective-permute-start(bf16[32,1920]{1,0:T(8,128)(2,1)S(1)} %shard_map.66.after_ref), channel_id=1, source_target_pairs={{0,2},{2,0},{4,6},{6,4},{8,10},{10,8},{12,14},{14,12},{1,3},{3,1},... | collective-permute-start | bytes 368648 | tf_op jit(solution)/shard_map/ppermute | solution.py:424
  21.7 6.6 %collective-permute-start.6 = (bf16[128,1920]{1,0:T(8,128)(2,1)S(1)}, bf16[128,1920]{1,0:T(8,128)(2,1)S(1)}, u32[]{:S(2)}, u32[]{:S(2)}) collective-permute-start(bf16[128,1920]{1,0:T(8,128)(2,1)S(1)} %pad_maximum_fusion.1), channel_id=1, source_target_pairs={{0,1},{1,0},{2,3},{3,2},{4,5},{5,4},{6,7},{7,6},{8,9},{9,8},{10,11... | collective-permute-start | bytes 1474568 | tf_op jit(solution)/shard_map/ppermute | solution.py:421
  25.1 3.3 %collective-permute-start.7 = (bf16[128,1920]{1,0:T(8,128)(2,1)S(1)}, bf16[128,1920]{1,0:T(8,128)(2,1)S(1)}, u32[]{:S(2)}, u32[]{:S(2)}) collective-permute-start(bf16[128,1920]{1,0:T(8,128)(2,1)S(1)} %shard_map.68), channel_id=1, source_target_pairs={{0,1},{1,0},{2,3},{3,2},{4,5},{5,4},{6,7},{7,6},{8,9},{9,8},{10,11... | collective-permute-start | bytes 1474568 | tf_op jit(solution)/shard_map/ppermute | solution.py:421
  49.4 1.9 %collective-permute-start.9 = (bf16[128,1792]{1,0:T(8,128)(2,1)S(1)}, bf16[128,1792]{1,0:T(8,128)(2,1)S(1)}, u32[]{:S(2)}, u32[]{:S(2)}) collective-permute-start(bf16[128,1792]{1,0:T(8,128)(2,1)S(1)} %get-tuple-element.24), channel_id=1, source_target_pairs={{0,1},{1,0},{2,3},{3,2},{4,5},{5,4},{6,7},{7,6},{8,9},{9,8},{10,11... | collective-permute-start | bytes 1376264 | tf_op jit(solution)/shard_map/ppermute | solution.py:421
  49.5 4.1 %collective-permute-start.8 = (bf16[128,1792]{1,0:T(8,128)(2,1)S(1)}, bf16[128,1792]{1,0:T(8,128)(2,1)S(1)}, u32[]{:S(2)}, u32[]{:S(2)}) collective-permute-start(bf16[128,1792]{1,0:T(8,128)(2,1)S(1)} %get-tuple-element.22), channel_id=1, source_target_pairs={{0,1},{1,0},{2,3},{3,2},{4,5},{5,4},{6,7},{7,6},{8,9},{9,8},{10,11... | collective-permute-start | bytes 1376264 | tf_op jit(solution)/shard_map/ppermute | solution.py:421
  51.3 6.0 %collective-permute-start.11 = (bf16[32,1792]{1,0:T(8,128)(2,1)S(1)}, bf16[32,1792]{1,0:T(8,128)(2,1)S(1)}, u32[]{:S(2)}, u32[]{:S(2)}) collective-permute-start(bf16[32,1792]{1,0:T(8,128)(2,1)S(1)} %shard_map.73), channel_id=1, source_target_pairs={{0,2},{2,0},{4,6},{6,4},{8,10},{10,8},{12,14},{14,12},{1,3},{3,1},... | collective-permute-start | bytes 344072 | tf_op jit(solution)/shard_map/ppermute | solution.py:424
  57.4 10.0 %collective-permute-start.14 = (bf16[64,1792]{1,0:T(8,128)(2,1)S(1)}, bf16[64,1792]{1,0:T(8,128)(2,1)S(1)}, u32[]{:S(2)}, u32[]{:S(2)}) collective-permute-start(bf16[64,1792]{1,0:T(8,128)(2,1)S(1)} %shard_map.76), channel_id=1, source_target_pairs={{0,2},{2,0},{4,6},{6,4},{8,10},{10,8},{12,14},{14,12},{1,3},{3,1},... | collective-permute-start | bytes 688136 | tf_op jit(solution)/shard_map/ppermute | solution.py:424
  59.2 8.0 %collective-permute-start.10 = (bf16[32,1792]{1,0:T(8,128)(2,1)S(1)}, bf16[32,1792]{1,0:T(8,128)(2,1)S(1)}, u32[]{:S(2)}, u32[]{:S(2)}) collective-permute-start(bf16[32,1792]{1,0:T(8,128)(2,1)S(1)} %shard_map.72), channel_id=1, source_target_pairs={{0,2},{2,0},{4,6},{6,4},{8,10},{10,8},{12,14},{14,12},{1,3},{3,1},... | collective-permute-start | bytes 344072 | tf_op jit(solution)/shard_map/ppermute | solution.py:424
  59.6 7.6 %collective-permute-start.12 = (bf16[32,1792]{1,0:T(8,128)(2,1)S(1)}, bf16[32,1792]{1,0:T(8,128)(2,1)S(1)}, u32[]{:S(2)}, u32[]{:S(2)}) collective-permute-start(bf16[32,1792]{1,0:T(8,128)(2,1)S(1)} %shard_map.74.refs_2_), channel_id=1, source_target_pairs={{0,4},{2,6},{4,0},{6,2},{8,12},{10,14},{12,8},{14,10},{1,5},{3,7},... | collective-permute-start | bytes 344072 | tf_op jit(solution)/shard_map/ppermute | solution.py:424
  67.3 6.7 %collective-permute-start.13 = (bf16[32,1792]{1,0:T(8,128)(2,1)S(1)}, bf16[32,1792]{1,0:T(8,128)(2,1)S(1)}, u32[]{:S(2)}, u32[]{:S(2)}) collective-permute-start(bf16[32,1792]{1,0:T(8,128)(2,1)S(1)} %shard_map.75), channel_id=1, source_target_pairs={{0,8},{2,10},{4,12},{6,14},{8,0},{10,2},{12,4},{14,6},{1,9},{3,11}... | collective-permute-start | bytes 344072 | tf_op jit(solution)/shard_map/ppermute | solution.py:424
  67.4 6.6 %collective-permute-start.15 = (bf16[32,1792]{1,0:T(8,128)(2,1)S(1)}, bf16[32,1792]{1,0:T(8,128)(2,1)S(1)}, u32[]{:S(2)}, u32[]{:S(2)}) collective-permute-start(bf16[32,1792]{1,0:T(8,128)(2,1)S(1)} %shard_map.77), channel_id=1, source_target_pairs={{0,4},{2,6},{4,0},{6,2},{8,12},{10,14},{12,8},{14,10},{1,5},{3,7},... | collective-permute-start | bytes 344072 | tf_op jit(solution)/shard_map/ppermute | solution.py:424

commit v3 on v2

--- a/solution.py
+++ b/solution.py
@@ -8,8 +8,8 @@
 from jax.sharding import PartitionSpec as P
 
 META = 128
-AHEAD = 2
-RING = 4
+RING = 6
+FETCHED = (4, 6)
 MIB = 1024 * 1024
 
 
@@ -34,13 +34,13 @@
         copy.wait()
 
 
-def prepare(core, tokens, routes, gating):
+def prepare(tokens, routes, gating):
     step_count, tok_dev, features = tokens.shape
     topk = routes.shape[2]
     half = features // 2
 
-    def kernel(core_ref, tokens_ref, routes_hbm, gating_hbm, out_ref, routes_ref, gating_ref, sems):
-        columns = pl.ds(pl.multiple_of(core_ref[0] * half, 128), half)
+    def kernel(tokens_ref, routes_hbm, gating_hbm, out_ref, routes_ref, gating_ref, sems):
+        columns = pl.ds(pl.multiple_of(lax.axis_index("tensor") * half, 128), half)
         copies = [
             pltpu.make_async_copy(
                 tokens_ref.at[s, :, columns],
@@ -78,7 +78,7 @@
 
     return pl.pallas_call(
         kernel,
-        in_specs=[pl.BlockSpec(memory_space=pltpu.SMEM), HBM_SPEC, HBM_SPEC, HBM_SPEC],
+        in_specs=[HBM_SPEC, HBM_SPEC, HBM_SPEC],
         out_specs=VMEM_SPEC,
         out_shape=pltpu.VMEM((step_count * tok_dev, half + META), jnp.bfloat16),
         scratch_shapes=[
@@ -88,37 +88,10 @@
         ],
         compiler_params=pltpu.CompilerParams(vmem_limit_bytes=2 * MIB),
     )(
-        core,
         in_hbm(tokens),
         in_hbm(routes.transpose(0, 2, 1)),
         in_hbm(gating.transpose(0, 2, 1)),
     )
-
-
-def fetch_first(gate_weight, up_weight, after):
-    def kernel(gate_ref, up_ref, after_ref, out_ref, done_ref, sems):
-        done_ref[...] = jnp.zeros_like(done_ref)
-        run_copies(
-            [
-                pltpu.make_async_copy(
-                    (gate_ref, up_ref)[j % 2].at[j // 2], out_ref.at[j], sems.at[j]
-                )
-                for j in range(AHEAD)
-            ]
-        )
-
-    shape = (AHEAD,) + gate_weight.shape[1:]
-    return pl.pallas_call(
-        kernel,
-        in_specs=[HBM_SPEC, HBM_SPEC, HBM_SPEC],
-        out_specs=(VMEM_SPEC, VMEM_SPEC),
-        out_shape=(pltpu.VMEM(shape, gate_weight.dtype), DONE),
-        scratch_shapes=[pltpu.SemaphoreType.DMA((AHEAD,))],
-        compiler_params=pltpu.CompilerParams(vmem_limit_bytes=MIB),
-        cost_estimate=pl.CostEstimate(
-            flops=0, bytes_accessed=2 * AHEAD * gate_weight[0].size, transcendentals=0
-        ),
-    )(in_hbm(gate_weight), in_hbm(up_weight), in_vmem(after))
 
 
 def fetch_part(weight, lower, upper, after):
@@ -187,13 +160,12 @@
     topk,
     cap_cold,
     cap_hot,
-    place_ref,
     mine_ref,
     theirs_ref,
     gate_ref,
     up_ref,
+    down_ref_hbm,
     down_refs,
-    first_ref,
     keep_near,
     keep_far,
     send_near,
@@ -207,13 +179,15 @@
     hot_seen,
     ring,
     sems,
+    down_ring,
+    down_sems,
 ):
     experts_here, features, hidden = gate_ref.shape
     rows = mine_ref.shape[0]
     half = features // 2
     cold_rows = experts_here * cap_cold
     blocks = 2 * experts_here
-    core = place_ref[1]
+    core = lax.axis_index("tensor")
     my_half = pl.ds(pl.multiple_of(core * half, 128), half)
     other_half = pl.ds(pl.multiple_of((1 - core) * half, 128), half)
 
@@ -227,7 +201,7 @@
             source.at[lax.div(block, 2)], ring.at[slot], sems.at[slot]
         )
 
-    for block in range(AHEAD, min(AHEAD + RING, blocks)):
+    for block in range(min(RING, blocks)):
         refill(block, block % 2).start()
 
     def gather(selector, target):
@@ -245,7 +219,7 @@
     hot_seen[0] = -1
     meta = mine_ref[:, half:].astype(jnp.float32)
     lane = lax.broadcasted_iota(jnp.int32, (rows, 128), 1)
-    wanted = (place_ref[0] * experts_here + lane).astype(jnp.float32)
+    wanted = (lax.axis_index("expert") * experts_here + lane).astype(jnp.float32)
     member = jnp.zeros((rows, 128), jnp.float32)
     weight = jnp.zeros((rows, 128), jnp.float32)
     for k in range(topk):
@@ -271,11 +245,15 @@
     for e in range(experts_here):
         counts[e] = totals[0, e].astype(jnp.int32)
     selector = jnp.concatenate([pick(e, cap_cold) for e in range(experts_here)], axis=0)
-    gather(selector.astype(jnp.bfloat16), gathered)
-
-    def project(expert, which, row_data, fetched):
-        if fetched:
-            return jnp.dot(row_data, first_ref[which], preferred_element_type=jnp.float32)
+    gather(selector.astype(jnp.bfloat16), gathered.at[:cold_rows])
+
+    def stream(expert):
+        place = expert - FETCHED[1]
+        return pltpu.make_async_copy(
+            down_ref_hbm.at[expert], down_ring.at[place], down_sems.at[place]
+        )
+
+    def project(expert, which, row_data):
         block = 2 * expert + which
         refill(block, which).wait()
         value = jnp.dot(row_data, ring[slot_of(block)], preferred_element_type=jnp.float32)
@@ -286,21 +264,27 @@
 
         return value
 
-    def visit(expert, fetched, down_ref, base):
-        def forward(row_data, weight_column):
-            gate_proj = project(expert, 0, row_data, fetched)
-            up_proj = project(expert, 1, row_data, fetched)
+    def visit(expert, down_ref, base, streamed):
+        def forward(row_data, weight_column, count):
+            gate_proj = project(expert, 0, row_data)[:count]
+            up_proj = project(expert, 1, row_data)[:count]
             active = (jax.nn.silu(gate_proj) * up_proj).astype(jnp.bfloat16)
+            if streamed:
+                stream(expert).wait()
             partial = jnp.dot(
                 active, down_ref[expert - base], preferred_element_type=jnp.float32
             )
             return (partial * weight_column).astype(jnp.bfloat16)
 
-        first_row = expert * cap_cold
-        if not isinstance(first_row, int):
-            first_row = pl.multiple_of(first_row, cap_cold)
+        first_row = pl.multiple_of(expert * cap_cold, cap_cold)
         block = pl.ds(first_row, cap_cold)
+        wide = pl.ds(first_row, 4 * cap_cold)
         is_hot = counts[expert] > cap_cold
+
+        @pl.when((expert + 2 >= FETCHED[1]) & (expert + 2 < experts_here))
+        def _():
+            stream(expert + 2).start()
+
 
         @pl.when(jnp.logical_not(is_hot))
         def _():
@@ -309,7 +293,7 @@
                 axis=1,
                 keepdims=True,
             )
-            returned[block, :] = forward(gathered[block, :], weight_column)
+            returned[block, :] = forward(gathered[wide, :], weight_column, cap_cold)
 
         @pl.when(is_hot)
         def _():
@@ -319,16 +303,15 @@
                 selector * weight_rows[pl.ds(expert, 1), :], axis=1, keepdims=True
             )
             returned[block, :] = jnp.zeros((cap_cold, features), jnp.bfloat16)
-            returned[cold_rows:, :] = forward(hot_rows[...], weight_column)
+            returned[cold_rows:, :] = forward(hot_rows[...], weight_column, cap_hot)
             hot_seen[0] = expert
 
-    visit(0, True, down_refs[0], 0)
     base = 0
-    for down_ref in down_refs:
-
-        @pl.loop(max(base, 1), base + down_ref.shape[0])
+    for down_ref, streamed in [(ref, False) for ref in down_refs] + [(down_ring, True)]:
+
+        @pl.loop(base, base + down_ref.shape[0])
         def _(expert):
-            visit(expert, False, down_ref, base)
+            visit(expert, down_ref, base, streamed)
 
         base += down_ref.shape[0]
 
@@ -361,7 +344,7 @@
 
 
 def run_experts(
-    place, mine, theirs, gate_weight, up_weight, down_parts, first, topk, cap_cold, cap_hot
+    mine, theirs, gate_weight, up_weight, down_weight, down_parts, topk, cap_cold, cap_hot
 ):
     rows = mine.shape[0]
     experts_here, features, hidden = gate_weight.shape
@@ -370,13 +353,12 @@
     return pl.pallas_call(
         functools.partial(expert_kernel, topk, cap_cold, cap_hot),
         in_specs=[
-            pl.BlockSpec(memory_space=pltpu.SMEM),
             VMEM_SPEC,
             VMEM_SPEC,
             HBM_SPEC,
             HBM_SPEC,
+            HBM_SPEC,
             [VMEM_SPEC] * len(down_parts),
-            VMEM_SPEC,
         ],
         out_specs=[VMEM_SPEC] * 4,
         out_shape=[out] * 4,
@@ -384,27 +366,28 @@
             pltpu.VMEM((128, rows), jnp.float32),
             pltpu.VMEM((128, rows), jnp.float32),
             pltpu.SMEM((experts_here,), jnp.int32),
-            pltpu.VMEM((experts_here * cap_cold, features), jnp.bfloat16),
+            pltpu.VMEM(((experts_here + 3) * cap_cold, features), jnp.bfloat16),
             pltpu.VMEM((experts_here * cap_cold + cap_hot, features), jnp.bfloat16),
             pltpu.VMEM((cap_hot, features), jnp.bfloat16),
             pltpu.SMEM((1,), jnp.int32),
             pltpu.VMEM((RING, features, hidden), jnp.bfloat16),
             pltpu.SemaphoreType.DMA((RING,)),
+            pltpu.VMEM((experts_here - FETCHED[1], hidden, features), jnp.bfloat16),
+            pltpu.SemaphoreType.DMA((experts_here - FETCHED[1],)),
         ],
-        compiler_params=pltpu.CompilerParams(vmem_limit_bytes=24 * MIB),
+        compiler_params=pltpu.CompilerParams(vmem_limit_bytes=38 * MIB),
         cost_estimate=pl.CostEstimate(
             flops=6 * rows * features * hidden,
             bytes_accessed=4 * experts_here * features * hidden,
             transcendentals=0,
         ),
     )(
-        place,
         in_vmem(mine),
         in_vmem(theirs),
         in_hbm(gate_weight),
         in_hbm(up_weight),
+        in_hbm(down_weight),
         [in_vmem(part) for part in down_parts],
-        in_vmem(first),
     )
 
 
@@ -415,7 +398,6 @@
     devices = lax.axis_size("expert")
     half = features // 2
     rows = step_count * tok_dev
-    core = lax.axis_index("tensor").astype(jnp.int32)
 
     def across(value):
         return lax.ppermute(value, "tensor", [(0, 1), (1, 0)])
@@ -423,32 +405,29 @@
     def trade(value, k):
         return lax.ppermute(value, "expert", [(i, i ^ k) for i in range(devices)])
 
-    own = prepare(core[None], tokens, routes, gating)
+    own = prepare(tokens, routes, gating)
     there2 = trade(own, 4)
     there1 = trade(own, 2)
     beside0 = trade(own, 1)
-    down_a, _ = fetch_part(down_weight, 0, 4, own)
+    beside1 = trade(own, 3)
+    down_a, fetched_a = fetch_part(down_weight, 0, FETCHED[0], own)
     there3 = trade(there2, 2)
-    beside12 = trade(jnp.concatenate([there1, there2]), 1)
-    down_b, fetched_b = fetch_part(down_weight, 4, 7, there1)
-    there3 = stack([there3], fetched_b)
-    beside3 = trade(there3, 1)
-    first, fetched_first = fetch_first(gate_weight, up_weight, there3)
-    column = jnp.concatenate([own, there1, there2, there3])
-    beside = stack([beside0, beside12, beside3], fetched_first)
-    down_c, _ = fetch_part(down_weight, 7, 8, beside3)
-    mine = jnp.concatenate([column, beside])
-    theirs = jnp.concatenate([across(column), across(beside)])
-
-    place = jnp.stack([lax.axis_index("expert").astype(jnp.int32), core])
+    beside3 = trade(there2, 3)
+    beside2 = trade(there2, 1)
+    early = stack([own, there1, there2, beside0, beside1], fetched_a)
+    other_early = across(early)
+    down_b, fetched_b = fetch_part(down_weight, FETCHED[0], FETCHED[1], there2)
+    late = stack([there3, beside2, beside3], fetched_b)
+    mine = jnp.concatenate([early, late])
+    theirs = jnp.concatenate([other_early, across(late)])
+
     keep_near, keep_far, send_near, send_far = run_experts(
-        place,
         mine,
         theirs,
         gate_weight,
         up_weight,
-        [down_a, down_b, down_c],
-        first,
+        down_weight,
+        [down_a, down_b],
         topk,
         step_count * devices * 2,
         step_count * devices * (tok_dev * 5 // 8),
@@ -456,17 +435,25 @@
 
     other_far = across(send_far)
     other_near = across(send_near)
-    from3 = trade(add(rows, (keep_far, 3 * rows), (other_far, 3 * rows)), 1)
-    from2 = trade(add(rows, (keep_far, 2 * rows), (other_far, 2 * rows)), 1)
-    sum3 = add(rows, (keep_near, 3 * rows), (other_near, 3 * rows), (from3, 0))
-    from01 = trade(add(2 * rows, (keep_far, 0), (other_far, 0), after=sum3), 1)
-    on3 = trade(sum3, 2)
-    sum2 = add(rows, (keep_near, 2 * rows), (other_near, 2 * rows), (from2, 0), (on3, 0))
+
+    def both(place, after=None):
+        keep, other = (keep_near, other_near) if place < 4 else (keep_far, other_far)
+        lower = (place % 4) * rows
+        return add(rows, (keep, lower), (other, lower), after=after)
+
+    from2 = trade(both(6), 1)
+    from3 = trade(both(7), 3)
+    from_there3 = trade(both(5), 2)
+    from1 = trade(both(4, other_near), 3)
+    from0 = trade(both(3), 1)
+    from_there1 = trade(both(1), 2)
+    far2 = 2 * rows
+    sum2 = add(
+        rows, (keep_near, far2), (other_near, far2), (from2, 0), (from3, 0), (from_there3, 0)
+    )
     on2 = trade(sum2, 4)
-    sum1 = add(rows, (keep_near, rows), (other_near, rows), (from01, rows))
-    on1 = trade(sum1, 2)
     total = on2.astype(jnp.float32)
-    for term in (on1, from01[:rows], other_near[:rows], keep_near[:rows]):
+    for term in (from1, from0, from_there1, other_near[:rows], keep_near[:rows]):
         total = total + term.astype(jnp.float32)
     return total.astype(jnp.bfloat16).reshape(step_count, tok_dev, half)
 

time: 74.5 us -> 69.4 us (0.932)
  Pallas kernels: 38 us -> 32.6 us
  starting transfers between devices: 16.7 us -> 21.4 us
  waiting for transfers between devices: 18.3 us -> 14.2 us
    ppermute x12 -> x14, waiting for transfers between devices: 16.9 us -> 11.3 us  [trade(): return lax.ppermute(value, 'expert', [(i, i ^ k) for i in range(devices)])]
    ppermute x12 -> x14, starting transfers between devices: 15.6 us -> 20.7 us  [trade(): return lax.ppermute(value, 'expert', [(i, i ^ k) for i in range(devices)])]
    pallas_call x3 -> x2, Pallas kernels: 12.7 us -> 8.45 us  [fetch_part(): pl.pallas_call(kernel, in_specs=[HBM_SPEC, HBM_SPEC], out_specs=(VMEM_SPE...]
    pallas_call x2 -> x1, Pallas kernels: 4.09 us -> 0.91 us  [prepare(): pl.pallas_call(kernel, in_specs=[HBM_SPEC, HBM_SPEC, HBM_SPEC], out_specs...]
    pallas_call x1, Pallas kernels: 20.9 us -> 22.9 us  [run_experts(): pl.pallas_call(functools.partial(expert_kernel, topk, cap_cold, cap_hot),...]
    ppermute x4, waiting for transfers between devices: 1.31 us -> 2.9 us  [across(): return lax.ppermute(value, 'tensor', [(0, 1), (1, 0)])]
  transfers between devices with their start and end apart: 16 -> 18, of which waited for: 6 -> 9; matrix products, arithmetic and copies ran while one was open for 1% -> 0% of each run, Pallas kernels for 22% -> 13%
where the time goes in v3:
time: 69.4 us; the launch traced here: 69.2 us
  Pallas kernels  32.6 us (47%)
  starting transfers between devices  21.4 us (31%)
  waiting for transfers between devices  14.2 us (20%)
  other arithmetic  0.89 us (1%)
    pallas_call x1, Pallas kernels, run_experts(): pl.pallas_call(functools.partial(expert_kernel, topk, cap_cold, cap_hot),...  22.9 us
    ppermute x14, starting transfers between devices, trade(): return lax.ppermute(value, 'expert', [(i, i ^ k) for i in range(devices)])  20.7 us
    ppermute x14, waiting for transfers between devices, trade(): return lax.ppermute(value, 'expert', [(i, i ^ k) for i in range(devices)])  11.3 us
    pallas_call x2, Pallas kernels, fetch_part(): pl.pallas_call(kernel, in_specs=[HBM_SPEC, HBM_SPEC], out_specs=(VMEM_SPE...  8.45 us
    ppermute x4, waiting for transfers between devices, across(): return lax.ppermute(value, 'tensor', [(0, 1), (1, 0)])  2.9 us
  transfers between devices with their start and end apart: 18, of which 9 were waited for; matrix products, arithmetic and copies ran while one was open for 0% of the time, Pallas kernels for 13%

profile of v3, /device:TPU:0, one launch (start us, length us, event | category | flops | bytes accessed | tf_op | source)
XLA Modules:
  0.0 69.2 jit_solution(5483098562843282781)
XLA Ops:
  0.0 0.9 %shard_map.64.after_ref.refs_0_ = bf16[32,1920]{1,0:T(8,128)(2,1)S(1)} custom-call(bf16[2,16,3584]{2,1,0:T(8,128)(2,1)} %tokens_ref.1, s32[2,8,16]{2,1,0:T(8,128)} %bitcast.3, f32[2,8,16]{2,1,0:T(8,128)} %bitcast.4), custom_call_target="tpu_custom_call" | custom-call | tf_op jit(solution)/shard_map/pallas_call | solution.py:79
  0.9 4.0 %collective-permute-start.3 = (bf16[32,1920]{1,0:T(8,128)(2,1)S(1)}, bf16[32,1920]{1,0:T(8,128)(2,1)S(1)}, u32[]{:S(2)}, u32[]{:S(2)}) collective-permute-start(bf16[32,1920]{1,0:T(8,128)(2,1)S(1)} %shard_map.64.after_ref.refs_0_), channel_id=1, source_target_pairs={{0,6},{2,4},{4,2},{6,0},{8,14},{10,12},{12,10},{14,8},{1,7},{3,5},... | collective-permute-start | bytes 368648 | tf_op jit(solution)/shard_map/ppermute | solution.py:406
  4.9 0.5 collective-permute-start.2
  5.5 2.6 %collective-permute-start.1 = (bf16[32,1920]{1,0:T(8,128)(2,1)S(1)}, bf16[32,1920]{1,0:T(8,128)(2,1)S(1)}, u32[]{:S(2)}, u32[]{:S(2)}) collective-permute-start(bf16[32,1920]{1,0:T(8,128)(2,1)S(1)} %shard_map.64.after_ref.refs_0_), channel_id=1, source_target_pairs={{0,8},{2,10},{4,12},{6,14},{8,0},{10,2},{12,4},{14,6},{1,9},{3,11}... | collective-permute-start | bytes 368648 | tf_op jit(solution)/shard_map/ppermute | solution.py:406
  8.1 0.4 collective-permute-start
  8.5 5.3 %shard_map.65 = (bf16[4,512,3584]{2,1,0:T(8,128)(2,1)S(1)}, f32[8,128]{1,0:T(8,128)S(1)}) custom-call(bf16[8,512,3584]{2,1,0:T(8,128)(2,1)} %down_ref_hbm.1, bf16[32,1920]{1,0:T(8,128)(2,1)S(1)} %shard_map.64.after_ref.refs_0_), custom_call_target="tpu_custom_call" | custom-call | bytes 14680064 | tf_op jit(solution)/shard_map/pallas_call | solution.py:107
  13.8 0.0 collective-permute-done.3.refs_4_
  13.8 0.0 collective-permute-done.2.refs_3_
  13.8 0.0 collective-permute-done.1.refs_2_.after_ref
  13.8 0.0 collective-permute-done.refs_1_
  13.9 0.1 collective-permute-start.7
  14.0 2.6 %collective-permute-start.6 = (bf16[32,1920]{1,0:T(8,128)(2,1)S(1)}, bf16[32,1920]{1,0:T(8,128)(2,1)S(1)}, u32[]{:S(2)}, u32[]{:S(2)}) collective-permute-start(bf16[32,1920]{1,0:T(8,128)(2,1)S(1)} %collective-permute-done.1.refs_2_.after_ref), channel_id=1, source_target_pairs={{0,6},{2,4},{4,2},{6,0},{8,14},{10,12},{12,10},{14,8},{1,7},{3,5},... | collective-permute-start | bytes 368648 | tf_op jit(solution)/shard_map/ppermute | solution.py:406
  16.5 0.5 collective-permute-start.5
  17.1 0.4 collective-permute-start.4
  17.5 3.2 %shard_map.67 = (bf16[2,512,3584]{2,1,0:T(8,128)(2,1)S(1)}, f32[8,128]{1,0:T(8,128)S(1)}) custom-call(bf16[8,512,3584]{2,1,0:T(8,128)(2,1)} %down_ref_hbm.1, bf16[32,1920]{1,0:T(8,128)(2,1)S(1)} %collective-permute-done.1.refs_2_.after_ref), custom_call_target="tpu_custom_call" | custom-call | bytes 7340032 | tf_op jit(solution)/shard_map/pallas_call | solution.py:107
  20.7 0.0 collective-permute-done.6.refs_2_
  20.7 2.5 %collective-permute-done.5.refs_1_ = bf16[32,1920]{1,0:T(8,128)(2,1)S(1)} collective-permute-done((bf16[32,1920]{1,0:T(8,128)(2,1)S(1)}, bf16[32,1920]{1,0:T(8,128)(2,1)S(1)}, u32[]{:S(2)}, u32[]{:S(2)}) %collective-permute-start.5) | collective-permute-done | bytes 122912 | tf_op jit(solution)/shard_map/ppermute | solution.py:406
  23.2 0.4 collective-permute-done.4.refs_0_
  23.7 0.1 collective-permute-start.8
  23.7 0.1 pad_maximum_fusion.mine_ref
  23.8 1.6 %collective-permute-done.8 = bf16[96,1920]{1,0:T(8,128)(2,1)S(1)} collective-permute-done((bf16[96,1920]{1,0:T(8,128)(2,1)S(1)}, bf16[96,1920]{1,0:T(8,128)(2,1)S(1)}, u32[]{:S(2)}, u32[]{:S(2)}) %collective-permute-start.8) | collective-permute-done | bytes 368672 | tf_op jit(solution)/shard_map/ppermute | solution.py:403
  25.4 0.0 collective-permute-done.7
  25.4 0.1 pad_maximum_fusion.1.theirs_ref
  25.5 22.9 %shard_map.69 = (bf16[128,1792]{1,0:T(8,128)(2,1)S(1)}, bf16[128,1792]{1,0:T(8,128)(2,1)S(1)}, bf16[128,1792]{1,0:T(8,128)(2,1)S(1)}, bf16[128,1792]{1,0:T(8,128)(2,1)S(1)}) custom-call(bf16[256,1920]{1,0:T(8,128)(2,1)S(1)} %pad_maximum_fusion.mine_ref, bf16[256,1920]{1,0:T(8,128)(2,1)S(1)} %pad_maximum_fusion.1.theirs_ref, bf16[8,3584,512]{2,1,0:T(8,128)(2,1)} %gate_ref.1, ...), custom_call_target="tpu_custom_call" | custom-call | flops 2818572288 | bytes 58720256 | tf_op jit(solution)/shard_map/pallas_call | solution.py:353
  48.4 0.2 collective-permute-start.10
  48.6 0.4 collective-permute-start.9
  49.0 1.3 %collective-permute-done.10.refs_1_ = bf16[128,1792]{1,0:T(8,128)(2,1)S(1)} collective-permute-done((bf16[128,1792]{1,0:T(8,128)(2,1)S(1)}, bf16[128,1792]{1,0:T(8,128)(2,1)S(1)}, u32[]{:S(2)}, u32[]{:S(2)}) %collective-permute-start.10) | collective-permute-done | bytes 458784 | tf_op jit(solution)/shard_map/ppermute | solution.py:403
  50.3 1.5 %collective-permute-start.11 = (bf16[32,1792]{1,0:T(8,128)(2,1)S(1)}, bf16[32,1792]{1,0:T(8,128)(2,1)S(1)}, u32[]{:S(2)}, u32[]{:S(2)}) collective-permute-start(bf16[32,1792]{1,0:T(8,128)(2,1)S(1)} %shard_map.70), channel_id=1, source_target_pairs={{0,2},{2,0},{4,6},{6,4},{8,10},{10,8},{12,14},{14,12},{1,3},{3,1},... | collective-permute-start | bytes 344072 | tf_op jit(solution)/shard_map/ppermute | solution.py:406
  51.8 1.4 %collective-permute-start.12 = (bf16[32,1792]{1,0:T(8,128)(2,1)S(1)}, bf16[32,1792]{1,0:T(8,128)(2,1)S(1)}, u32[]{:S(2)}, u32[]{:S(2)}) collective-permute-start(bf16[32,1792]{1,0:T(8,128)(2,1)S(1)} %shard_map.71), channel_id=1, source_target_pairs={{0,6},{2,4},{4,2},{6,0},{8,14},{10,12},{12,10},{14,8},{1,7},{3,5},... | collective-permute-start | bytes 344072 | tf_op jit(solution)/shard_map/ppermute | solution.py:406
  53.3 0.8 %collective-permute-start.13 = (bf16[32,1792]{1,0:T(8,128)(2,1)S(1)}, bf16[32,1792]{1,0:T(8,128)(2,1)S(1)}, u32[]{:S(2)}, u32[]{:S(2)}) collective-permute-start(bf16[32,1792]{1,0:T(8,128)(2,1)S(1)} %shard_map.72), channel_id=1, source_target_pairs={{0,4},{2,6},{4,0},{6,2},{8,12},{10,14},{12,8},{14,10},{1,5},{3,7},... | collective-permute-start | bytes 344072 | tf_op jit(solution)/shard_map/ppermute | solution.py:406
  54.1 0.0 collective-permute-done.9.refs_1_.refs_2_
  54.1 1.5 %collective-permute-start.16 = (bf16[32,1792]{1,0:T(8,128)(2,1)S(1)}, bf16[32,1792]{1,0:T(8,128)(2,1)S(1)}, u32[]{:S(2)}, u32[]{:S(2)}) collective-permute-start(bf16[32,1792]{1,0:T(8,128)(2,1)S(1)} %shard_map.75), channel_id=1, source_target_pairs={{0,2},{2,0},{4,6},{6,4},{8,10},{10,8},{12,14},{14,12},{1,3},{3,1},... | collective-permute-start | bytes 344072 | tf_op jit(solution)/shard_map/ppermute | solution.py:406
  55.6 0.6 collective-permute-start.17
  56.3 1.5 %collective-permute-done.11.refs_2_ = bf16[32,1792]{1,0:T(8,128)(2,1)S(1)} collective-permute-done((bf16[32,1792]{1,0:T(8,128)(2,1)S(1)}, bf16[32,1792]{1,0:T(8,128)(2,1)S(1)}, u32[]{:S(2)}, u32[]{:S(2)}) %collective-permute-start.11) | collective-permute-done | bytes 114720 | tf_op jit(solution)/shard_map/ppermute | solution.py:406
  57.8 1.5 %collective-permute-start.15 = (bf16[32,1792]{1,0:T(8,128)(2,1)S(1)}, bf16[32,1792]{1,0:T(8,128)(2,1)S(1)}, u32[]{:S(2)}, u32[]{:S(2)}) collective-permute-start(bf16[32,1792]{1,0:T(8,128)(2,1)S(1)} %shard_map.74), channel_id=1, source_target_pairs={{0,6},{2,4},{4,2},{6,0},{8,14},{10,12},{12,10},{14,8},{1,7},{3,5},... | collective-permute-start | bytes 344072 | tf_op jit(solution)/shard_map/ppermute | solution.py:406
  59.3 0.0 collective-permute-done.12.refs_3_
  59.3 1.1 %collective-permute-done.13.refs_4_ = bf16[32,1792]{1,0:T(8,128)(2,1)S(1)} collective-permute-done((bf16[32,1792]{1,0:T(8,128)(2,1)S(1)}, bf16[32,1792]{1,0:T(8,128)(2,1)S(1)}, u32[]{:S(2)}, u32[]{:S(2)}) %collective-permute-start.13) | collective-permute-done | bytes 114720 | tf_op jit(solution)/shard_map/ppermute | solution.py:406
  60.4 0.1 shard_map.73
  60.5 2.2 %collective-permute-start.14 = (bf16[32,1792]{1,0:T(8,128)(2,1)S(1)}, bf16[32,1792]{1,0:T(8,128)(2,1)S(1)}, u32[]{:S(2)}, u32[]{:S(2)}) collective-permute-start(bf16[32,1792]{1,0:T(8,128)(2,1)S(1)} %shard_map.73), channel_id=1, source_target_pairs={{0,8},{2,10},{4,12},{6,14},{8,0},{10,2},{12,4},{14,6},{1,9},{3,11}... | collective-permute-start | bytes 344072 | tf_op jit(solution)/shard_map/ppermute | solution.py:406
  62.7 0.0 collective-permute-done.16
  62.7 1.4 %collective-permute-done.17 = bf16[32,1792]{1,0:T(8,128)(2,1)S(1)} collective-permute-done((bf16[32,1792]{1,0:T(8,128)(2,1)S(1)}, bf16[32,1792]{1,0:T(8,128)(2,1)S(1)}, u32[]{:S(2)}, u32[]{:S(2)}) %collective-permute-start.17) | collective-permute-done | bytes 114720 | tf_op jit(solution)/shard_map/ppermute | solution.py:406
  64.1 2.7 %collective-permute-done.15 = bf16[32,1792]{1,0:T(8,128)(2,1)S(1)} collective-permute-done((bf16[32,1792]{1,0:T(8,128)(2,1)S(1)}, bf16[32,1792]{1,0:T(8,128)(2,1)S(1)}, u32[]{:S(2)}, u32[]{:S(2)}) %collective-permute-start.15) | collective-permute-done | bytes 114720 | tf_op jit(solution)/shard_map/ppermute | solution.py:406
  66.8 1.6 %collective-permute-done.14 = bf16[32,1792]{1,0:T(8,128)(2,1)S(1)} collective-permute-done((bf16[32,1792]{1,0:T(8,128)(2,1)S(1)}, bf16[32,1792]{1,0:T(8,128)(2,1)S(1)}, u32[]{:S(2)}, u32[]{:S(2)}) %collective-permute-start.14) | collective-permute-done | bytes 114720 | tf_op jit(solution)/shard_map/ppermute | solution.py:406
  68.5 0.7 %add_convert_fusion = bf16[32,1792]{1,0:T(8,128)(2,1)} fusion(bf16[32,1792]{1,0:T(8,128)(2,1)S(1)} %collective-permute-done.17, bf16[32,1792]{1,0:T(8,128)(2,1)S(1)} %collective-permute-done.16, bf16[32,1792]{1,0:T(8,128)(2,1)S(1)} %collective-permute-done.15, bf16[32,1792]{1,0:T(8,128)(2,1)S(1)} %collective-permute-done.14, ...), kind=kLoop, calls=%fused_computation.2 | loop fusion | flops 688128 | bytes 802816 | tf_op jit(solution)/shard_map/convert_element_type | solution.py:458
  (8 shorter events, 0.3 us)
Async XLA Ops:
  0.9 12.9 %collective-permute-start.3 = (bf16[32,1920]{1,0:T(8,128)(2,1)S(1)}, bf16[32,1920]{1,0:T(8,128)(2,1)S(1)}, u32[]{:S(2)}, u32[]{:S(2)}) collective-permute-start(bf16[32,1920]{1,0:T(8,128)(2,1)S(1)} %shard_map.64.after_ref.refs_0_), channel_id=1, source_target_pairs={{0,6},{2,4},{4,2},{6,0},{8,14},{10,12},{12,10},{14,8},{1,7},{3,5},... | collective-permute-start | bytes 368648 | tf_op jit(solution)/shard_map/ppermute | solution.py:406
  4.9 8.9 %collective-permute-start.2 = (bf16[32,1920]{1,0:T(8,128)(2,1)S(1)}, bf16[32,1920]{1,0:T(8,128)(2,1)S(1)}, u32[]{:S(2)}, u32[]{:S(2)}) collective-permute-start(bf16[32,1920]{1,0:T(8,128)(2,1)S(1)} %shard_map.64.after_ref.refs_0_), channel_id=1, source_target_pairs={{0,2},{2,0},{4,6},{6,4},{8,10},{10,8},{12,14},{14,12},{1,3},{3,1},... | collective-permute-start | bytes 368648 | tf_op jit(solution)/shard_map/ppermute | solution.py:406
  5.5 8.4 %collective-permute-start.1 = (bf16[32,1920]{1,0:T(8,128)(2,1)S(1)}, bf16[32,1920]{1,0:T(8,128)(2,1)S(1)}, u32[]{:S(2)}, u32[]{:S(2)}) collective-permute-start(bf16[32,1920]{1,0:T(8,128)(2,1)S(1)} %shard_map.64.after_ref.refs_0_), channel_id=1, source_target_pairs={{0,8},{2,10},{4,12},{6,14},{8,0},{10,2},{12,4},{14,6},{1,9},{3,11}... | collective-permute-start | bytes 368648 | tf_op jit(solution)/shard_map/ppermute | solution.py:406
  8.1 5.8 %collective-permute-start = (bf16[32,1920]{1,0:T(8,128)(2,1)S(1)}, bf16[32,1920]{1,0:T(8,128)(2,1)S(1)}, u32[]{:S(2)}, u32[]{:S(2)}) collective-permute-start(bf16[32,1920]{1,0:T(8,128)(2,1)S(1)} %shard_map.64.after_ref.refs_0_), channel_id=1, source_target_pairs={{0,4},{2,6},{4,0},{6,2},{8,12},{10,14},{12,8},{14,10},{1,5},{3,7},... | collective-permute-start | bytes 368648 | tf_op jit(solution)/shard_map/ppermute | solution.py:406
  13.9 11.5 %collective-permute-start.7 = (bf16[160,1920]{1,0:T(8,128)(2,1)S(1)}, bf16[160,1920]{1,0:T(8,128)(2,1)S(1)}, u32[]{:S(2)}, u32[]{:S(2)}) collective-permute-start(bf16[160,1920]{1,0:T(8,128)(2,1)S(1)} %shard_map.66), channel_id=1, source_target_pairs={{0,1},{1,0},{2,3},{3,2},{4,5},{5,4},{6,7},{7,6},{8,9},{9,8},{10,11... | collective-permute-start | bytes 1843208 | tf_op jit(solution)/shard_map/ppermute | solution.py:403
  14.0 6.7 %collective-permute-start.6 = (bf16[32,1920]{1,0:T(8,128)(2,1)S(1)}, bf16[32,1920]{1,0:T(8,128)(2,1)S(1)}, u32[]{:S(2)}, u32[]{:S(2)}) collective-permute-start(bf16[32,1920]{1,0:T(8,128)(2,1)S(1)} %collective-permute-done.1.refs_2_.after_ref), channel_id=1, source_target_pairs={{0,6},{2,4},{4,2},{6,0},{8,14},{10,12},{12,10},{14,8},{1,7},{3,5},... | collective-permute-start | bytes 368648 | tf_op jit(solution)/shard_map/ppermute | solution.py:406
  16.5 6.7 %collective-permute-start.5 = (bf16[32,1920]{1,0:T(8,128)(2,1)S(1)}, bf16[32,1920]{1,0:T(8,128)(2,1)S(1)}, u32[]{:S(2)}, u32[]{:S(2)}) collective-permute-start(bf16[32,1920]{1,0:T(8,128)(2,1)S(1)} %collective-permute-done.1.refs_2_.after_ref), channel_id=1, source_target_pairs={{0,2},{2,0},{4,6},{6,4},{8,10},{10,8},{12,14},{14,12},{1,3},{3,1},... | collective-permute-start | bytes 368648 | tf_op jit(solution)/shard_map/ppermute | solution.py:406
  17.1 6.5 %collective-permute-start.4 = (bf16[32,1920]{1,0:T(8,128)(2,1)S(1)}, bf16[32,1920]{1,0:T(8,128)(2,1)S(1)}, u32[]{:S(2)}, u32[]{:S(2)}) collective-permute-start(bf16[32,1920]{1,0:T(8,128)(2,1)S(1)} %collective-permute-done.1.refs_2_.after_ref), channel_id=1, source_target_pairs={{0,4},{2,6},{4,0},{6,2},{8,12},{10,14},{12,8},{14,10},{1,5},{3,7},... | collective-permute-start | bytes 368648 | tf_op jit(solution)/shard_map/ppermute | solution.py:406
  23.7 1.8 %collective-permute-start.8 = (bf16[96,1920]{1,0:T(8,128)(2,1)S(1)}, bf16[96,1920]{1,0:T(8,128)(2,1)S(1)}, u32[]{:S(2)}, u32[]{:S(2)}) collective-permute-start(bf16[96,1920]{1,0:T(8,128)(2,1)S(1)} %shard_map.68), channel_id=1, source_target_pairs={{0,1},{1,0},{2,3},{3,2},{4,5},{5,4},{6,7},{7,6},{8,9},{9,8},{10,11... | collective-permute-start | bytes 1105928 | tf_op jit(solution)/shard_map/ppermute | solution.py:403
  48.4 1.9 %collective-permute-start.10 = (bf16[128,1792]{1,0:T(8,128)(2,1)S(1)}, bf16[128,1792]{1,0:T(8,128)(2,1)S(1)}, u32[]{:S(2)}, u32[]{:S(2)}) collective-permute-start(bf16[128,1792]{1,0:T(8,128)(2,1)S(1)} %get-tuple-element.20), channel_id=1, source_target_pairs={{0,1},{1,0},{2,3},{3,2},{4,5},{5,4},{6,7},{7,6},{8,9},{9,8},{10,11... | collective-permute-start | bytes 1376264 | tf_op jit(solution)/shard_map/ppermute | solution.py:403
  48.6 5.5 %collective-permute-start.9 = (bf16[128,1792]{1,0:T(8,128)(2,1)S(1)}, bf16[128,1792]{1,0:T(8,128)(2,1)S(1)}, u32[]{:S(2)}, u32[]{:S(2)}) collective-permute-start(bf16[128,1792]{1,0:T(8,128)(2,1)S(1)} %get-tuple-element.18), channel_id=1, source_target_pairs={{0,1},{1,0},{2,3},{3,2},{4,5},{5,4},{6,7},{7,6},{8,9},{9,8},{10,11... | collective-permute-start | bytes 1376264 | tf_op jit(solution)/shard_map/ppermute | solution.py:403
  50.3 7.5 %collective-permute-start.11 = (bf16[32,1792]{1,0:T(8,128)(2,1)S(1)}, bf16[32,1792]{1,0:T(8,128)(2,1)S(1)}, u32[]{:S(2)}, u32[]{:S(2)}) collective-permute-start(bf16[32,1792]{1,0:T(8,128)(2,1)S(1)} %shard_map.70), channel_id=1, source_target_pairs={{0,2},{2,0},{4,6},{6,4},{8,10},{10,8},{12,14},{14,12},{1,3},{3,1},... | collective-permute-start | bytes 344072 | tf_op jit(solution)/shard_map/ppermute | solution.py:406
  51.8 7.5 %collective-permute-start.12 = (bf16[32,1792]{1,0:T(8,128)(2,1)S(1)}, bf16[32,1792]{1,0:T(8,128)(2,1)S(1)}, u32[]{:S(2)}, u32[]{:S(2)}) collective-permute-start(bf16[32,1792]{1,0:T(8,128)(2,1)S(1)} %shard_map.71), channel_id=1, source_target_pairs={{0,6},{2,4},{4,2},{6,0},{8,14},{10,12},{12,10},{14,8},{1,7},{3,5},... | collective-permute-start | bytes 344072 | tf_op jit(solution)/shard_map/ppermute | solution.py:406
  53.3 7.2 %collective-permute-start.13 = (bf16[32,1792]{1,0:T(8,128)(2,1)S(1)}, bf16[32,1792]{1,0:T(8,128)(2,1)S(1)}, u32[]{:S(2)}, u32[]{:S(2)}) collective-permute-start(bf16[32,1792]{1,0:T(8,128)(2,1)S(1)} %shard_map.72), channel_id=1, source_target_pairs={{0,4},{2,6},{4,0},{6,2},{8,12},{10,14},{12,8},{14,10},{1,5},{3,7},... | collective-permute-start | bytes 344072 | tf_op jit(solution)/shard_map/ppermute | solution.py:406
  54.1 8.6 %collective-permute-start.16 = (bf16[32,1792]{1,0:T(8,128)(2,1)S(1)}, bf16[32,1792]{1,0:T(8,128)(2,1)S(1)}, u32[]{:S(2)}, u32[]{:S(2)}) collective-permute-start(bf16[32,1792]{1,0:T(8,128)(2,1)S(1)} %shard_map.75), channel_id=1, source_target_pairs={{0,2},{2,0},{4,6},{6,4},{8,10},{10,8},{12,14},{14,12},{1,3},{3,1},... | collective-permute-start | bytes 344072 | tf_op jit(solution)/shard_map/ppermute | solution.py:406
  55.6 8.5 %collective-permute-start.17 = (bf16[32,1792]{1,0:T(8,128)(2,1)S(1)}, bf16[32,1792]{1,0:T(8,128)(2,1)S(1)}, u32[]{:S(2)}, u32[]{:S(2)}) collective-permute-start(bf16[32,1792]{1,0:T(8,128)(2,1)S(1)} %shard_map.76), channel_id=1, source_target_pairs={{0,4},{2,6},{4,0},{6,2},{8,12},{10,14},{12,8},{14,10},{1,5},{3,7},... | collective-permute-start | bytes 344072 | tf_op jit(solution)/shard_map/ppermute | solution.py:406
  57.8 9.0 %collective-permute-start.15 = (bf16[32,1792]{1,0:T(8,128)(2,1)S(1)}, bf16[32,1792]{1,0:T(8,128)(2,1)S(1)}, u32[]{:S(2)}, u32[]{:S(2)}) collective-permute-start(bf16[32,1792]{1,0:T(8,128)(2,1)S(1)} %shard_map.74), channel_id=1, source_target_pairs={{0,6},{2,4},{4,2},{6,0},{8,14},{10,12},{12,10},{14,8},{1,7},{3,5},... | collective-permute-start | bytes 344072 | tf_op jit(solution)/shard_map/ppermute | solution.py:406
  60.5 7.9 %collective-permute-start.14 = (bf16[32,1792]{1,0:T(8,128)(2,1)S(1)}, bf16[32,1792]{1,0:T(8,128)(2,1)S(1)}, u32[]{:S(2)}, u32[]{:S(2)}) collective-permute-start(bf16[32,1792]{1,0:T(8,128)(2,1)S(1)} %shard_map.73), channel_id=1, source_target_pairs={{0,8},{2,10},{4,12},{6,14},{8,0},{10,2},{12,4},{14,6},{1,9},{3,11}... | collective-permute-start | bytes 344072 | tf_op jit(solution)/shard_map/ppermute | solution.py:406

commit v4 on v3

--- a/solution.py
+++ b/solution.py
@@ -8,8 +8,9 @@
 from jax.sharding import PartitionSpec as P
 
 META = 128
-RING = 6
-FETCHED = (4, 6)
+LOOK = 4
+RING = 5
+FETCHED = (4, 7)
 MIB = 1024 * 1024
 
 
@@ -201,7 +202,7 @@
             source.at[lax.div(block, 2)], ring.at[slot], sems.at[slot]
         )
 
-    for block in range(min(RING, blocks)):
+    for block in range(2):
         refill(block, block % 2).start()
 
     def gather(selector, target):
@@ -247,6 +248,9 @@
     selector = jnp.concatenate([pick(e, cap_cold) for e in range(experts_here)], axis=0)
     gather(selector.astype(jnp.bfloat16), gathered.at[:cold_rows])
 
+    for block in range(2, min(LOOK, blocks)):
+        refill(block, block % 2).start()
+
     def stream(expert):
         place = expert - FETCHED[1]
         return pltpu.make_async_copy(
@@ -256,12 +260,12 @@
     def project(expert, which, row_data):
         block = 2 * expert + which
         refill(block, which).wait()
+
+        @pl.when(block + LOOK < blocks)
+        def _():
+            refill(block + LOOK, (which + LOOK) % 2).start()
+
         value = jnp.dot(row_data, ring[slot_of(block)], preferred_element_type=jnp.float32)
-
-        @pl.when(block + RING < blocks)
-        def _():
-            refill(block + RING, which).start()
-
         return value
 
     def visit(expert, down_ref, base, streamed):
@@ -375,7 +379,7 @@
             pltpu.VMEM((experts_here - FETCHED[1], hidden, features), jnp.bfloat16),
             pltpu.SemaphoreType.DMA((experts_here - FETCHED[1],)),
         ],
-        compiler_params=pltpu.CompilerParams(vmem_limit_bytes=38 * MIB),
+        compiler_params=pltpu.CompilerParams(vmem_limit_bytes=33 * MIB),
         cost_estimate=pl.CostEstimate(
             flops=6 * rows * features * hidden,
             bytes_accessed=4 * experts_here * features * hidden,

time: 69.4 us -> 69.2 us (level)
  waiting for transfers between devices: 14.2 us -> 12.6 us
  Pallas kernels: 32.6 us -> 33.3 us
    ppermute x14, waiting for transfers between devices: 11.3 us -> 9.71 us  [trade(): return lax.ppermute(value, 'expert', [(i, i ^ k) for i in range(devices)])]
    pallas_call x2, Pallas kernels: 8.45 us -> 9.51 us  [fetch_part(): pl.pallas_call(kernel, in_specs=[HBM_SPEC, HBM_SPEC], out_specs=(VMEM_SPE...]
  transfers between devices with their start and end apart: 18 -> 18, of which waited for: 9 -> 9; matrix products, arithmetic and copies ran while one was open for 0% -> 0% of each run, Pallas kernels for 13% -> 14%
where the time goes in v4:
time: 69.2 us; the launch traced here: 68.9 us
  Pallas kernels  33.3 us (48%)
  starting transfers between devices  22 us (32%)
  waiting for transfers between devices  12.6 us (18%)
  other arithmetic  0.89 us (1%)
    pallas_call x1, Pallas kernels, run_experts(): pl.pallas_call(functools.partial(expert_kernel, topk, cap_cold, cap_hot),...  22.6 us
    ppermute x14, starting transfers between devices, trade(): return lax.ppermute(value, 'expert', [(i, i ^ k) for i in range(devices)])  21.3 us
    ppermute x14, waiting for transfers between devices, trade(): return lax.ppermute(value, 'expert', [(i, i ^ k) for i in range(devices)])  9.71 us
    pallas_call x2, Pallas kernels, fetch_part(): pl.pallas_call(kernel, in_specs=[HBM_SPEC, HBM_SPEC], out_specs=(VMEM_SPE...  9.51 us
    ppermute x4, waiting for transfers between devices, across(): return lax.ppermute(value, 'tensor', [(0, 1), (1, 0)])  2.9 us
  transfers between devices with their start and end apart: 18, of which 9 were waited for; matrix products, arithmetic and copies ran while one was open for 0% of the time, Pallas kernels for 14%

profile of v4, /device:TPU:0, one launch (start us, length us, event | category | flops | bytes accessed | tf_op | source)
XLA Modules:
  0.0 68.9 jit_solution(4291142813623743651)
XLA Ops:
  0.0 0.9 %shard_map.64.after_ref.refs_0_ = bf16[32,1920]{1,0:T(8,128)(2,1)S(1)} custom-call(bf16[2,16,3584]{2,1,0:T(8,128)(2,1)} %tokens_ref.1, s32[2,8,16]{2,1,0:T(8,128)} %bitcast.3, f32[2,8,16]{2,1,0:T(8,128)} %bitcast.4), custom_call_target="tpu_custom_call" | custom-call | tf_op jit(solution)/shard_map/pallas_call | solution.py:80
  0.9 4.0 %collective-permute-start.3 = (bf16[32,1920]{1,0:T(8,128)(2,1)S(1)}, bf16[32,1920]{1,0:T(8,128)(2,1)S(1)}, u32[]{:S(2)}, u32[]{:S(2)}) collective-permute-start(bf16[32,1920]{1,0:T(8,128)(2,1)S(1)} %shard_map.64.after_ref.refs_0_), channel_id=1, source_target_pairs={{0,6},{2,4},{4,2},{6,0},{8,14},{10,12},{12,10},{14,8},{1,7},{3,5},... | collective-permute-start | bytes 368648 | tf_op jit(solution)/shard_map/ppermute | solution.py:410
  4.9 0.5 collective-permute-start.2
  5.5 2.6 %collective-permute-start.1 = (bf16[32,1920]{1,0:T(8,128)(2,1)S(1)}, bf16[32,1920]{1,0:T(8,128)(2,1)S(1)}, u32[]{:S(2)}, u32[]{:S(2)}) collective-permute-start(bf16[32,1920]{1,0:T(8,128)(2,1)S(1)} %shard_map.64.after_ref.refs_0_), channel_id=1, source_target_pairs={{0,8},{2,10},{4,12},{6,14},{8,0},{10,2},{12,4},{14,6},{1,9},{3,11}... | collective-permute-start | bytes 368648 | tf_op jit(solution)/shard_map/ppermute | solution.py:410
  8.1 0.4 collective-permute-start
  8.5 5.3 %shard_map.65 = (bf16[4,512,3584]{2,1,0:T(8,128)(2,1)S(1)}, f32[8,128]{1,0:T(8,128)S(1)}) custom-call(bf16[8,512,3584]{2,1,0:T(8,128)(2,1)} %down_ref_hbm.1, bf16[32,1920]{1,0:T(8,128)(2,1)S(1)} %shard_map.64.after_ref.refs_0_), custom_call_target="tpu_custom_call" | custom-call | bytes 14680064 | tf_op jit(solution)/shard_map/pallas_call | solution.py:108
  13.8 0.0 collective-permute-done.3.refs_4_
  13.8 0.0 collective-permute-done.2.refs_3_
  13.8 0.0 collective-permute-done.1.refs_2_.after_ref
  13.8 0.0 collective-permute-done.refs_1_
  13.9 0.1 collective-permute-start.7
  14.0 2.6 %collective-permute-start.6 = (bf16[32,1920]{1,0:T(8,128)(2,1)S(1)}, bf16[32,1920]{1,0:T(8,128)(2,1)S(1)}, u32[]{:S(2)}, u32[]{:S(2)}) collective-permute-start(bf16[32,1920]{1,0:T(8,128)(2,1)S(1)} %collective-permute-done.1.refs_2_.after_ref), channel_id=1, source_target_pairs={{0,6},{2,4},{4,2},{6,0},{8,14},{10,12},{12,10},{14,8},{1,7},{3,5},... | collective-permute-start | bytes 368648 | tf_op jit(solution)/shard_map/ppermute | solution.py:410
  16.5 0.5 collective-permute-start.5
  17.1 0.4 collective-permute-start.4
  17.5 4.2 %shard_map.67 = (bf16[3,512,3584]{2,1,0:T(8,128)(2,1)S(1)}, f32[8,128]{1,0:T(8,128)S(1)}) custom-call(bf16[8,512,3584]{2,1,0:T(8,128)(2,1)} %down_ref_hbm.1, bf16[32,1920]{1,0:T(8,128)(2,1)S(1)} %collective-permute-done.1.refs_2_.after_ref), custom_call_target="tpu_custom_call" | custom-call | bytes 11010048 | tf_op jit(solution)/shard_map/pallas_call | solution.py:108
  21.8 0.0 collective-permute-done.6.refs_2_
  21.8 1.5 %collective-permute-done.5.refs_1_ = bf16[32,1920]{1,0:T(8,128)(2,1)S(1)} collective-permute-done((bf16[32,1920]{1,0:T(8,128)(2,1)S(1)}, bf16[32,1920]{1,0:T(8,128)(2,1)S(1)}, u32[]{:S(2)}, u32[]{:S(2)}) %collective-permute-start.5) | collective-permute-done | bytes 122912 | tf_op jit(solution)/shard_map/ppermute | solution.py:410
  23.2 0.4 collective-permute-done.4.refs_0_
  23.7 0.1 collective-permute-start.8
  23.7 0.1 pad_maximum_fusion.mine_ref
  23.8 1.6 %collective-permute-done.8 = bf16[96,1920]{1,0:T(8,128)(2,1)S(1)} collective-permute-done((bf16[96,1920]{1,0:T(8,128)(2,1)S(1)}, bf16[96,1920]{1,0:T(8,128)(2,1)S(1)}, u32[]{:S(2)}, u32[]{:S(2)}) %collective-permute-start.8) | collective-permute-done | bytes 368672 | tf_op jit(solution)/shard_map/ppermute | solution.py:407
  25.4 0.0 collective-permute-done.7
  25.4 0.1 pad_maximum_fusion.1.theirs_ref
  25.5 22.6 %shard_map.69 = (bf16[128,1792]{1,0:T(8,128)(2,1)S(1)}, bf16[128,1792]{1,0:T(8,128)(2,1)S(1)}, bf16[128,1792]{1,0:T(8,128)(2,1)S(1)}, bf16[128,1792]{1,0:T(8,128)(2,1)S(1)}) custom-call(bf16[256,1920]{1,0:T(8,128)(2,1)S(1)} %pad_maximum_fusion.mine_ref, bf16[256,1920]{1,0:T(8,128)(2,1)S(1)} %pad_maximum_fusion.1.theirs_ref, bf16[8,3584,512]{2,1,0:T(8,128)(2,1)} %gate_ref.1, ...), custom_call_target="tpu_custom_call" | custom-call | flops 2818572288 | bytes 58720256 | tf_op jit(solution)/shard_map/pallas_call | solution.py:357
  48.1 0.2 collective-permute-start.10
  48.3 0.4 collective-permute-start.9
  48.6 1.3 %collective-permute-done.10.refs_1_ = bf16[128,1792]{1,0:T(8,128)(2,1)S(1)} collective-permute-done((bf16[128,1792]{1,0:T(8,128)(2,1)S(1)}, bf16[128,1792]{1,0:T(8,128)(2,1)S(1)}, u32[]{:S(2)}, u32[]{:S(2)}) %collective-permute-start.10) | collective-permute-done | bytes 458784 | tf_op jit(solution)/shard_map/ppermute | solution.py:407
  50.0 1.5 %collective-permute-start.11 = (bf16[32,1792]{1,0:T(8,128)(2,1)S(1)}, bf16[32,1792]{1,0:T(8,128)(2,1)S(1)}, u32[]{:S(2)}, u32[]{:S(2)}) collective-permute-start(bf16[32,1792]{1,0:T(8,128)(2,1)S(1)} %shard_map.70), channel_id=1, source_target_pairs={{0,2},{2,0},{4,6},{6,4},{8,10},{10,8},{12,14},{14,12},{1,3},{3,1},... | collective-permute-start | bytes 344072 | tf_op jit(solution)/shard_map/ppermute | solution.py:410
  51.5 1.4 %collective-permute-start.12 = (bf16[32,1792]{1,0:T(8,128)(2,1)S(1)}, bf16[32,1792]{1,0:T(8,128)(2,1)S(1)}, u32[]{:S(2)}, u32[]{:S(2)}) collective-permute-start(bf16[32,1792]{1,0:T(8,128)(2,1)S(1)} %shard_map.71), channel_id=1, source_target_pairs={{0,6},{2,4},{4,2},{6,0},{8,14},{10,12},{12,10},{14,8},{1,7},{3,5},... | collective-permute-start | bytes 344072 | tf_op jit(solution)/shard_map/ppermute | solution.py:410
  52.9 0.8 %collective-permute-start.13 = (bf16[32,1792]{1,0:T(8,128)(2,1)S(1)}, bf16[32,1792]{1,0:T(8,128)(2,1)S(1)}, u32[]{:S(2)}, u32[]{:S(2)}) collective-permute-start(bf16[32,1792]{1,0:T(8,128)(2,1)S(1)} %shard_map.72), channel_id=1, source_target_pairs={{0,4},{2,6},{4,0},{6,2},{8,12},{10,14},{12,8},{14,10},{1,5},{3,7},... | collective-permute-start | bytes 344072 | tf_op jit(solution)/shard_map/ppermute | solution.py:410
  53.7 0.0 collective-permute-done.9.refs_1_.refs_2_
  53.8 1.5 %collective-permute-start.16 = (bf16[32,1792]{1,0:T(8,128)(2,1)S(1)}, bf16[32,1792]{1,0:T(8,128)(2,1)S(1)}, u32[]{:S(2)}, u32[]{:S(2)}) collective-permute-start(bf16[32,1792]{1,0:T(8,128)(2,1)S(1)} %shard_map.75), channel_id=1, source_target_pairs={{0,2},{2,0},{4,6},{6,4},{8,10},{10,8},{12,14},{14,12},{1,3},{3,1},... | collective-permute-start | bytes 344072 | tf_op jit(solution)/shard_map/ppermute | solution.py:410
  55.3 0.6 collective-permute-start.17
  55.9 1.5 %collective-permute-done.11.refs_2_ = bf16[32,1792]{1,0:T(8,128)(2,1)S(1)} collective-permute-done((bf16[32,1792]{1,0:T(8,128)(2,1)S(1)}, bf16[32,1792]{1,0:T(8,128)(2,1)S(1)}, u32[]{:S(2)}, u32[]{:S(2)}) %collective-permute-start.11) | collective-permute-done | bytes 114720 | tf_op jit(solution)/shard_map/ppermute | solution.py:410
  57.4 1.5 %collective-permute-start.15 = (bf16[32,1792]{1,0:T(8,128)(2,1)S(1)}, bf16[32,1792]{1,0:T(8,128)(2,1)S(1)}, u32[]{:S(2)}, u32[]{:S(2)}) collective-permute-start(bf16[32,1792]{1,0:T(8,128)(2,1)S(1)} %shard_map.74), channel_id=1, source_target_pairs={{0,6},{2,4},{4,2},{6,0},{8,14},{10,12},{12,10},{14,8},{1,7},{3,5},... | collective-permute-start | bytes 344072 | tf_op jit(solution)/shard_map/ppermute | solution.py:410
  58.9 0.0 collective-permute-done.12.refs_3_
  58.9 1.1 %collective-permute-done.13.refs_4_ = bf16[32,1792]{1,0:T(8,128)(2,1)S(1)} collective-permute-done((bf16[32,1792]{1,0:T(8,128)(2,1)S(1)}, bf16[32,1792]{1,0:T(8,128)(2,1)S(1)}, u32[]{:S(2)}, u32[]{:S(2)}) %collective-permute-start.13) | collective-permute-done | bytes 114720 | tf_op jit(solution)/shard_map/ppermute | solution.py:410
  60.1 0.1 shard_map.73
  60.2 2.8 %collective-permute-start.14 = (bf16[32,1792]{1,0:T(8,128)(2,1)S(1)}, bf16[32,1792]{1,0:T(8,128)(2,1)S(1)}, u32[]{:S(2)}, u32[]{:S(2)}) collective-permute-start(bf16[32,1792]{1,0:T(8,128)(2,1)S(1)} %shard_map.73), channel_id=1, source_target_pairs={{0,8},{2,10},{4,12},{6,14},{8,0},{10,2},{12,4},{14,6},{1,9},{3,11}... | collective-permute-start | bytes 344072 | tf_op jit(solution)/shard_map/ppermute | solution.py:410
  63.0 0.0 collective-permute-done.16
  63.0 0.8 %collective-permute-done.17 = bf16[32,1792]{1,0:T(8,128)(2,1)S(1)} collective-permute-done((bf16[32,1792]{1,0:T(8,128)(2,1)S(1)}, bf16[32,1792]{1,0:T(8,128)(2,1)S(1)}, u32[]{:S(2)}, u32[]{:S(2)}) %collective-permute-start.17) | collective-permute-done | bytes 114720 | tf_op jit(solution)/shard_map/ppermute | solution.py:410
  63.8 2.7 %collective-permute-done.15 = bf16[32,1792]{1,0:T(8,128)(2,1)S(1)} collective-permute-done((bf16[32,1792]{1,0:T(8,128)(2,1)S(1)}, bf16[32,1792]{1,0:T(8,128)(2,1)S(1)}, u32[]{:S(2)}, u32[]{:S(2)}) %collective-permute-start.15) | collective-permute-done | bytes 114720 | tf_op jit(solution)/shard_map/ppermute | solution.py:410
  66.4 1.8 %collective-permute-done.14 = bf16[32,1792]{1,0:T(8,128)(2,1)S(1)} collective-permute-done((bf16[32,1792]{1,0:T(8,128)(2,1)S(1)}, bf16[32,1792]{1,0:T(8,128)(2,1)S(1)}, u32[]{:S(2)}, u32[]{:S(2)}) %collective-permute-start.14) | collective-permute-done | bytes 114720 | tf_op jit(solution)/shard_map/ppermute | solution.py:410
  68.2 0.7 %add_convert_fusion = bf16[32,1792]{1,0:T(8,128)(2,1)} fusion(bf16[32,1792]{1,0:T(8,128)(2,1)S(1)} %collective-permute-done.17, bf16[32,1792]{1,0:T(8,128)(2,1)S(1)} %collective-permute-done.16, bf16[32,1792]{1,0:T(8,128)(2,1)S(1)} %collective-permute-done.15, bf16[32,1792]{1,0:T(8,128)(2,1)S(1)} %collective-permute-done.14, ...), kind=kLoop, calls=%fused_computation.2 | loop fusion | flops 688128 | bytes 802816 | tf_op jit(solution)/shard_map/convert_element_type | solution.py:462
  (8 shorter events, 0.3 us)
Async XLA Ops:
  0.9 12.9 %collective-permute-start.3 = (bf16[32,1920]{1,0:T(8,128)(2,1)S(1)}, bf16[32,1920]{1,0:T(8,128)(2,1)S(1)}, u32[]{:S(2)}, u32[]{:S(2)}) collective-permute-start(bf16[32,1920]{1,0:T(8,128)(2,1)S(1)} %shard_map.64.after_ref.refs_0_), channel_id=1, source_target_pairs={{0,6},{2,4},{4,2},{6,0},{8,14},{10,12},{12,10},{14,8},{1,7},{3,5},... | collective-permute-start | bytes 368648 | tf_op jit(solution)/shard_map/ppermute | solution.py:410
  4.9 8.9 %collective-permute-start.2 = (bf16[32,1920]{1,0:T(8,128)(2,1)S(1)}, bf16[32,1920]{1,0:T(8,128)(2,1)S(1)}, u32[]{:S(2)}, u32[]{:S(2)}) collective-permute-start(bf16[32,1920]{1,0:T(8,128)(2,1)S(1)} %shard_map.64.after_ref.refs_0_), channel_id=1, source_target_pairs={{0,2},{2,0},{4,6},{6,4},{8,10},{10,8},{12,14},{14,12},{1,3},{3,1},... | collective-permute-start | bytes 368648 | tf_op jit(solution)/shard_map/ppermute | solution.py:410
  5.5 8.4 %collective-permute-start.1 = (bf16[32,1920]{1,0:T(8,128)(2,1)S(1)}, bf16[32,1920]{1,0:T(8,128)(2,1)S(1)}, u32[]{:S(2)}, u32[]{:S(2)}) collective-permute-start(bf16[32,1920]{1,0:T(8,128)(2,1)S(1)} %shard_map.64.after_ref.refs_0_), channel_id=1, source_target_pairs={{0,8},{2,10},{4,12},{6,14},{8,0},{10,2},{12,4},{14,6},{1,9},{3,11}... | collective-permute-start | bytes 368648 | tf_op jit(solution)/shard_map/ppermute | solution.py:410
  8.1 5.8 %collective-permute-start = (bf16[32,1920]{1,0:T(8,128)(2,1)S(1)}, bf16[32,1920]{1,0:T(8,128)(2,1)S(1)}, u32[]{:S(2)}, u32[]{:S(2)}) collective-permute-start(bf16[32,1920]{1,0:T(8,128)(2,1)S(1)} %shard_map.64.after_ref.refs_0_), channel_id=1, source_target_pairs={{0,4},{2,6},{4,0},{6,2},{8,12},{10,14},{12,8},{14,10},{1,5},{3,7},... | collective-permute-start | bytes 368648 | tf_op jit(solution)/shard_map/ppermute | solution.py:410
  13.9 11.5 %collective-permute-start.7 = (bf16[160,1920]{1,0:T(8,128)(2,1)S(1)}, bf16[160,1920]{1,0:T(8,128)(2,1)S(1)}, u32[]{:S(2)}, u32[]{:S(2)}) collective-permute-start(bf16[160,1920]{1,0:T(8,128)(2,1)S(1)} %shard_map.66), channel_id=1, source_target_pairs={{0,1},{1,0},{2,3},{3,2},{4,5},{5,4},{6,7},{7,6},{8,9},{9,8},{10,11... | collective-permute-start | bytes 1843208 | tf_op jit(solution)/shard_map/ppermute | solution.py:407
  14.0 7.8 %collective-permute-start.6 = (bf16[32,1920]{1,0:T(8,128)(2,1)S(1)}, bf16[32,1920]{1,0:T(8,128)(2,1)S(1)}, u32[]{:S(2)}, u32[]{:S(2)}) collective-permute-start(bf16[32,1920]{1,0:T(8,128)(2,1)S(1)} %collective-permute-done.1.refs_2_.after_ref), channel_id=1, source_target_pairs={{0,6},{2,4},{4,2},{6,0},{8,14},{10,12},{12,10},{14,8},{1,7},{3,5},... | collective-permute-start | bytes 368648 | tf_op jit(solution)/shard_map/ppermute | solution.py:410
  16.5 6.7 %collective-permute-start.5 = (bf16[32,1920]{1,0:T(8,128)(2,1)S(1)}, bf16[32,1920]{1,0:T(8,128)(2,1)S(1)}, u32[]{:S(2)}, u32[]{:S(2)}) collective-permute-start(bf16[32,1920]{1,0:T(8,128)(2,1)S(1)} %collective-permute-done.1.refs_2_.after_ref), channel_id=1, source_target_pairs={{0,2},{2,0},{4,6},{6,4},{8,10},{10,8},{12,14},{14,12},{1,3},{3,1},... | collective-permute-start | bytes 368648 | tf_op jit(solution)/shard_map/ppermute | solution.py:410
  17.1 6.5 %collective-permute-start.4 = (bf16[32,1920]{1,0:T(8,128)(2,1)S(1)}, bf16[32,1920]{1,0:T(8,128)(2,1)S(1)}, u32[]{:S(2)}, u32[]{:S(2)}) collective-permute-start(bf16[32,1920]{1,0:T(8,128)(2,1)S(1)} %collective-permute-done.1.refs_2_.after_ref), channel_id=1, source_target_pairs={{0,4},{2,6},{4,0},{6,2},{8,12},{10,14},{12,8},{14,10},{1,5},{3,7},... | collective-permute-start | bytes 368648 | tf_op jit(solution)/shard_map/ppermute | solution.py:410
  23.7 1.8 %collective-permute-start.8 = (bf16[96,1920]{1,0:T(8,128)(2,1)S(1)}, bf16[96,1920]{1,0:T(8,128)(2,1)S(1)}, u32[]{:S(2)}, u32[]{:S(2)}) collective-permute-start(bf16[96,1920]{1,0:T(8,128)(2,1)S(1)} %shard_map.68), channel_id=1, source_target_pairs={{0,1},{1,0},{2,3},{3,2},{4,5},{5,4},{6,7},{7,6},{8,9},{9,8},{10,11... | collective-permute-start | bytes 1105928 | tf_op jit(solution)/shard_map/ppermute | solution.py:407
  48.1 1.9 %collective-permute-start.10 = (bf16[128,1792]{1,0:T(8,128)(2,1)S(1)}, bf16[128,1792]{1,0:T(8,128)(2,1)S(1)}, u32[]{:S(2)}, u32[]{:S(2)}) collective-permute-start(bf16[128,1792]{1,0:T(8,128)(2,1)S(1)} %get-tuple-element.20), channel_id=1, source_target_pairs={{0,1},{1,0},{2,3},{3,2},{4,5},{5,4},{6,7},{7,6},{8,9},{9,8},{10,11... | collective-permute-start | bytes 1376264 | tf_op jit(solution)/shard_map/ppermute | solution.py:407
  48.3 5.5 %collective-permute-start.9 = (bf16[128,1792]{1,0:T(8,128)(2,1)S(1)}, bf16[128,1792]{1,0:T(8,128)(2,1)S(1)}, u32[]{:S(2)}, u32[]{:S(2)}) collective-permute-start(bf16[128,1792]{1,0:T(8,128)(2,1)S(1)} %get-tuple-element.18), channel_id=1, source_target_pairs={{0,1},{1,0},{2,3},{3,2},{4,5},{5,4},{6,7},{7,6},{8,9},{9,8},{10,11... | collective-permute-start | bytes 1376264 | tf_op jit(solution)/shard_map/ppermute | solution.py:407
  50.0 7.5 %collective-permute-start.11 = (bf16[32,1792]{1,0:T(8,128)(2,1)S(1)}, bf16[32,1792]{1,0:T(8,128)(2,1)S(1)}, u32[]{:S(2)}, u32[]{:S(2)}) collective-permute-start(bf16[32,1792]{1,0:T(8,128)(2,1)S(1)} %shard_map.70), channel_id=1, source_target_pairs={{0,2},{2,0},{4,6},{6,4},{8,10},{10,8},{12,14},{14,12},{1,3},{3,1},... | collective-permute-start | bytes 344072 | tf_op jit(solution)/shard_map/ppermute | solution.py:410
  51.5 7.5 %collective-permute-start.12 = (bf16[32,1792]{1,0:T(8,128)(2,1)S(1)}, bf16[32,1792]{1,0:T(8,128)(2,1)S(1)}, u32[]{:S(2)}, u32[]{:S(2)}) collective-permute-start(bf16[32,1792]{1,0:T(8,128)(2,1)S(1)} %shard_map.71), channel_id=1, source_target_pairs={{0,6},{2,4},{4,2},{6,0},{8,14},{10,12},{12,10},{14,8},{1,7},{3,5},... | collective-permute-start | bytes 344072 | tf_op jit(solution)/shard_map/ppermute | solution.py:410
  52.9 7.2 %collective-permute-start.13 = (bf16[32,1792]{1,0:T(8,128)(2,1)S(1)}, bf16[32,1792]{1,0:T(8,128)(2,1)S(1)}, u32[]{:S(2)}, u32[]{:S(2)}) collective-permute-start(bf16[32,1792]{1,0:T(8,128)(2,1)S(1)} %shard_map.72), channel_id=1, source_target_pairs={{0,4},{2,6},{4,0},{6,2},{8,12},{10,14},{12,8},{14,10},{1,5},{3,7},... | collective-permute-start | bytes 344072 | tf_op jit(solution)/shard_map/ppermute | solution.py:410
  53.8 9.2 %collective-permute-start.16 = (bf16[32,1792]{1,0:T(8,128)(2,1)S(1)}, bf16[32,1792]{1,0:T(8,128)(2,1)S(1)}, u32[]{:S(2)}, u32[]{:S(2)}) collective-permute-start(bf16[32,1792]{1,0:T(8,128)(2,1)S(1)} %shard_map.75), channel_id=1, source_target_pairs={{0,2},{2,0},{4,6},{6,4},{8,10},{10,8},{12,14},{14,12},{1,3},{3,1},... | collective-permute-start | bytes 344072 | tf_op jit(solution)/shard_map/ppermute | solution.py:410
  55.3 8.5 %collective-permute-start.17 = (bf16[32,1792]{1,0:T(8,128)(2,1)S(1)}, bf16[32,1792]{1,0:T(8,128)(2,1)S(1)}, u32[]{:S(2)}, u32[]{:S(2)}) collective-permute-start(bf16[32,1792]{1,0:T(8,128)(2,1)S(1)} %shard_map.76), channel_id=1, source_target_pairs={{0,4},{2,6},{4,0},{6,2},{8,12},{10,14},{12,8},{14,10},{1,5},{3,7},... | collective-permute-start | bytes 344072 | tf_op jit(solution)/shard_map/ppermute | solution.py:410
  57.4 9.0 %collective-permute-start.15 = (bf16[32,1792]{1,0:T(8,128)(2,1)S(1)}, bf16[32,1792]{1,0:T(8,128)(2,1)S(1)}, u32[]{:S(2)}, u32[]{:S(2)}) collective-permute-start(bf16[32,1792]{1,0:T(8,128)(2,1)S(1)} %shard_map.74), channel_id=1, source_target_pairs={{0,6},{2,4},{4,2},{6,0},{8,14},{10,12},{12,10},{14,8},{1,7},{3,5},... | collective-permute-start | bytes 344072 | tf_op jit(solution)/shard_map/ppermute | solution.py:410
  60.2 8.0 %collective-permute-start.14 = (bf16[32,1792]{1,0:T(8,128)(2,1)S(1)}, bf16[32,1792]{1,0:T(8,128)(2,1)S(1)}, u32[]{:S(2)}, u32[]{:S(2)}) collective-permute-start(bf16[32,1792]{1,0:T(8,128)(2,1)S(1)} %shard_map.73), channel_id=1, source_target_pairs={{0,8},{2,10},{4,12},{6,14},{8,0},{10,2},{12,4},{14,6},{1,9},{3,11}... | collective-permute-start | bytes 344072 | tf_op jit(solution)/shard_map/ppermute | solution.py:410

commit v5 on v4

--- a/solution.py
+++ b/solution.py
@@ -270,15 +270,15 @@
 
     def visit(expert, down_ref, base, streamed):
         def forward(row_data, weight_column, count):
-            gate_proj = project(expert, 0, row_data)[:count]
-            up_proj = project(expert, 1, row_data)[:count]
+            gate_proj = project(expert, 0, row_data)
+            up_proj = project(expert, 1, row_data)
             active = (jax.nn.silu(gate_proj) * up_proj).astype(jnp.bfloat16)
             if streamed:
                 stream(expert).wait()
             partial = jnp.dot(
                 active, down_ref[expert - base], preferred_element_type=jnp.float32
             )
-            return (partial * weight_column).astype(jnp.bfloat16)
+            return (partial[:count] * weight_column).astype(jnp.bfloat16)
 
         first_row = pl.multiple_of(expert * cap_cold, cap_cold)
         block = pl.ds(first_row, cap_cold)

time: 69.2 us -> 69.1 us (level)
  waiting for transfers between devices: 12.6 us -> 13.8 us
  starting transfers between devices: 22 us -> 20.8 us
    ppermute x14, waiting for transfers between devices: 9.71 us -> 10.9 us  [trade(): return lax.ppermute(value, 'expert', [(i, i ^ k) for i in range(devices)])]
    ppermute x14, starting transfers between devices: 21.3 us -> 20.1 us  [trade(): return lax.ppermute(value, 'expert', [(i, i ^ k) for i in range(devices)])]
  transfers between devices with their start and end apart: 18 -> 18, of which waited for: 9 -> 10; matrix products, arithmetic and copies ran while one was open for 0% -> 0% of each run, Pallas kernels for 14% -> 14%
where the time goes in v5:
time: 69.1 us; the launch traced here: 68.9 us
  Pallas kernels  33.3 us (48%)
  starting transfers between devices  20.8 us (30%)
  waiting for transfers between devices  13.8 us (20%)
  other arithmetic  0.89 us (1%)
    pallas_call x1, Pallas kernels, run_experts(): pl.pallas_call(functools.partial(expert_kernel, topk, cap_cold, cap_hot),...  22.5 us
    ppermute x14, starting transfers between devices, trade(): return lax.ppermute(value, 'expert', [(i, i ^ k) for i in range(devices)])  20.1 us
    ppermute x14, waiting for transfers between devices, trade(): return lax.ppermute(value, 'expert', [(i, i ^ k) for i in range(devices)])  10.9 us
    pallas_call x2, Pallas kernels, fetch_part(): pl.pallas_call(kernel, in_specs=[HBM_SPEC, HBM_SPEC], out_specs=(VMEM_SPE...  9.51 us
    ppermute x4, waiting for transfers between devices, across(): return lax.ppermute(value, 'tensor', [(0, 1), (1, 0)])  2.9 us
  transfers between devices with their start and end apart: 18, of which 10 were waited for; matrix products, arithmetic and copies ran while one was open for 0% of the time, Pallas kernels for 14%

profile of v5, /device:TPU:0, one launch (start us, length us, event | category | flops | bytes accessed | tf_op | source)
XLA Modules:
  0.0 68.9 jit_solution(15924773996767539075)
XLA Ops:
  0.0 0.9 %shard_map.64.after_ref.refs_0_ = bf16[32,1920]{1,0:T(8,128)(2,1)S(1)} custom-call(bf16[2,16,3584]{2,1,0:T(8,128)(2,1)} %tokens_ref.1, s32[2,8,16]{2,1,0:T(8,128)} %bitcast.3, f32[2,8,16]{2,1,0:T(8,128)} %bitcast.4), custom_call_target="tpu_custom_call" | custom-call | tf_op jit(solution)/shard_map/pallas_call | solution.py:80
  0.9 4.0 %collective-permute-start.3 = (bf16[32,1920]{1,0:T(8,128)(2,1)S(1)}, bf16[32,1920]{1,0:T(8,128)(2,1)S(1)}, u32[]{:S(2)}, u32[]{:S(2)}) collective-permute-start(bf16[32,1920]{1,0:T(8,128)(2,1)S(1)} %shard_map.64.after_ref.refs_0_), channel_id=1, source_target_pairs={{0,6},{2,4},{4,2},{6,0},{8,14},{10,12},{12,10},{14,8},{1,7},{3,5},... | collective-permute-start | bytes 368648 | tf_op jit(solution)/shard_map/ppermute | solution.py:410
  4.9 0.5 collective-permute-start.2
  5.5 2.6 %collective-permute-start.1 = (bf16[32,1920]{1,0:T(8,128)(2,1)S(1)}, bf16[32,1920]{1,0:T(8,128)(2,1)S(1)}, u32[]{:S(2)}, u32[]{:S(2)}) collective-permute-start(bf16[32,1920]{1,0:T(8,128)(2,1)S(1)} %shard_map.64.after_ref.refs_0_), channel_id=1, source_target_pairs={{0,8},{2,10},{4,12},{6,14},{8,0},{10,2},{12,4},{14,6},{1,9},{3,11}... | collective-permute-start | bytes 368648 | tf_op jit(solution)/shard_map/ppermute | solution.py:410
  8.1 0.4 collective-permute-start
  8.5 5.3 %shard_map.65 = (bf16[4,512,3584]{2,1,0:T(8,128)(2,1)S(1)}, f32[8,128]{1,0:T(8,128)S(1)}) custom-call(bf16[8,512,3584]{2,1,0:T(8,128)(2,1)} %down_ref_hbm.1, bf16[32,1920]{1,0:T(8,128)(2,1)S(1)} %shard_map.64.after_ref.refs_0_), custom_call_target="tpu_custom_call" | custom-call | bytes 14680064 | tf_op jit(solution)/shard_map/pallas_call | solution.py:108
  13.8 0.0 collective-permute-done.3.refs_4_
  13.8 0.0 collective-permute-done.2.refs_3_
  13.8 0.0 collective-permute-done.1.refs_2_.after_ref
  13.8 0.0 collective-permute-done.refs_1_
  13.9 0.1 collective-permute-start.7
  14.0 2.6 %collective-permute-start.6 = (bf16[32,1920]{1,0:T(8,128)(2,1)S(1)}, bf16[32,1920]{1,0:T(8,128)(2,1)S(1)}, u32[]{:S(2)}, u32[]{:S(2)}) collective-permute-start(bf16[32,1920]{1,0:T(8,128)(2,1)S(1)} %collective-permute-done.1.refs_2_.after_ref), channel_id=1, source_target_pairs={{0,6},{2,4},{4,2},{6,0},{8,14},{10,12},{12,10},{14,8},{1,7},{3,5},... | collective-permute-start | bytes 368648 | tf_op jit(solution)/shard_map/ppermute | solution.py:410
  16.5 0.5 collective-permute-start.5
  17.1 0.4 collective-permute-start.4
  17.5 4.2 %shard_map.67 = (bf16[3,512,3584]{2,1,0:T(8,128)(2,1)S(1)}, f32[8,128]{1,0:T(8,128)S(1)}) custom-call(bf16[8,512,3584]{2,1,0:T(8,128)(2,1)} %down_ref_hbm.1, bf16[32,1920]{1,0:T(8,128)(2,1)S(1)} %collective-permute-done.1.refs_2_.after_ref), custom_call_target="tpu_custom_call" | custom-call | bytes 11010048 | tf_op jit(solution)/shard_map/pallas_call | solution.py:108
  21.8 0.0 collective-permute-done.6.refs_2_
  21.8 1.5 %collective-permute-done.5.refs_1_ = bf16[32,1920]{1,0:T(8,128)(2,1)S(1)} collective-permute-done((bf16[32,1920]{1,0:T(8,128)(2,1)S(1)}, bf16[32,1920]{1,0:T(8,128)(2,1)S(1)}, u32[]{:S(2)}, u32[]{:S(2)}) %collective-permute-start.5) | collective-permute-done | bytes 122912 | tf_op jit(solution)/shard_map/ppermute | solution.py:410
  23.2 0.4 collective-permute-done.4.refs_0_
  23.7 0.1 collective-permute-start.8
  23.7 0.1 pad_maximum_fusion.mine_ref
  23.8 1.6 %collective-permute-done.8 = bf16[96,1920]{1,0:T(8,128)(2,1)S(1)} collective-permute-done((bf16[96,1920]{1,0:T(8,128)(2,1)S(1)}, bf16[96,1920]{1,0:T(8,128)(2,1)S(1)}, u32[]{:S(2)}, u32[]{:S(2)}) %collective-permute-start.8) | collective-permute-done | bytes 368672 | tf_op jit(solution)/shard_map/ppermute | solution.py:407
  25.4 0.0 collective-permute-done.7
  25.4 0.1 pad_maximum_fusion.1.theirs_ref
  25.5 22.5 %shard_map.69 = (bf16[128,1792]{1,0:T(8,128)(2,1)S(1)}, bf16[128,1792]{1,0:T(8,128)(2,1)S(1)}, bf16[128,1792]{1,0:T(8,128)(2,1)S(1)}, bf16[128,1792]{1,0:T(8,128)(2,1)S(1)}) custom-call(bf16[256,1920]{1,0:T(8,128)(2,1)S(1)} %pad_maximum_fusion.mine_ref, bf16[256,1920]{1,0:T(8,128)(2,1)S(1)} %pad_maximum_fusion.1.theirs_ref, bf16[8,3584,512]{2,1,0:T(8,128)(2,1)} %gate_ref.1, ...), custom_call_target="tpu_custom_call" | custom-call | flops 2818572288 | bytes 58720256 | tf_op jit(solution)/shard_map/pallas_call | solution.py:357
  48.0 0.2 collective-permute-start.10
  48.2 0.4 collective-permute-start.9
  48.6 1.3 %collective-permute-done.10.refs_1_ = bf16[128,1792]{1,0:T(8,128)(2,1)S(1)} collective-permute-done((bf16[128,1792]{1,0:T(8,128)(2,1)S(1)}, bf16[128,1792]{1,0:T(8,128)(2,1)S(1)}, u32[]{:S(2)}, u32[]{:S(2)}) %collective-permute-start.10) | collective-permute-done | bytes 458784 | tf_op jit(solution)/shard_map/ppermute | solution.py:407
  50.0 2.1 %collective-permute-start.11 = (bf16[32,1792]{1,0:T(8,128)(2,1)S(1)}, bf16[32,1792]{1,0:T(8,128)(2,1)S(1)}, u32[]{:S(2)}, u32[]{:S(2)}) collective-permute-start(bf16[32,1792]{1,0:T(8,128)(2,1)S(1)} %shard_map.70), channel_id=1, source_target_pairs={{0,2},{2,0},{4,6},{6,4},{8,10},{10,8},{12,14},{14,12},{1,3},{3,1},... | collective-permute-start | bytes 344072 | tf_op jit(solution)/shard_map/ppermute | solution.py:410
  52.0 0.8 %collective-permute-start.12 = (bf16[32,1792]{1,0:T(8,128)(2,1)S(1)}, bf16[32,1792]{1,0:T(8,128)(2,1)S(1)}, u32[]{:S(2)}, u32[]{:S(2)}) collective-permute-start(bf16[32,1792]{1,0:T(8,128)(2,1)S(1)} %shard_map.71), channel_id=1, source_target_pairs={{0,6},{2,4},{4,2},{6,0},{8,14},{10,12},{12,10},{14,8},{1,7},{3,5},... | collective-permute-start | bytes 344072 | tf_op jit(solution)/shard_map/ppermute | solution.py:410
  52.9 0.8 %collective-permute-start.13 = (bf16[32,1792]{1,0:T(8,128)(2,1)S(1)}, bf16[32,1792]{1,0:T(8,128)(2,1)S(1)}, u32[]{:S(2)}, u32[]{:S(2)}) collective-permute-start(bf16[32,1792]{1,0:T(8,128)(2,1)S(1)} %shard_map.72), channel_id=1, source_target_pairs={{0,4},{2,6},{4,0},{6,2},{8,12},{10,14},{12,8},{14,10},{1,5},{3,7},... | collective-permute-start | bytes 344072 | tf_op jit(solution)/shard_map/ppermute | solution.py:410
  53.7 0.0 collective-permute-done.9.refs_1_.refs_2_
  53.7 2.1 %collective-permute-start.16 = (bf16[32,1792]{1,0:T(8,128)(2,1)S(1)}, bf16[32,1792]{1,0:T(8,128)(2,1)S(1)}, u32[]{:S(2)}, u32[]{:S(2)}) collective-permute-start(bf16[32,1792]{1,0:T(8,128)(2,1)S(1)} %shard_map.75), channel_id=1, source_target_pairs={{0,2},{2,0},{4,6},{6,4},{8,10},{10,8},{12,14},{14,12},{1,3},{3,1},... | collective-permute-start | bytes 344072 | tf_op jit(solution)/shard_map/ppermute | solution.py:410
  55.8 0.1 collective-permute-start.17
  56.0 2.0 %collective-permute-done.11.refs_2_ = bf16[32,1792]{1,0:T(8,128)(2,1)S(1)} collective-permute-done((bf16[32,1792]{1,0:T(8,128)(2,1)S(1)}, bf16[32,1792]{1,0:T(8,128)(2,1)S(1)}, u32[]{:S(2)}, u32[]{:S(2)}) %collective-permute-start.11) | collective-permute-done | bytes 114720 | tf_op jit(solution)/shard_map/ppermute | solution.py:410
  58.0 0.9 %collective-permute-start.15 = (bf16[32,1792]{1,0:T(8,128)(2,1)S(1)}, bf16[32,1792]{1,0:T(8,128)(2,1)S(1)}, u32[]{:S(2)}, u32[]{:S(2)}) collective-permute-start(bf16[32,1792]{1,0:T(8,128)(2,1)S(1)} %shard_map.74), channel_id=1, source_target_pairs={{0,6},{2,4},{4,2},{6,0},{8,14},{10,12},{12,10},{14,8},{1,7},{3,5},... | collective-permute-start | bytes 344072 | tf_op jit(solution)/shard_map/ppermute | solution.py:410
  58.9 0.1 collective-permute-done.12.refs_3_
  59.0 1.0 %collective-permute-done.13.refs_4_ = bf16[32,1792]{1,0:T(8,128)(2,1)S(1)} collective-permute-done((bf16[32,1792]{1,0:T(8,128)(2,1)S(1)}, bf16[32,1792]{1,0:T(8,128)(2,1)S(1)}, u32[]{:S(2)}, u32[]{:S(2)}) %collective-permute-start.13) | collective-permute-done | bytes 114720 | tf_op jit(solution)/shard_map/ppermute | solution.py:410
  60.1 0.1 shard_map.73
  60.2 2.2 %collective-permute-start.14 = (bf16[32,1792]{1,0:T(8,128)(2,1)S(1)}, bf16[32,1792]{1,0:T(8,128)(2,1)S(1)}, u32[]{:S(2)}, u32[]{:S(2)}) collective-permute-start(bf16[32,1792]{1,0:T(8,128)(2,1)S(1)} %shard_map.73), channel_id=1, source_target_pairs={{0,8},{2,10},{4,12},{6,14},{8,0},{10,2},{12,4},{14,6},{1,9},{3,11}... | collective-permute-start | bytes 344072 | tf_op jit(solution)/shard_map/ppermute | solution.py:410
  62.3 0.0 collective-permute-done.16
  62.3 1.4 %collective-permute-done.17 = bf16[32,1792]{1,0:T(8,128)(2,1)S(1)} collective-permute-done((bf16[32,1792]{1,0:T(8,128)(2,1)S(1)}, bf16[32,1792]{1,0:T(8,128)(2,1)S(1)}, u32[]{:S(2)}, u32[]{:S(2)}) %collective-permute-start.17) | collective-permute-done | bytes 114720 | tf_op jit(solution)/shard_map/ppermute | solution.py:410
  63.8 3.2 %collective-permute-done.15 = bf16[32,1792]{1,0:T(8,128)(2,1)S(1)} collective-permute-done((bf16[32,1792]{1,0:T(8,128)(2,1)S(1)}, bf16[32,1792]{1,0:T(8,128)(2,1)S(1)}, u32[]{:S(2)}, u32[]{:S(2)}) %collective-permute-start.15) | collective-permute-done | bytes 114720 | tf_op jit(solution)/shard_map/ppermute | solution.py:410
  66.9 1.2 %collective-permute-done.14 = bf16[32,1792]{1,0:T(8,128)(2,1)S(1)} collective-permute-done((bf16[32,1792]{1,0:T(8,128)(2,1)S(1)}, bf16[32,1792]{1,0:T(8,128)(2,1)S(1)}, u32[]{:S(2)}, u32[]{:S(2)}) %collective-permute-start.14) | collective-permute-done | bytes 114720 | tf_op jit(solution)/shard_map/ppermute | solution.py:410
  68.2 0.7 %add_convert_fusion = bf16[32,1792]{1,0:T(8,128)(2,1)} fusion(bf16[32,1792]{1,0:T(8,128)(2,1)S(1)} %collective-permute-done.17, bf16[32,1792]{1,0:T(8,128)(2,1)S(1)} %collective-permute-done.16, bf16[32,1792]{1,0:T(8,128)(2,1)S(1)} %collective-permute-done.15, bf16[32,1792]{1,0:T(8,128)(2,1)S(1)} %collective-permute-done.14, ...), kind=kLoop, calls=%fused_computation.2 | loop fusion | flops 688128 | bytes 802816 | tf_op jit(solution)/shard_map/convert_element_type | solution.py:462
  (8 shorter events, 0.3 us)
Async XLA Ops:
  0.9 12.9 %collective-permute-start.3 = (bf16[32,1920]{1,0:T(8,128)(2,1)S(1)}, bf16[32,1920]{1,0:T(8,128)(2,1)S(1)}, u32[]{:S(2)}, u32[]{:S(2)}) collective-permute-start(bf16[32,1920]{1,0:T(8,128)(2,1)S(1)} %shard_map.64.after_ref.refs_0_), channel_id=1, source_target_pairs={{0,6},{2,4},{4,2},{6,0},{8,14},{10,12},{12,10},{14,8},{1,7},{3,5},... | collective-permute-start | bytes 368648 | tf_op jit(solution)/shard_map/ppermute | solution.py:410
  4.9 8.9 %collective-permute-start.2 = (bf16[32,1920]{1,0:T(8,128)(2,1)S(1)}, bf16[32,1920]{1,0:T(8,128)(2,1)S(1)}, u32[]{:S(2)}, u32[]{:S(2)}) collective-permute-start(bf16[32,1920]{1,0:T(8,128)(2,1)S(1)} %shard_map.64.after_ref.refs_0_), channel_id=1, source_target_pairs={{0,2},{2,0},{4,6},{6,4},{8,10},{10,8},{12,14},{14,12},{1,3},{3,1},... | collective-permute-start | bytes 368648 | tf_op jit(solution)/shard_map/ppermute | solution.py:410
  5.5 8.4 %collective-permute-start.1 = (bf16[32,1920]{1,0:T(8,128)(2,1)S(1)}, bf16[32,1920]{1,0:T(8,128)(2,1)S(1)}, u32[]{:S(2)}, u32[]{:S(2)}) collective-permute-start(bf16[32,1920]{1,0:T(8,128)(2,1)S(1)} %shard_map.64.after_ref.refs_0_), channel_id=1, source_target_pairs={{0,8},{2,10},{4,12},{6,14},{8,0},{10,2},{12,4},{14,6},{1,9},{3,11}... | collective-permute-start | bytes 368648 | tf_op jit(solution)/shard_map/ppermute | solution.py:410
  8.1 5.8 %collective-permute-start = (bf16[32,1920]{1,0:T(8,128)(2,1)S(1)}, bf16[32,1920]{1,0:T(8,128)(2,1)S(1)}, u32[]{:S(2)}, u32[]{:S(2)}) collective-permute-start(bf16[32,1920]{1,0:T(8,128)(2,1)S(1)} %shard_map.64.after_ref.refs_0_), channel_id=1, source_target_pairs={{0,4},{2,6},{4,0},{6,2},{8,12},{10,14},{12,8},{14,10},{1,5},{3,7},... | collective-permute-start | bytes 368648 | tf_op jit(solution)/shard_map/ppermute | solution.py:410
  13.9 11.5 %collective-permute-start.7 = (bf16[160,1920]{1,0:T(8,128)(2,1)S(1)}, bf16[160,1920]{1,0:T(8,128)(2,1)S(1)}, u32[]{:S(2)}, u32[]{:S(2)}) collective-permute-start(bf16[160,1920]{1,0:T(8,128)(2,1)S(1)} %shard_map.66), channel_id=1, source_target_pairs={{0,1},{1,0},{2,3},{3,2},{4,5},{5,4},{6,7},{7,6},{8,9},{9,8},{10,11... | collective-permute-start | bytes 1843208 | tf_op jit(solution)/shard_map/ppermute | solution.py:407
  14.0 7.8 %collective-permute-start.6 = (bf16[32,1920]{1,0:T(8,128)(2,1)S(1)}, bf16[32,1920]{1,0:T(8,128)(2,1)S(1)}, u32[]{:S(2)}, u32[]{:S(2)}) collective-permute-start(bf16[32,1920]{1,0:T(8,128)(2,1)S(1)} %collective-permute-done.1.refs_2_.after_ref), channel_id=1, source_target_pairs={{0,6},{2,4},{4,2},{6,0},{8,14},{10,12},{12,10},{14,8},{1,7},{3,5},... | collective-permute-start | bytes 368648 | tf_op jit(solution)/shard_map/ppermute | solution.py:410
  16.5 6.7 %collective-permute-start.5 = (bf16[32,1920]{1,0:T(8,128)(2,1)S(1)}, bf16[32,1920]{1,0:T(8,128)(2,1)S(1)}, u32[]{:S(2)}, u32[]{:S(2)}) collective-permute-start(bf16[32,1920]{1,0:T(8,128)(2,1)S(1)} %collective-permute-done.1.refs_2_.after_ref), channel_id=1, source_target_pairs={{0,2},{2,0},{4,6},{6,4},{8,10},{10,8},{12,14},{14,12},{1,3},{3,1},... | collective-permute-start | bytes 368648 | tf_op jit(solution)/shard_map/ppermute | solution.py:410
  17.1 6.5 %collective-permute-start.4 = (bf16[32,1920]{1,0:T(8,128)(2,1)S(1)}, bf16[32,1920]{1,0:T(8,128)(2,1)S(1)}, u32[]{:S(2)}, u32[]{:S(2)}) collective-permute-start(bf16[32,1920]{1,0:T(8,128)(2,1)S(1)} %collective-permute-done.1.refs_2_.after_ref), channel_id=1, source_target_pairs={{0,4},{2,6},{4,0},{6,2},{8,12},{10,14},{12,8},{14,10},{1,5},{3,7},... | collective-permute-start | bytes 368648 | tf_op jit(solution)/shard_map/ppermute | solution.py:410
  23.7 1.8 %collective-permute-start.8 = (bf16[96,1920]{1,0:T(8,128)(2,1)S(1)}, bf16[96,1920]{1,0:T(8,128)(2,1)S(1)}, u32[]{:S(2)}, u32[]{:S(2)}) collective-permute-start(bf16[96,1920]{1,0:T(8,128)(2,1)S(1)} %shard_map.68), channel_id=1, source_target_pairs={{0,1},{1,0},{2,3},{3,2},{4,5},{5,4},{6,7},{7,6},{8,9},{9,8},{10,11... | collective-permute-start | bytes 1105928 | tf_op jit(solution)/shard_map/ppermute | solution.py:407
  48.0 1.9 %collective-permute-start.10 = (bf16[128,1792]{1,0:T(8,128)(2,1)S(1)}, bf16[128,1792]{1,0:T(8,128)(2,1)S(1)}, u32[]{:S(2)}, u32[]{:S(2)}) collective-permute-start(bf16[128,1792]{1,0:T(8,128)(2,1)S(1)} %get-tuple-element.20), channel_id=1, source_target_pairs={{0,1},{1,0},{2,3},{3,2},{4,5},{5,4},{6,7},{7,6},{8,9},{9,8},{10,11... | collective-permute-start | bytes 1376264 | tf_op jit(solution)/shard_map/ppermute | solution.py:407
  48.2 5.5 %collective-permute-start.9 = (bf16[128,1792]{1,0:T(8,128)(2,1)S(1)}, bf16[128,1792]{1,0:T(8,128)(2,1)S(1)}, u32[]{:S(2)}, u32[]{:S(2)}) collective-permute-start(bf16[128,1792]{1,0:T(8,128)(2,1)S(1)} %get-tuple-element.18), channel_id=1, source_target_pairs={{0,1},{1,0},{2,3},{3,2},{4,5},{5,4},{6,7},{7,6},{8,9},{9,8},{10,11... | collective-permute-start | bytes 1376264 | tf_op jit(solution)/shard_map/ppermute | solution.py:407
  50.0 8.0 %collective-permute-start.11 = (bf16[32,1792]{1,0:T(8,128)(2,1)S(1)}, bf16[32,1792]{1,0:T(8,128)(2,1)S(1)}, u32[]{:S(2)}, u32[]{:S(2)}) collective-permute-start(bf16[32,1792]{1,0:T(8,128)(2,1)S(1)} %shard_map.70), channel_id=1, source_target_pairs={{0,2},{2,0},{4,6},{6,4},{8,10},{10,8},{12,14},{14,12},{1,3},{3,1},... | collective-permute-start | bytes 344072 | tf_op jit(solution)/shard_map/ppermute | solution.py:410
  52.0 7.0 %collective-permute-start.12 = (bf16[32,1792]{1,0:T(8,128)(2,1)S(1)}, bf16[32,1792]{1,0:T(8,128)(2,1)S(1)}, u32[]{:S(2)}, u32[]{:S(2)}) collective-permute-start(bf16[32,1792]{1,0:T(8,128)(2,1)S(1)} %shard_map.71), channel_id=1, source_target_pairs={{0,6},{2,4},{4,2},{6,0},{8,14},{10,12},{12,10},{14,8},{1,7},{3,5},... | collective-permute-start | bytes 344072 | tf_op jit(solution)/shard_map/ppermute | solution.py:410
  52.9 7.2 %collective-permute-start.13 = (bf16[32,1792]{1,0:T(8,128)(2,1)S(1)}, bf16[32,1792]{1,0:T(8,128)(2,1)S(1)}, u32[]{:S(2)}, u32[]{:S(2)}) collective-permute-start(bf16[32,1792]{1,0:T(8,128)(2,1)S(1)} %shard_map.72), channel_id=1, source_target_pairs={{0,4},{2,6},{4,0},{6,2},{8,12},{10,14},{12,8},{14,10},{1,5},{3,7},... | collective-permute-start | bytes 344072 | tf_op jit(solution)/shard_map/ppermute | solution.py:410
  53.7 8.6 %collective-permute-start.16 = (bf16[32,1792]{1,0:T(8,128)(2,1)S(1)}, bf16[32,1792]{1,0:T(8,128)(2,1)S(1)}, u32[]{:S(2)}, u32[]{:S(2)}) collective-permute-start(bf16[32,1792]{1,0:T(8,128)(2,1)S(1)} %shard_map.75), channel_id=1, source_target_pairs={{0,2},{2,0},{4,6},{6,4},{8,10},{10,8},{12,14},{14,12},{1,3},{3,1},... | collective-permute-start | bytes 344072 | tf_op jit(solution)/shard_map/ppermute | solution.py:410
  55.8 7.9 %collective-permute-start.17 = (bf16[32,1792]{1,0:T(8,128)(2,1)S(1)}, bf16[32,1792]{1,0:T(8,128)(2,1)S(1)}, u32[]{:S(2)}, u32[]{:S(2)}) collective-permute-start(bf16[32,1792]{1,0:T(8,128)(2,1)S(1)} %shard_map.76), channel_id=1, source_target_pairs={{0,4},{2,6},{4,0},{6,2},{8,12},{10,14},{12,8},{14,10},{1,5},{3,7},... | collective-permute-start | bytes 344072 | tf_op jit(solution)/shard_map/ppermute | solution.py:410
  58.0 9.0 %collective-permute-start.15 = (bf16[32,1792]{1,0:T(8,128)(2,1)S(1)}, bf16[32,1792]{1,0:T(8,128)(2,1)S(1)}, u32[]{:S(2)}, u32[]{:S(2)}) collective-permute-start(bf16[32,1792]{1,0:T(8,128)(2,1)S(1)} %shard_map.74), channel_id=1, source_target_pairs={{0,6},{2,4},{4,2},{6,0},{8,14},{10,12},{12,10},{14,8},{1,7},{3,5},... | collective-permute-start | bytes 344072 | tf_op jit(solution)/shard_map/ppermute | solution.py:410
  60.2 8.0 %collective-permute-start.14 = (bf16[32,1792]{1,0:T(8,128)(2,1)S(1)}, bf16[32,1792]{1,0:T(8,128)(2,1)S(1)}, u32[]{:S(2)}, u32[]{:S(2)}) collective-permute-start(bf16[32,1792]{1,0:T(8,128)(2,1)S(1)} %shard_map.73), channel_id=1, source_target_pairs={{0,8},{2,10},{4,12},{6,14},{8,0},{10,2},{12,4},{14,6},{1,9},{3,11}... | collective-permute-start | bytes 344072 | tf_op jit(solution)/shard_map/ppermute | solution.py:410
